TPU v7x, 32 devices: a whole 2x2x4 slice. The times are simulated.
32 devices in a mesh: section: 4 (over y, core), dp: 8 (over z, x).
Axes of the slice: x: 2, y: 2, z: 4, core: 2. Of those that a mesh axis runs over, the one named last changes fastest.
Arguments:
- tokens: bfloat16 [128, 56, 768], P(('section', 'dp')), may hold values from -6 to 6
- cotangent: bfloat16 [128, 56, 768], P(('section', 'dp')), may hold values from -6 to 6
- task_flags: int32 [128], P(('section', 'dp')), may hold values from 0 to 2
- w_query: bfloat16 [4, 768, 768], P('section'), may hold values from -0.21875 to 0.21875
- w_key: bfloat16 [4, 768, 768], P('section'), may hold values from -0.21875 to 0.21875
- w_value: bfloat16 [4, 768, 768], P('section'), may hold values from -0.21875 to 0.21875
- w_attn_out: bfloat16 [4, 768, 768], P('section'), may hold values from -0.5 to 0.5
- b_query: bfloat16 [4, 768], P('section'), may hold values from -2 to 2
- b_value: bfloat16 [4, 768], P('section'), may hold values from -2 to 2
- b_attn_out: bfloat16 [4, 768], P('section'), may hold values from -2 to 2
- norm1_gain: bfloat16 [4, 768], P('section'), may hold values from 0.25 to 1.75
- norm1_bias: bfloat16 [4, 768], P('section'), may hold values from -1.5 to 1.5
- w_inner: bfloat16 [4, 768, 3072], P('section'), may hold values from -0.21875 to 0.21875
- b_inner: bfloat16 [4, 3072], P('section'), may hold values from -2 to 2
- w_outer: bfloat16 [4, 3072, 768], P('section'), may hold values from -0.109375 to 0.109375
- b_outer: bfloat16 [4, 768], P('section'), may hold values from -2 to 2
- norm2_gain: bfloat16 [4, 768], P('section'), may hold values from 0.25 to 1.75
- norm2_bias: bfloat16 [4, 768], P('section'), may hold values from -1.5 to 1.5
Outputs:
- mixed: bfloat16 [128, 56, 768], P(('section', 'dp'))
- tokens_grad: bfloat16 [128, 56, 768], P(('section', 'dp'))
- grad_w_query: float32 [4, 768, 768], P('section')
- grad_w_key: float32 [4, 768, 768], P('section')
- grad_w_value: float32 [4, 768, 768], P('section')
- grad_w_attn_out: float32 [4, 768, 768], P('section')
- grad_b_query: float32 [4, 768], P('section')
- grad_b_value: float32 [4, 768], P('section')
- grad_b_attn_out: float32 [4, 768], P('section')
- grad_norm1_gain: float32 [4, 768], P('section')
- grad_norm1_bias: float32 [4, 768], P('section')
- grad_w_inner: float32 [4, 768, 3072], P('section')
- grad_b_inner: float32 [4, 3072], P('section')
- grad_w_outer: float32 [4, 3072, 768], P('section')
- grad_b_outer: float32 [4, 768], P('section')
- grad_norm2_gain: float32 [4, 768], P('section')
- grad_norm2_bias: float32 [4, 768], P('section')
All inputs are finite; a program needn't handle non-finite values.
Results may differ from a plain program's by a relative error of at most 0.025.
Values may be sent and summed in bfloat16 or wider, within the bound.
No kernel may reach another device: no remote copies, remote signals or barrier semaphores. Data moves between devices by JAX's collectives and lax.ppermute only.
A program may use at most 768 MiB of HBM per device.

v0:
```python
from functools import partial

import jax
import jax.numpy as jnp
from jax import lax
from jax.sharding import PartitionSpec as P

HEADS = 12
OBJ = 36
MB = 4


EPS = 1e-06
NEG = -1000000000.0


def for_sending(x):

    def short(part):
        return part.astype(jnp.bfloat16) if part.dtype == jnp.float32 else part

    return jax.tree.map(short, x)


def shifted_2(value, axis, steps):
    count = lax.axis_size(axis)
    first, last = (max(0, -steps), min(count, count - steps))
    return lax.ppermute(value, axis, [(source, source + steps) for source in range(first, last)])


def head_mask(flags, head_count):
    levels = (jnp.arange(head_count) % 3).astype(jnp.float32)
    return (levels[None, :] != flags.astype(jnp.float32)[:, None]).astype(jnp.float32)


def norm_parts(values, gain, bias):
    centered = values - jnp.mean(values, -1, keepdims=True)
    inverse = lax.rsqrt(jnp.mean(centered * centered, -1, keepdims=True) + EPS)
    normed = centered * inverse
    return (normed * gain + bias, normed, inverse)


def norm_back(grad_out, normed, inverse, gain):
    scaled = grad_out * gain
    return inverse * (
        scaled
        - jnp.mean(scaled, -1, keepdims=True)
        - normed * jnp.mean(scaled * normed, -1, keepdims=True)
    )


def pad_rows(piece, lower, upper, seq_len, axis):
    widths = [(0, 0)] * piece.ndim
    widths[axis] = (lower, seq_len - upper)
    return jnp.pad(piece, widths)


def cross_mask(count):
    visual = jnp.arange(count) < OBJ
    return visual[:, None] != visual[None, :]


def window_forward(full_inputs, head_used, params, lower, upper, crossing, with_ffn):
    (
        w_query,
        w_key,
        w_value,
        w_attn_out,
        b_query,
        b_value,
        b_attn_out,
        norm1_gain,
        norm1_bias,
        w_inner,
        b_inner,
        w_outer,
        b_outer,
        norm2_gain,
        norm2_bias,
    ) = params
    items, seq_len, model_width = full_inputs.shape
    ffn_width = w_inner.shape[1]
    head_count = head_used.shape[1]
    inputs = full_inputs[:, lower:upper]
    count = upper - lower
    row_count = items * count
    split = (items, count, head_count, model_width // head_count)
    scale = (model_width // head_count) ** (-0.5)
    flat = inputs.reshape(row_count, model_width)
    queries = (jnp.dot(flat, w_query, preferred_element_type=jnp.float32) + b_query).astype(
        jnp.bfloat16
    )
    key_rows = jnp.dot(flat, w_key, preferred_element_type=jnp.float32).astype(jnp.bfloat16)
    values = (jnp.dot(flat, w_value, preferred_element_type=jnp.float32) + b_value).astype(
        jnp.bfloat16
    )
    scores = (
        jnp.einsum(
            "nihd,njhd->nhij",
            queries.reshape(split),
            key_rows.reshape(split),
            preferred_element_type=jnp.float32,
        )
        * scale
    )
    if crossing:
        scores = jnp.where(cross_mask(count), scores, NEG)
    row_max = jnp.max(scores, -1, keepdims=True)
    shifted = jnp.exp(scores - row_max)
    totals = jnp.sum(shifted, -1, keepdims=True)
    log_total = row_max + jnp.log(totals)
    probs = (shifted / totals).astype(jnp.bfloat16)
    context = (
        jnp.einsum(
            "nhij,njhd->nihd", probs, values.reshape(split), preferred_element_type=jnp.float32
        )
        * head_used[:, None, :, None]
    )
    context = context.reshape(row_count, model_width).astype(jnp.bfloat16)
    before = flat.astype(jnp.float32) + (
        jnp.dot(context, w_attn_out, preferred_element_type=jnp.float32) + b_attn_out
    )
    middle = norm_parts(before, norm1_gain, norm1_bias)[0]
    if with_ffn:
        inner = (
            jnp.dot(middle.astype(jnp.bfloat16), w_inner, preferred_element_type=jnp.float32)
            + b_inner
        )
        activated = jax.nn.gelu(inner, approximate=False).astype(jnp.bfloat16)
        after = middle + (jnp.dot(activated, w_outer, preferred_element_type=jnp.float32) + b_outer)
        result = norm_parts(after, norm2_gain, norm2_bias)[0]
    else:
        inner = jnp.zeros((row_count, ffn_width), jnp.float32)
        after = jnp.zeros((row_count, model_width), jnp.float32)
        result = middle
    result = result.reshape(items, count, model_width).astype(jnp.bfloat16)
    output = jnp.concatenate([full_inputs[:, :lower], result, full_inputs[:, upper:]], 1)
    rows_first = tuple(
        (
            piece.reshape(items, count, piece.shape[-1])
            for piece in (queries, key_rows, values, context, before, middle, inner, after)
        )
    )
    padded = tuple((pad_rows(piece, lower, upper, seq_len, 1) for piece in rows_first))
    saved = padded[:3] + (pad_rows(log_total, lower, upper, seq_len, 2),) + padded[3:]
    return (output, saved)


def forward_empty(items, seq_len, model_width, ffn_width, head_count):
    narrow = jnp.zeros((items, seq_len, model_width), jnp.bfloat16)
    wide = jnp.zeros((items, seq_len, model_width), jnp.float32)
    saved = (
        narrow,
        narrow,
        narrow,
        jnp.zeros((items, head_count, seq_len, 1), jnp.float32),
        narrow,
        wide,
        wide,
        jnp.zeros((items, seq_len, ffn_width), jnp.float32),
        wide,
    )
    return (narrow, saved)


def window_ffn_backward(saved, grad_full, params, lower, upper, with_ffn):
    w_inner, b_inner, w_outer, b_outer, norm2_gain, norm2_bias = params[9:]
    if not with_ffn:
        return (grad_full, tuple((jnp.zeros(p.shape, jnp.float32) for p in params[9:])))
    items, seq_len, model_width = grad_full.shape
    count = upper - lower
    row_count = items * count
    middle, inner, after = (
        piece[:, lower:upper].reshape(row_count, piece.shape[-1]) for piece in saved[6:]
    )
    grad_out = grad_full[:, lower:upper].reshape(row_count, model_width)
    normed_two, inverse_two = norm_parts(after, norm2_gain, norm2_bias)[1:]
    grad_after = norm_back(grad_out, normed_two, inverse_two, norm2_gain)
    grad_gain_two = jnp.sum(grad_out * normed_two, 0)
    grad_bias_two = jnp.sum(grad_out, 0)
    grad_outer = grad_after.astype(jnp.bfloat16)
    activated, gelu_pull = jax.vjp(partial(jax.nn.gelu, approximate=False), inner)
    grad_w_outer = jnp.einsum(
        "rf,rd->fd", activated.astype(jnp.bfloat16), grad_outer, preferred_element_type=jnp.float32
    )
    grad_b_outer = jnp.sum(grad_outer.astype(jnp.float32), 0)
    back_hidden = jnp.einsum("rd,fd->rf", grad_outer, w_outer, preferred_element_type=jnp.float32)
    grad_inner = gelu_pull(back_hidden)[0].astype(jnp.bfloat16)
    grad_w_inner = jnp.einsum(
        "rd,rf->df", middle.astype(jnp.bfloat16), grad_inner, preferred_element_type=jnp.float32
    )
    grad_b_inner = jnp.sum(grad_inner.astype(jnp.float32), 0)
    grad_middle = grad_after + jnp.einsum(
        "rf,df->rd", grad_inner, w_inner, preferred_element_type=jnp.float32
    )
    grad_middle = jnp.concatenate(
        [
            grad_full[:, :lower],
            grad_middle.reshape(items, count, model_width),
            grad_full[:, upper:],
        ],
        1,
    )
    return (
        grad_middle,
        (grad_w_inner, grad_b_inner, grad_w_outer, grad_b_outer, grad_gain_two, grad_bias_two),
    )


def window_attn_backward(saved, grad_full, full_inputs, head_used, params, lower, upper, crossing):
    w_query, w_key, w_value, w_attn_out, b_query, b_value, b_attn_out, norm1_gain, norm1_bias = (
        params[:9]
    )
    items, seq_len, model_width = full_inputs.shape
    count = upper - lower
    head_count = head_used.shape[1]
    split = (items, count, head_count, model_width // head_count)
    scale = (model_width // head_count) ** (-0.5)
    row_count = items * count
    flat = full_inputs[:, lower:upper].reshape(row_count, model_width)
    queries, key_rows, values, context, before = (
        saved[index][:, lower:upper].reshape(row_count, model_width) for index in (0, 1, 2, 4, 5)
    )
    log_total = saved[3][:, :, lower:upper]
    grad_middle = grad_full[:, lower:upper].reshape(row_count, model_width)
    normed_one, inverse_one = norm_parts(before, norm1_gain, norm1_bias)[1:]
    grad_before = norm_back(grad_middle, normed_one, inverse_one, norm1_gain)
    grad_gain_one = jnp.sum(grad_middle * normed_one, 0)
    grad_bias_one = jnp.sum(grad_middle, 0)
    grad_attn = grad_before.astype(jnp.bfloat16)
    grad_w_attn_out = jnp.einsum(
        "rc,rd->cd", context, grad_attn, preferred_element_type=jnp.float32
    )
    grad_b_attn_out = jnp.sum(grad_attn.astype(jnp.float32), 0)
    grad_context = jnp.einsum(
        "rd,cd->rc", grad_attn, w_attn_out, preferred_element_type=jnp.float32
    )
    grad_context = grad_context.astype(jnp.bfloat16).reshape(split) * head_used[
        :, None, :, None
    ].astype(jnp.bfloat16)
    query_heads = queries.reshape(split)
    key_heads = key_rows.reshape(split)
    scores = (
        jnp.einsum("nihd,njhd->nhij", query_heads, key_heads, preferred_element_type=jnp.float32)
        * scale
    )
    if crossing:
        scores = jnp.where(cross_mask(count), scores, NEG)
    probs = jnp.exp(scores - log_total)
    grad_values = jnp.einsum(
        "nhij,nihd->njhd",
        probs.astype(jnp.bfloat16),
        grad_context,
        preferred_element_type=jnp.float32,
    )
    grad_probs = jnp.einsum(
        "nihd,njhd->nhij", grad_context, values.reshape(split), preferred_element_type=jnp.float32
    )
    grad_scores = probs * (grad_probs - jnp.sum(probs * grad_probs, -1, keepdims=True))
    if crossing:
        grad_scores = jnp.where(cross_mask(count), grad_scores, 0.0)
    grad_scores = grad_scores.astype(jnp.bfloat16)
    grad_queries = (
        (
            jnp.einsum(
                "nhij,njhd->nihd", grad_scores, key_heads, preferred_element_type=jnp.float32
            )
            * scale
        )
        .reshape(row_count, model_width)
        .astype(jnp.bfloat16)
    )
    grad_keys = (
        (
            jnp.einsum(
                "nhij,nihd->njhd", grad_scores, query_heads, preferred_element_type=jnp.float32
            )
            * scale
        )
        .reshape(row_count, model_width)
        .astype(jnp.bfloat16)
    )
    grad_values = grad_values.reshape(row_count, model_width).astype(jnp.bfloat16)
    grad_w_query = jnp.einsum("rd,re->de", flat, grad_queries, preferred_element_type=jnp.float32)
    grad_w_key = jnp.einsum("rd,re->de", flat, grad_keys, preferred_element_type=jnp.float32)
    grad_w_value = jnp.einsum("rd,re->de", flat, grad_values, preferred_element_type=jnp.float32)
    grad_b_query = jnp.sum(grad_queries.astype(jnp.float32), 0)
    grad_b_value = jnp.sum(grad_values.astype(jnp.float32), 0)
    grad_inputs = grad_before + jnp.einsum(
        "re,de->rd", grad_queries, w_query, preferred_element_type=jnp.float32
    )
    grad_inputs = grad_inputs + jnp.einsum(
        "re,de->rd", grad_keys, w_key, preferred_element_type=jnp.float32
    )
    grad_inputs = grad_inputs + jnp.einsum(
        "re,de->rd", grad_values, w_value, preferred_element_type=jnp.float32
    )
    grad_inputs = jnp.concatenate(
        [
            grad_full[:, :lower],
            grad_inputs.reshape(items, count, model_width),
            grad_full[:, upper:],
        ],
        1,
    )
    terms = (
        grad_w_query,
        grad_w_key,
        grad_w_value,
        grad_w_attn_out,
        grad_b_query,
        grad_b_value,
        grad_b_attn_out,
        grad_gain_one,
        grad_bias_one,
    )
    return (grad_inputs.astype(jnp.bfloat16), terms)


def keep_block(buffer, value, start, flag):
    current = lax.dynamic_slice_in_dim(buffer, start, value.shape[0], 0)
    return lax.dynamic_update_slice_in_dim(buffer, jnp.where(flag, value, current), start, 0)


def per_device(
    tokens,
    cotangent,
    task_flags,
    w_query,
    w_key,
    w_value,
    w_attn_out,
    b_query,
    b_value,
    b_attn_out,
    norm1_gain,
    norm1_bias,
    w_inner,
    b_inner,
    w_outer,
    b_outer,
    norm2_gain,
    norm2_bias,
):
    section_count = lax.axis_size("section")
    section_index = lax.axis_index("section")
    all_tokens, all_cotangent, all_flags = (
        lax.all_gather(tokens, "section", axis=0, tiled=True),
        lax.all_gather(cotangent, "section", axis=0, tiled=True),
        lax.all_gather(task_flags.astype(jnp.bfloat16), "section", axis=0, tiled=True),
    )
    params = tuple(
        (
            w[0]
            for w in (
                w_query,
                w_key,
                w_value,
                w_attn_out,
                b_query,
                b_value,
                b_attn_out,
                norm1_gain,
                norm1_bias,
                w_inner,
                b_inner,
                w_outer,
                b_outer,
                norm2_gain,
                norm2_bias,
            )
        )
    )
    item_count, seq_len, model_width = all_tokens.shape
    per_micro = item_count // MB
    ffn_width = w_inner.shape[2]
    heads_all = head_mask(all_flags, HEADS)
    windows = (
        (0, OBJ, False, True),
        (0, seq_len, True, False),
        (0, OBJ, False, True),
        (OBJ, seq_len, False, True),
    )
    empty_out, empty_saved = forward_empty(per_micro, seq_len, model_width, ffn_width, HEADS)
    kept_inputs = jnp.zeros((MB, per_micro, seq_len, model_width), jnp.bfloat16)
    finished = jnp.zeros_like(all_tokens)
    passing = empty_out
    ticks = MB + section_count - 1

    def run_forward(branch, section_input, heads_on):
        options = [
            partial(
                window_forward, section_input, heads_on, params, lower, upper, crossing, with_ffn
            )
            for lower, upper, crossing, with_ffn in windows
        ]
        options.append(lambda: (empty_out, empty_saved))
        return lax.switch(branch, options)

    for instant in range(ticks):
        micro_index = instant - section_index
        active = jnp.logical_and(micro_index >= 0, micro_index < MB)
        branch = jnp.where(active, section_index, 4)
        slot_index = jnp.clip(micro_index, 0, MB - 1)
        start = slot_index * per_micro
        own_rows = lax.dynamic_slice_in_dim(all_tokens, start, per_micro, 0)
        if instant == 0:
            arriving = own_rows
        else:
            arriving = jax.tree.map(
                lambda part, own: part.astype(own.dtype),
                shifted_2(for_sending(passing), "section", 1),
                passing,
            )
        section_input = jnp.where(section_index == 0, own_rows, arriving)
        heads_on = lax.dynamic_slice_in_dim(heads_all, start, per_micro, 0)
        kept_inputs = keep_block(kept_inputs, section_input[None], slot_index, active)
        passing, saved = run_forward(branch, section_input, heads_on)
        finished = keep_block(
            finished, passing, start, jnp.logical_and(active, section_index == section_count - 1)
        )
    attn_zero = tuple((jnp.zeros(p.shape, jnp.float32) for p in params[:9]))
    ffn_zero = tuple((jnp.zeros(p.shape, jnp.float32) for p in params[9:]))
    wide_zero = jnp.zeros((per_micro, seq_len, model_width), jnp.float32)
    attn_total = attn_zero
    ffn_total = ffn_zero
    input_grads = jnp.zeros_like(all_tokens)
    grad_back = empty_out
    for instant in range(ticks):
        micro_index = instant - (section_count - 1 - section_index)
        active = jnp.logical_and(micro_index >= 0, micro_index < MB)
        branch = jnp.where(active, section_index, 4)
        slot_index = jnp.clip(micro_index, 0, MB - 1)
        start = slot_index * per_micro
        own_rows = lax.dynamic_slice_in_dim(all_cotangent, start, per_micro, 0)
        if instant == 0:
            arriving = own_rows
        else:
            arriving = jax.tree.map(
                lambda part, own: part.astype(own.dtype),
                shifted_2(for_sending(grad_back), "section", -1),
                grad_back,
            )
        grad_out = jnp.where(section_index == section_count - 1, own_rows, arriving).astype(
            jnp.float32
        )
        section_input = lax.dynamic_index_in_dim(kept_inputs, slot_index, 0, keepdims=False)
        heads_on = lax.dynamic_slice_in_dim(heads_all, start, per_micro, 0)
        saved = run_forward(branch, section_input, heads_on)[1]
        ffn_options = [
            partial(window_ffn_backward, saved, grad_out, params, lower, upper, with_ffn)
            for lower, upper, crossing, with_ffn in windows
        ]
        ffn_options.append(lambda: (wide_zero, ffn_zero))
        grad_middle, ffn_terms = lax.switch(branch, ffn_options)
        ffn_total = tuple((total + term for total, term in zip(ffn_total, ffn_terms)))
        attn_options = [
            partial(
                window_attn_backward,
                saved,
                grad_middle,
                section_input,
                heads_on,
                params,
                lower,
                upper,
                crossing,
            )
            for lower, upper, crossing, with_ffn in windows
        ]
        attn_options.append(lambda: (empty_out, attn_zero))
        grad_back, attn_terms = lax.switch(branch, attn_options)
        attn_total = tuple((total + term for total, term in zip(attn_total, attn_terms)))
        input_grads = keep_block(
            input_grads, grad_back, start, jnp.logical_and(active, section_index == 0)
        )
    (
        sum_w_query,
        sum_w_key,
        sum_w_value,
        sum_w_attn_out,
        sum_b_query,
        sum_b_value,
        sum_b_attn_out,
        sum_gain_one,
        sum_bias_one,
    ) = attn_total
    sum_w_inner, sum_b_inner, sum_w_outer, sum_b_outer, sum_gain_two, sum_bias_two = ffn_total
    summed = (
        lax.psum(sum_w_query.astype(jnp.bfloat16), "dp").astype(jnp.float32),
        lax.psum(sum_w_key.astype(jnp.bfloat16), "dp").astype(jnp.float32),
        lax.psum(sum_w_value.astype(jnp.bfloat16), "dp").astype(jnp.float32),
        lax.psum(sum_w_attn_out.astype(jnp.bfloat16), "dp").astype(jnp.float32),
        lax.psum(sum_b_query.astype(jnp.bfloat16), "dp").astype(jnp.float32),
        lax.psum(sum_b_value.astype(jnp.bfloat16), "dp").astype(jnp.float32),
        lax.psum(sum_b_attn_out.astype(jnp.bfloat16), "dp").astype(jnp.float32),
        lax.psum(sum_gain_one.astype(jnp.bfloat16), "dp").astype(jnp.float32),
        lax.psum(sum_bias_one.astype(jnp.bfloat16), "dp").astype(jnp.float32),
        lax.psum(sum_w_inner.astype(jnp.bfloat16), "dp").astype(jnp.float32),
        lax.psum(sum_b_inner.astype(jnp.bfloat16), "dp").astype(jnp.float32),
        lax.psum(sum_w_outer.astype(jnp.bfloat16), "dp").astype(jnp.float32),
        lax.psum(sum_b_outer.astype(jnp.bfloat16), "dp").astype(jnp.float32),
        lax.psum(sum_gain_two.astype(jnp.bfloat16), "dp").astype(jnp.float32),
        lax.psum(sum_bias_two.astype(jnp.bfloat16), "dp").astype(jnp.float32),
    )
    gathered_out, gathered_grads = (
        lax.all_to_all(finished, "section", split_axis=0, concat_axis=0, tiled=True),
        lax.all_to_all(input_grads, "section", split_axis=0, concat_axis=0, tiled=True),
    )
    piece_items = item_count // section_count
    mixed = gathered_out[(section_count - 1) * piece_items :]
    tokens_grad = gathered_grads[:piece_items]
    outputs = tuple((total[None] for total in summed))
    return (
        mixed,
        tokens_grad,
        outputs[0],
        outputs[1],
        outputs[2],
        outputs[3],
        outputs[4],
        outputs[5],
        outputs[6],
        outputs[7],
        outputs[8],
        outputs[9],
        outputs[10],
        outputs[11],
        outputs[12],
        outputs[13],
        outputs[14],
    )


def solution(mesh):
    placed = (
        P(("section", "dp"), None, None),
        P(("section", "dp"), None, None),
        P(("section", "dp")),
        P("section", None, None),
        P("section", None, None),
        P("section", None, None),
        P("section", None, None),
        P("section", None),
        P("section", None),
        P("section", None),
        P("section", None),
        P("section", None),
        P("section", None, None),
        P("section", None),
        P("section", None, None),
        P("section", None),
        P("section", None),
        P("section", None),
    )
    return jax.shard_map(
        per_device,
        mesh=mesh,
        in_specs=placed,
        out_specs=(
            P(("section", "dp"), None, None),
            P(("section", "dp"), None, None),
            P("section", None, None),
            P("section", None, None),
            P("section", None, None),
            P("section", None, None),
            P("section", None),
            P("section", None),
            P("section", None),
            P("section", None),
            P("section", None),
            P("section", None, None),
            P("section", None),
            P("section", None, None),
            P("section", None),
            P("section", None),
            P("section", None),
        ),
        check_vma=False,
    )
```

profile of v0, /device:TPU:30, one launch (start us, length us, event | category | flops | bytes accessed | tf_op | source)
XLA Modules:
  0.0 2412.5 jit_solution(8836705440550925137)
XLA Ops:
  10.8 5.8 all-reduce.189
  30.4 17.4 conditional.28
  50.0 6.4 collective-permute-done
  58.4 19.1 conditional.29
  79.6 55.0 %collective-permute-done.1 = bf16[4,56,768]{2,1,0:T(8,128)(2,1)} collective-permute-done((bf16[4,56,768]{2,1,0:T(8,128)(2,1)}, bf16[4,56,768]{2,1,0:T(8,128)(2,1)}, u32[]{:S(2)}, u32[]{:S(2)}) %collective-permute-start.1) | collective-permute-done | bytes 344096 | tf_op jit(solution)/shard_map/ppermute | solution.py:28
  136.7 73.0 %conditional.30 = (bf16[4,56,768]{2,1,0:T(8,128)(2,1)}) conditional(s32[]{:T(128)} %clamp.58, (bf16[4,56,768]{2,1,0:T(8,128)(2,1)S(1)}, bf16[768,768]{1,0:T(8,128)(2,1)S(1)}, bf16[768]{0:T(1024)(128)(2,1)}, bf16[768,768]{1,0:T(8,128)(2,1)}, bf16[768]{0:T(1024)(128)(2,1)S(1)}, ...), branch_computations={%region_54.61_spmd, %region_61.66_spmd, %region_66.73_spmd, %regio... | conditional | flops 2096410880 | bytes 27871388 | solution.py:398
  183.9 10.7 fusion.6549
  211.6 7.0 collective-permute-done.2
  220.6 73.0 %conditional.31 = (bf16[4,56,768]{2,1,0:T(8,128)(2,1)}) conditional(s32[]{:T(128)} %clamp.59, (bf16[4,56,768]{2,1,0:T(8,128)(2,1)S(1)}, bf16[768,768]{1,0:T(8,128)(2,1)S(1)}, bf16[768]{0:T(1024)(128)(2,1)}, bf16[768,768]{1,0:T(8,128)(2,1)}, bf16[768]{0:T(1024)(128)(2,1)S(1)}, ...), branch_computations={%region_81.88_spmd, %region_88.93_spmd, %region_93.100_spmd, %regi... | conditional | flops 2096410880 | bytes 27871388 | solution.py:398
  267.8 10.7 fusion.6578
  295.6 6.9 collective-permute-done.3
  304.6 73.1 %conditional.32 = (bf16[4,56,768]{2,1,0:T(8,128)(2,1)}) conditional(s32[]{:T(128)} %clamp.60, (bf16[4,56,768]{2,1,0:T(8,128)(2,1)S(1)}, bf16[768,768]{1,0:T(8,128)(2,1)S(1)}, bf16[768]{0:T(1024)(128)(2,1)}, bf16[768,768]{1,0:T(8,128)(2,1)}, bf16[768]{0:T(1024)(128)(2,1)S(1)}, ...), branch_computations={%region_108.115_spmd, %region_115.120_spmd, %region_120.127_spmd, ... | conditional | flops 2096410880 | bytes 27871388 | solution.py:398
  351.8 10.7 fusion.6607
  379.6 6.9 collective-permute-done.4
  388.6 71.9 %conditional.33 = (bf16[4,56,768]{2,1,0:T(8,128)(2,1)}) conditional(s32[]{:T(128)} %clamp.61, (bf16[4,56,768]{2,1,0:T(8,128)(2,1)S(1)}, bf16[768,768]{1,0:T(8,128)(2,1)S(1)}, bf16[768]{0:T(1024)(128)(2,1)}, bf16[768,768]{1,0:T(8,128)(2,1)}, bf16[768]{0:T(1024)(128)(2,1)S(1)}, ...), branch_computations={%region_135.142_spmd, %region_142.147_spmd, %region_147.154_spmd, ... | conditional | flops 2096410880 | bytes 27871388 | solution.py:398
  435.8 10.7 fusion.6636
  474.8 22.4 conditional.35
  498.2 27.4 %conditional.36 = (f32[4,56,768]{2,1,0:T(8,128)}, f32[3072]{0:T(1024)S(1)}, f32[3072,768]{1,0:T(8,128)}, f32[768]{0:T(1024)S(1)}, f32[768]{0:T(1024)S(1)}, /*index=5*/f32[768]{0:T(1024)S(1)}, f32[768,3072]{1,0:T(8,128)}) conditional(s32[]{:T(128)} %clamp.63, (f32[4,56,768]{2,1,0:T(8,128)}, f32[4,56,768]{2,1,0:T(8,128)}, ...), branch_computations={%region_210.219_spmd, %region_219.220_spmd, %region_220.229_spmd, ... | conditional | flops 2783878656 | bytes 104408480 | solution.py:455
  526.4 32.5 %conditional.37 = (bf16[4,56,768]{2,1,0:T(8,128)(2,1)}, f32[768]{0:T(1024)S(1)}, f32[768]{0:T(1024)}, f32[768]{0:T(1024)S(1)}, f32[768]{0:T(1024)S(1)}, /*index=...) conditional(s32[]{:T(128)} %clamp.63, ...), branch_computations={%region_239.250_spmd, %region_250.261_spmd, %region_261.272_spmd, ... | conditional | flops 2220293888 | bytes 77292728 | solution.py:472
  560.9 45.7 %conditional.38 = (bf16[4,56,768]{2,1,0:T(8,128)(2,1)}, bf16[4,56,768]{2,1,0:T(8,128)(2,1)}, bf16[4,56,768]{2,1,0:T(8,128)(2,1)}, f32[4,12,56,1]{2,1,0,3:T(8,128...) conditional(s32[]{:T(128)} %clamp.64, ...), branch_computations={%region_284.289_spmd, %region_289.294_spmd, %region_294.299_spmd, ... | conditional | flops 2086317312 | bytes 58705364 | solution.py:398
  586.6 6.3 fusion.2946
  606.7 77.9 %collective-permute-done.6 = bf16[4,56,768]{2,1,0:T(8,128)(2,1)} collective-permute-done((bf16[4,56,768]{2,1,0:T(8,128)(2,1)}, bf16[4,56,768]{2,1,0:T(8,128)(2,1)}, u32[]{:S(2)}, u32[]{:S(2)}) %collective-permute-start.6) | collective-permute-done | bytes 344096 | tf_op jit(solution)/shard_map/ppermute | solution.py:28
  686.6 69.3 %conditional.39 = (f32[4,56,768]{2,1,0:T(8,128)}, f32[3072]{0:T(1024)S(1)}, f32[3072,768]{1,0:T(8,128)}, f32[768]{0:T(1024)S(1)}, f32[768]{0:T(1024)S(1)}, /*index=5*/f32[768]{0:T(1024)S(1)}, f32[768,3072]{1,0:T(8,128)}) conditional(s32[]{:T(128)} %clamp.64, (f32[4,56,768]{2,1,0:T(8,128)}, f32[4,56,768]{2,1,0:T(8,128)}, ...), branch_computations={%region_305.314_spmd, %region_314.315_spmd, %region_315.324_spmd, ... | conditional | flops 2783878656 | bytes 104408480 | solution.py:455
  708.5 8.6 convert_reduce_fusion.20
  721.7 10.6 convolution_bitcast_fusion.24
  737.4 9.6 copy.2211
  756.7 100.9 %conditional.40 = (bf16[4,56,768]{2,1,0:T(8,128)(2,1)}, f32[768]{0:T(1024)S(1)}, f32[768]{0:T(1024)}, f32[768]{0:T(1024)S(1)}, f32[768]{0:T(1024)S(1)}, /*index=...) conditional(s32[]{:T(128)} %clamp.64, ...), branch_computations={%region_334.345_spmd, %region_345.356_spmd, %region_356.367_spmd, ... | conditional | flops 2220293888 | bytes 77292728 | solution.py:472
  859.6 45.7 %conditional.41 = (bf16[4,56,768]{2,1,0:T(8,128)(2,1)}, bf16[4,56,768]{2,1,0:T(8,128)(2,1)}, bf16[4,56,768]{2,1,0:T(8,128)(2,1)}, f32[4,12,56,1]{2,1,0,3:T(8,128...) conditional(s32[]{:T(128)} %clamp.65, ...), branch_computations={%region_379.384_spmd, %region_384.389_spmd, %region_389.394_spmd, ... | conditional | flops 2086317312 | bytes 58705364 | solution.py:398
  885.3 6.3 fusion.3550
  907.8 75.4 %conditional.42 = (f32[4,56,768]{2,1,0:T(8,128)}, f32[3072]{0:T(1024)S(1)}, f32[3072,768]{1,0:T(8,128)}, f32[768]{0:T(1024)S(1)}, f32[768]{0:T(1024)S(1)}, /*index=5*/f32[768]{0:T(1024)S(1)}, f32[768,3072]{1,0:T(8,128)}) conditional(s32[]{:T(128)} %clamp.65, (f32[4,56,768]{2,1,0:T(8,128)}, f32[4,56,768]{2,1,0:T(8,128)}, ...), branch_computations={%region_400.409_spmd, %region_409.410_spmd, %region_410.419_spmd, ... | conditional | flops 2783878656 | bytes 104408480 | solution.py:455
  935.8 8.6 convert_reduce_fusion.38
  949.0 10.7 convolution_bitcast_fusion.46
  964.7 9.6 copy.2236
  983.9 100.9 %conditional.43 = (bf16[4,56,768]{2,1,0:T(8,128)(2,1)}, f32[768]{0:T(1024)S(1)}, f32[768]{0:T(1024)}, f32[768]{0:T(1024)S(1)}, f32[768]{0:T(1024)S(1)}, /*index=...) conditional(s32[]{:T(128)} %clamp.65, ...), branch_computations={%region_429.440_spmd, %region_440.451_spmd, %region_451.462_spmd, ... | conditional | flops 2220293888 | bytes 77292728 | solution.py:472
  1086.9 45.9 %conditional.44 = (bf16[4,56,768]{2,1,0:T(8,128)(2,1)}, bf16[4,56,768]{2,1,0:T(8,128)(2,1)}, bf16[4,56,768]{2,1,0:T(8,128)(2,1)}, f32[4,12,56,1]{2,1,0,3:T(8,128...) conditional(s32[]{:T(128)} %clamp.66, ...), branch_computations={%region_474.479_spmd, %region_479.484_spmd, %region_484.489_spmd, ... | conditional | flops 2086317312 | bytes 58705364 | solution.py:398
  1112.7 6.3 fusion.4154
  1135.3 75.5 %conditional.45 = (f32[4,56,768]{2,1,0:T(8,128)}, f32[3072]{0:T(1024)S(1)}, f32[3072,768]{1,0:T(8,128)}, f32[768]{0:T(1024)S(1)}, f32[768]{0:T(1024)S(1)}, /*index=5*/f32[768]{0:T(1024)S(1)}, f32[768,3072]{1,0:T(8,128)}) conditional(s32[]{:T(128)} %clamp.66, (f32[4,56,768]{2,1,0:T(8,128)}, f32[4,56,768]{2,1,0:T(8,128)}, ...), branch_computations={%region_495.504_spmd, %region_504.505_spmd, %region_505.514_spmd, ... | conditional | flops 2783878656 | bytes 104408480 | solution.py:455
  1163.2 8.7 convert_reduce_fusion.56
  1176.4 10.8 convolution_bitcast_fusion.68
  1192.3 9.5 copy.2261
  1211.5 101.1 %conditional.46 = (bf16[4,56,768]{2,1,0:T(8,128)(2,1)}, f32[768]{0:T(1024)S(1)}, f32[768]{0:T(1024)}, f32[768]{0:T(1024)S(1)}, f32[768]{0:T(1024)S(1)}, /*index=...) conditional(s32[]{:T(128)} %clamp.66, ...), branch_computations={%region_524.535_spmd, %region_535.546_spmd, %region_546.557_spmd, ... | conditional | flops 2220293888 | bytes 77292728 | solution.py:472
  1314.6 45.8 %conditional.47 = (bf16[4,56,768]{2,1,0:T(8,128)(2,1)}, bf16[4,56,768]{2,1,0:T(8,128)(2,1)}, bf16[4,56,768]{2,1,0:T(8,128)(2,1)}, f32[4,12,56,1]{2,1,0,3:T(8,128...) conditional(s32[]{:T(128)} %clamp.67, ...), branch_computations={%region_569.574_spmd, %region_574.579_spmd, %region_579.584_spmd, ... | conditional | flops 2086317312 | bytes 58705364 | solution.py:398
  1340.4 6.3 fusion.4758
  1362.9 75.7 %conditional.48 = (f32[4,56,768]{2,1,0:T(8,128)}, f32[3072]{0:T(1024)S(1)}, f32[3072,768]{1,0:T(8,128)}, f32[768]{0:T(1024)S(1)}, f32[768]{0:T(1024)S(1)}, /*index=5*/f32[768]{0:T(1024)S(1)}, f32[768,3072]{1,0:T(8,128)}) conditional(s32[]{:T(128)} %clamp.67, (f32[4,56,768]{2,1,0:T(8,128)}, f32[4,56,768]{2,1,0:T(8,128)}, ...), branch_computations={%region_590.599_spmd, %region_599.600_spmd, %region_600.609_spmd, ... | conditional | flops 2783878656 | bytes 104408480 | solution.py:455
  1390.9 8.6 convert_reduce_fusion.74
  1404.1 10.8 convolution_bitcast_fusion.90
  1420.0 9.6 copy.2286
  1439.3 101.1 %conditional.49 = (bf16[4,56,768]{2,1,0:T(8,128)(2,1)}, f32[768]{0:T(1024)S(1)}, f32[768]{0:T(1024)}, f32[768]{0:T(1024)S(1)}, f32[768]{0:T(1024)S(1)}, /*index=...) conditional(s32[]{:T(128)} %clamp.67, ...), branch_computations={%region_619.630_spmd, %region_630.641_spmd, %region_641.652_spmd, ... | conditional | flops 2220293888 | bytes 77292728 | solution.py:472
  1542.4 25.1 %conditional.50 = (bf16[4,56,768]{2,1,0:T(8,128)(2,1)}, bf16[4,56,768]{2,1,0:T(8,128)(2,1)}, bf16[4,56,768]{2,1,0:T(8,128)(2,1)}, f32[4,12,56,1]{2,1,0,3:T(8,128...) conditional(s32[]{:T(128)} %clamp.68, ...), branch_computations={%region_664.669_spmd, %region_669.674_spmd, %region_674.679_spmd, ... | conditional | flops 2086317312 | bytes 58705364 | solution.py:398
  1570.0 25.8 %conditional.51 = (f32[4,56,768]{2,1,0:T(8,128)}, f32[3072]{0:T(1024)S(1)}, f32[3072,768]{1,0:T(8,128)}, f32[768]{0:T(1024)S(1)}, f32[768]{0:T(1024)S(1)}, /*index=5*/f32[768]{0:T(1024)S(1)}, f32[768,3072]{1,0:T(8,128)}) conditional(s32[]{:T(128)} %clamp.68, (f32[4,56,768]{2,1,0:T(8,128)}, f32[4,56,768]{2,1,0:T(8,128)}, ...), branch_computations={%region_685.694_spmd, %region_694.695_spmd, %region_695.704_spmd, ... | conditional | flops 2783878656 | bytes 104408480 | solution.py:455
  1596.5 32.7 %conditional.52 = (bf16[4,56,768]{2,1,0:T(8,128)(2,1)}, f32[768]{0:T(1024)S(1)}, f32[768]{0:T(1024)}, f32[768]{0:T(1024)S(1)}, f32[768]{0:T(1024)S(1)}, /*index=...) conditional(s32[]{:T(128)} %clamp.68, ...), branch_computations={%region_714.725_spmd, %region_725.736_spmd, %region_736.747_spmd, ... | conditional | flops 2220293888 | bytes 77292728 | solution.py:472
  1629.2 62.4 %collective-permute-start.11 = (bf16[4,56,768]{2,1,0:T(8,128)(2,1)}, bf16[4,56,768]{2,1,0:T(8,128)(2,1)}, u32[]{:S(2)}, u32[]{:S(2)}) collective-permute-start(bf16[4,56,768]{2,1,0:T(8,128)(2,1)} %get-tuple-element.4408), channel_id=1, source_target_pairs={{8,0},{16,8},{24,16},{9,1},{17,9},{25,17},{10,2},{18,10},{26,18},{... | collective-permute-start | bytes 1032200 | tf_op jit(solution)/shard_map/ppermute | solution.py:28
  1691.7 22.4 conditional.53
  1716.6 27.6 %conditional.54 = (f32[4,56,768]{2,1,0:T(8,128)}, f32[3072]{0:T(1024)S(1)}, f32[3072,768]{1,0:T(8,128)}, f32[768]{0:T(1024)}, f32[768]{0:T(1024)}, /*index=5*/f32[768]{0:T(1024)}, f32[768,3072]{1,0:T(8,128)}) conditional(s32[]{:T(128)} %clamp.69, (f32[4,56,768]{2,1,0:T(8,128)}, f32[4,56,768]{2,1,0:T(8,128)}, ...), branch_computations={%region_780.789_spmd, %region_789.790_spmd, %region_790.799_spmd, ... | conditional | flops 2783878656 | bytes 105302576 | solution.py:455
  1744.8 31.9 %conditional.55 = (bf16[4,56,768]{2,1,0:T(8,128)(2,1)}, f32[768]{0:T(1024)S(1)}, f32[768]{0:T(1024)S(1)}, f32[768]{0:T(1024)S(1)}, f32[768]{0:T(1024)S(1)}, /*in...) conditional(s32[]{:T(128)} %clamp.69, ...), branch_computations={%region_809.820_spmd, %region_820.831_spmd, %region_831.842_spmd, ... | conditional | flops 2220293888 | bytes 78669016 | solution.py:472
  1776.7 23.5 fusion.6462
  1800.2 24.4 %fusion.6461 = bf16[1,768,3072]{2,1,0:T(8,128)(2,1)} fusion(f32[768,3072]{1,0:T(8,128)} %get-tuple-element.5591, f32[768,3072]{1,0:T(8,128)} %get-tuple-element.5586, f32[768,3072]{1,0:T(8,128)} %get-tuple-element.5581, f32[768,3072]{1,0:T(8,128)} %get-tuple-element.5576, f32[768,3072]{1,0:T(8,128)} %get-tuple-element.5571, ...), kind=kLoop, calls=%fused_computation.9095 | loop fusion | flops 16515072 | bytes 70778880 | tf_op jit(solution)/shard_map/broadcast_in_dim | solution.py:513
  1824.7 12.3 fusion.6465
  1838.7 9.8 fusion.6463
  1851.8 15.1 conditional.34
  1868.7 101.0 %all-to-all-start = ((bf16[16,56,768]{2,1,0:T(8,128)(2,1)}), bf16[16,56,768]{2,1,0:T(8,128)(2,1)S(1)}, u32[]{:S(2)}, u32[]{:S(2)}) async-start(bf16[16,56,768]{2,1,0:T(8,128)(2,1)} %select_dynamic-update-slice_fusion.7), calls=%async_computation | async-start | bytes 2752512 | tf_op jit(solution)/shard_map/all_to_all | solution.py:507
  1975.3 10.7 all-to-all-done
  2002.8 35.1 %all-reduce.190 = (bf16[1,768]{1,0:T(2,128)(2,1)S(1)}, bf16[1,768]{1,0:T(2,128)(2,1)S(1)}, bf16[1,768]{1,0:T(2,128)(2,1)S(1)}, bf16[1,768]{1,0:T(2,128)(2,1)S(1)...) all-reduce(bf16[1,768]{1,0:T(2,128)(2,1)S(1)} %broadcast_in_dim.556, ...), channel_id=1, replica_groups=mesh['section'=4,'dp'=8] {'dp'}, use_global_device_ids=true, to_apply=%region_858.859 | all-reduce | flops 9216 | bytes 36864 | tf_op jit(solution)/shard_map/psum | solution.py:494
  2043.8 343.3 %all-reduce.194.cloned.1.call-done = (bf16[1,768,768]{2,1,0:T(8,128)(2,1)}, bf16[1,768,768]{2,1,0:T(8,128)(2,1)}, bf16[1,768,768]{2,1,0:T(8,128)(2,1)}, bf16[1,7...) async-done(((bf16[1,768,768]{2,1,0:T(8,128)(2,1)}, bf16[1,768,768]{2,1,0:T(8,128)(2,1)}, bf16[1,768,768]{2,1,0:T(8,128)(2,1)}, ...) | async-done | bytes 14155792 | tf_op jit(solution)/shard_map/psum | solution.py:490
  (1490 shorter events, 904.8 us)
Async XLA Ops:
  7.2 21.0 all-gather.3.cloned.1.call-start
  7.9 454.6 %all-gather.5.cloned.1.call-start = ((), (), s32[]{:S(2)}) async-start(), calls=%async_computation.3 | async-start | bytes 1720320 | tf_op jit(solution)/shard_map/all_gather | solution.py:349
  17.5 457.3 %copy-start.106 = (bf16[768]{0:T(1024)(128)(2,1)}, bf16[768]{0:T(1024)(128)(2,1)S(1)}, u32[]{:S(2)}) copy-start(bf16[768]{0:T(1024)(128)(2,1)S(1)} %reduce.402) | copy-start | bytes 4612
  18.2 456.6 %copy-start.186 = (bf16[768]{0:T(1024)(128)(2,1)}, bf16[768]{0:T(1024)(128)(2,1)S(1)}, u32[]{:S(2)}) copy-start(bf16[768]{0:T(1024)(128)(2,1)S(1)} %reduce.400) | copy-start | bytes 4612
  26.6 448.1 %copy-start.158 = (bf16[3072]{0:T(1024)(128)(2,1)}, bf16[3072]{0:T(1024)(128)(2,1)S(1)}, u32[]{:S(2)}) copy-start(bf16[3072]{0:T(1024)(128)(2,1)S(1)} %reduce.404) | copy-start | bytes 18436
  47.9 8.6 collective-permute-start
  77.5 57.1 %collective-permute-start.1 = (bf16[4,56,768]{2,1,0:T(8,128)(2,1)}, bf16[4,56,768]{2,1,0:T(8,128)(2,1)}, u32[]{:S(2)}, u32[]{:S(2)}) collective-permute-start(bf16[4,56,768]{2,1,0:T(8,128)(2,1)} %get-tuple-element.7497), channel_id=1, source_target_pairs={{0,8},{8,16},{16,24},{1,9},{9,17},{17,25},{2,10},{10,18},{18,26},{... | collective-permute-start | bytes 1032200 | tf_op jit(solution)/shard_map/ppermute | solution.py:28
  79.6 2307.6 %all-reduce.194.cloned.1.call-start = ((), (), s32[]{:S(2)}) async-start(), calls=%async_computation.4 | async-start | bytes 28311552 | tf_op jit(solution)/shard_map/psum | solution.py:490
  209.7 8.9 collective-permute-start.2
  293.7 8.9 collective-permute-start.3
  377.7 8.9 collective-permute-start.4
  460.5 8.9 collective-permute-start.5
  558.9 125.7 %collective-permute-start.6 = (bf16[4,56,768]{2,1,0:T(8,128)(2,1)}, bf16[4,56,768]{2,1,0:T(8,128)(2,1)}, u32[]{:S(2)}, u32[]{:S(2)}) collective-permute-start(bf16[4,56,768]{2,1,0:T(8,128)(2,1)} %get-tuple-element.4353), channel_id=1, source_target_pairs={{8,0},{16,8},{24,16},{9,1},{17,9},{25,17},{10,2},{18,10},{26,18},{... | collective-permute-start | bytes 1032200 | tf_op jit(solution)/shard_map/ppermute | solution.py:28
  560.9 125.7 %copy-start.317 = (bf16[768]{0:T(1024)(128)(2,1)S(1)}, bf16[768]{0:T(1024)(128)(2,1)}, u32[]{:S(2)}) copy-start(bf16[768]{0:T(1024)(128)(2,1)} %reduce.406) | copy-start | bytes 4612
  606.7 79.9 %copy-start.76 = (f32[4,56,768]{2,1,0:T(8,128)}, f32[4,56,768]{2,1,0:T(8,128)S(1)}, u32[]{:S(2)}) copy-start(f32[4,56,768]{2,1,0:T(8,128)S(1)} %get-tuple-element.4355) | copy-start | bytes 2064388
  606.7 79.9 %copy-start.247 = (bf16[4,56,768]{2,0,1:T(4,128)(2,1)}, bf16[4,56,768]{2,0,1:T(4,128)(2,1)S(1)}, u32[]{:S(2)}) copy-start(bf16[4,56,768]{2,0,1:T(4,128)(2,1)S(1)} %get-tuple-element.4363) | copy-start | bytes 1032196
  606.7 79.9 %copy-start.610 = (f32[4,12,56,1]{2,1,0,3:T(8,128)}, f32[4,12,56,1]{2,1,0,3:T(8,128)S(1)}, u32[]{:S(2)}) copy-start(f32[4,12,56,1]{2,1,0,3:T(8,128)S(1)} %get-tuple-element.4361) | copy-start | bytes 32260
  756.6 102.9 %copy-start.96 = (bf16[4,56,768]{2,1,0:T(8,128)(2,1)S(1)}, bf16[4,56,768]{2,1,0:T(8,128)(2,1)}, u32[]{:S(2)}) copy-start(bf16[4,56,768]{2,1,0:T(8,128)(2,1)} %get-tuple-element.6553) | copy-start | bytes 1032196
  756.6 102.9 %copy-start.160 = (bf16[3072]{0:T(1024)(128)(2,1)S(1)}, bf16[3072]{0:T(1024)(128)(2,1)}, u32[]{:S(2)}) copy-start(bf16[3072]{0:T(1024)(128)(2,1)} %copy-done.158) | copy-start | bytes 18436
  756.6 102.9 %copy-start.188 = (bf16[768]{0:T(1024)(128)(2,1)S(1)}, bf16[768]{0:T(1024)(128)(2,1)}, u32[]{:S(2)}) copy-start(bf16[768]{0:T(1024)(128)(2,1)} %copy-done.186) | copy-start | bytes 4612
  756.6 102.9 %copy-start.196 = (bf16[768]{0:T(1024)(128)(2,1)S(1)}, bf16[768]{0:T(1024)(128)(2,1)}, u32[]{:S(2)}) copy-start(bf16[768]{0:T(1024)(128)(2,1)} %reduce.399) | copy-start | bytes 4612
  756.6 102.9 %copy-start.204 = (bf16[768]{0:T(1024)(128)(2,1)S(1)}, bf16[768]{0:T(1024)(128)(2,1)}, u32[]{:S(2)}) copy-start(bf16[768]{0:T(1024)(128)(2,1)} %reduce.401) | copy-start | bytes 4612
  756.6 102.9 %copy-start.212 = (bf16[768]{0:T(1024)(128)(2,1)S(1)}, bf16[768]{0:T(1024)(128)(2,1)}, u32[]{:S(2)}) copy-start(bf16[768]{0:T(1024)(128)(2,1)} %reduce.403) | copy-start | bytes 4612
  756.6 102.9 %copy-start.325 = (bf16[768]{0:T(1024)(128)(2,1)S(1)}, bf16[768]{0:T(1024)(128)(2,1)}, u32[]{:S(2)}) copy-start(bf16[768]{0:T(1024)(128)(2,1)} %reduce.405) | copy-start | bytes 4612
  857.6 47.8 %collective-permute-start.7 = (bf16[4,56,768]{2,1,0:T(8,128)(2,1)}, bf16[4,56,768]{2,1,0:T(8,128)(2,1)}, u32[]{:S(2)}, u32[]{:S(2)}) collective-permute-start(bf16[4,56,768]{2,1,0:T(8,128)(2,1)} %get-tuple-element.4364), channel_id=1, source_target_pairs={{8,0},{16,8},{24,16},{9,1},{17,9},{25,17},{10,2},{18,10},{26,18},{... | collective-permute-start | bytes 1032200 | tf_op jit(solution)/shard_map/ppermute | solution.py:28
  983.8 103.0 %copy-start.92 = (bf16[4,56,768]{2,1,0:T(8,128)(2,1)S(1)}, bf16[4,56,768]{2,1,0:T(8,128)(2,1)}, u32[]{:S(2)}) copy-start(bf16[4,56,768]{2,1,0:T(8,128)(2,1)} %get-tuple-element.6552) | copy-start | bytes 1032196
  983.8 103.0 %copy-start.161 = (bf16[3072]{0:T(1024)(128)(2,1)S(1)}, bf16[3072]{0:T(1024)(128)(2,1)}, u32[]{:S(2)}) copy-start(bf16[3072]{0:T(1024)(128)(2,1)} %copy-done.158) | copy-start | bytes 18436
  983.9 103.0 %copy-start.189 = (bf16[768]{0:T(1024)(128)(2,1)S(1)}, bf16[768]{0:T(1024)(128)(2,1)}, u32[]{:S(2)}) copy-start(bf16[768]{0:T(1024)(128)(2,1)} %copy-done.186) | copy-start | bytes 4612
  983.9 103.0 %copy-start.197 = (bf16[768]{0:T(1024)(128)(2,1)S(1)}, bf16[768]{0:T(1024)(128)(2,1)}, u32[]{:S(2)}) copy-start(bf16[768]{0:T(1024)(128)(2,1)} %reduce.399) | copy-start | bytes 4612
  983.9 103.0 %copy-start.205 = (bf16[768]{0:T(1024)(128)(2,1)S(1)}, bf16[768]{0:T(1024)(128)(2,1)}, u32[]{:S(2)}) copy-start(bf16[768]{0:T(1024)(128)(2,1)} %reduce.401) | copy-start | bytes 4612
  983.9 103.0 %copy-start.213 = (bf16[768]{0:T(1024)(128)(2,1)S(1)}, bf16[768]{0:T(1024)(128)(2,1)}, u32[]{:S(2)}) copy-start(bf16[768]{0:T(1024)(128)(2,1)} %reduce.403) | copy-start | bytes 4612
  983.9 103.0 %copy-start.326 = (bf16[768]{0:T(1024)(128)(2,1)S(1)}, bf16[768]{0:T(1024)(128)(2,1)}, u32[]{:S(2)}) copy-start(bf16[768]{0:T(1024)(128)(2,1)} %reduce.405) | copy-start | bytes 4612
  1084.9 48.0 %collective-permute-start.8 = (bf16[4,56,768]{2,1,0:T(8,128)(2,1)}, bf16[4,56,768]{2,1,0:T(8,128)(2,1)}, u32[]{:S(2)}, u32[]{:S(2)}) collective-permute-start(bf16[4,56,768]{2,1,0:T(8,128)(2,1)} %get-tuple-element.4375), channel_id=1, source_target_pairs={{8,0},{16,8},{24,16},{9,1},{17,9},{25,17},{10,2},{18,10},{26,18},{... | collective-permute-start | bytes 1032200 | tf_op jit(solution)/shard_map/ppermute | solution.py:28
  1135.2 76.2 %copy-start.4 = (bf16[1,768,768]{2,1,0:T(8,128)(2,1)S(1)}, bf16[1,768,768]{2,1,0:T(8,128)(2,1)}, u32[]{:S(2)}) copy-start(bf16[1,768,768]{2,1,0:T(8,128)(2,1)} %param.162) | copy-start | bytes 3538948
  1211.4 103.1 %copy-start.88 = (bf16[4,56,768]{2,1,0:T(8,128)(2,1)S(1)}, bf16[4,56,768]{2,1,0:T(8,128)(2,1)}, u32[]{:S(2)}) copy-start(bf16[4,56,768]{2,1,0:T(8,128)(2,1)} %get-tuple-element.6551) | copy-start | bytes 1032196
  1211.4 103.1 %copy-start.162 = (bf16[3072]{0:T(1024)(128)(2,1)S(1)}, bf16[3072]{0:T(1024)(128)(2,1)}, u32[]{:S(2)}) copy-start(bf16[3072]{0:T(1024)(128)(2,1)} %copy-done.158) | copy-start | bytes 18436
  1211.4 103.1 %copy-start.190 = (bf16[768]{0:T(1024)(128)(2,1)S(1)}, bf16[768]{0:T(1024)(128)(2,1)}, u32[]{:S(2)}) copy-start(bf16[768]{0:T(1024)(128)(2,1)} %copy-done.186) | copy-start | bytes 4612
  1211.4 103.1 %copy-start.198 = (bf16[768]{0:T(1024)(128)(2,1)S(1)}, bf16[768]{0:T(1024)(128)(2,1)}, u32[]{:S(2)}) copy-start(bf16[768]{0:T(1024)(128)(2,1)} %reduce.399) | copy-start | bytes 4612
  1211.4 103.1 %copy-start.206 = (bf16[768]{0:T(1024)(128)(2,1)S(1)}, bf16[768]{0:T(1024)(128)(2,1)}, u32[]{:S(2)}) copy-start(bf16[768]{0:T(1024)(128)(2,1)} %reduce.401) | copy-start | bytes 4612
  1211.4 103.1 %copy-start.214 = (bf16[768]{0:T(1024)(128)(2,1)S(1)}, bf16[768]{0:T(1024)(128)(2,1)}, u32[]{:S(2)}) copy-start(bf16[768]{0:T(1024)(128)(2,1)} %reduce.403) | copy-start | bytes 4612
  1211.4 103.1 %copy-start.327 = (bf16[768]{0:T(1024)(128)(2,1)S(1)}, bf16[768]{0:T(1024)(128)(2,1)}, u32[]{:S(2)}) copy-start(bf16[768]{0:T(1024)(128)(2,1)} %reduce.405) | copy-start | bytes 4612
  1312.6 47.9 %collective-permute-start.9 = (bf16[4,56,768]{2,1,0:T(8,128)(2,1)}, bf16[4,56,768]{2,1,0:T(8,128)(2,1)}, u32[]{:S(2)}, u32[]{:S(2)}) collective-permute-start(bf16[4,56,768]{2,1,0:T(8,128)(2,1)} %get-tuple-element.4386), channel_id=1, source_target_pairs={{8,0},{16,8},{24,16},{9,1},{17,9},{25,17},{10,2},{18,10},{26,18},{... | collective-permute-start | bytes 1032200 | tf_op jit(solution)/shard_map/ppermute | solution.py:28
  1362.8 76.3 %copy-start.5 = (bf16[1,768,768]{2,1,0:T(8,128)(2,1)S(1)}, bf16[1,768,768]{2,1,0:T(8,128)(2,1)}, u32[]{:S(2)}) copy-start(bf16[1,768,768]{2,1,0:T(8,128)(2,1)} %param.162) | copy-start | bytes 3538948
  1362.9 76.3 %copy-start.13 = (bf16[1,768,768]{2,1,0:T(8,128)(2,1)S(1)}, bf16[1,768,768]{2,1,0:T(8,128)(2,1)}, u32[]{:S(2)}) copy-start(bf16[1,768,768]{2,1,0:T(8,128)(2,1)} %param.164) | copy-start | bytes 3538948
  1362.9 76.3 %copy-start.111 = (bf16[768]{0:T(1024)(128)(2,1)S(1)}, bf16[768]{0:T(1024)(128)(2,1)}, u32[]{:S(2)}) copy-start(bf16[768]{0:T(1024)(128)(2,1)} %copy-done.106) | copy-start | bytes 4612
  1362.9 76.3 %copy-start.670 = (f32[4,12]{1,0:T(4,128)S(1)}, f32[4,12]{1,0:T(4,128)}, u32[]{:S(2)}) copy-start(f32[4,12]{1,0:T(4,128)} %get-tuple-element.6558) | copy-start | bytes 580
  1439.2 103.1 %copy-start.84 = (bf16[4,56,768]{2,1,0:T(8,128)(2,1)S(1)}, bf16[4,56,768]{2,1,0:T(8,128)(2,1)}, u32[]{:S(2)}) copy-start(bf16[4,56,768]{2,1,0:T(8,128)(2,1)} %get-tuple-element.6550) | copy-start | bytes 1032196
  1439.2 103.1 %copy-start.163 = (bf16[3072]{0:T(1024)(128)(2,1)S(1)}, bf16[3072]{0:T(1024)(128)(2,1)}, u32[]{:S(2)}) copy-start(bf16[3072]{0:T(1024)(128)(2,1)} %copy-done.158) | copy-start | bytes 18436
  1439.2 103.1 %copy-start.191 = (bf16[768]{0:T(1024)(128)(2,1)S(1)}, bf16[768]{0:T(1024)(128)(2,1)}, u32[]{:S(2)}) copy-start(bf16[768]{0:T(1024)(128)(2,1)} %copy-done.186) | copy-start | bytes 4612
  1439.2 103.1 %copy-start.199 = (bf16[768]{0:T(1024)(128)(2,1)S(1)}, bf16[768]{0:T(1024)(128)(2,1)}, u32[]{:S(2)}) copy-start(bf16[768]{0:T(1024)(128)(2,1)} %reduce.399) | copy-start | bytes 4612
  1439.2 103.1 %copy-start.207 = (bf16[768]{0:T(1024)(128)(2,1)S(1)}, bf16[768]{0:T(1024)(128)(2,1)}, u32[]{:S(2)}) copy-start(bf16[768]{0:T(1024)(128)(2,1)} %reduce.401) | copy-start | bytes 4612
  1439.2 103.1 %copy-start.215 = (bf16[768]{0:T(1024)(128)(2,1)S(1)}, bf16[768]{0:T(1024)(128)(2,1)}, u32[]{:S(2)}) copy-start(bf16[768]{0:T(1024)(128)(2,1)} %reduce.403) | copy-start | bytes 4612
  1439.3 103.1 %copy-start.328 = (bf16[768]{0:T(1024)(128)(2,1)S(1)}, bf16[768]{0:T(1024)(128)(2,1)}, u32[]{:S(2)}) copy-start(bf16[768]{0:T(1024)(128)(2,1)} %reduce.405) | copy-start | bytes 4612
  1540.4 27.2 %collective-permute-start.10 = (bf16[4,56,768]{2,1,0:T(8,128)(2,1)}, bf16[4,56,768]{2,1,0:T(8,128)(2,1)}, u32[]{:S(2)}, u32[]{:S(2)}) collective-permute-start(bf16[4,56,768]{2,1,0:T(8,128)(2,1)} %get-tuple-element.4397), channel_id=1, source_target_pairs={{8,0},{16,8},{24,16},{9,1},{17,9},{25,17},{10,2},{18,10},{26,18},{... | collective-permute-start | bytes 1032200 | tf_op jit(solution)/shard_map/ppermute | solution.py:28
  1596.4 95.2 %copy-start.82 = (bf16[4,56,768]{2,1,0:T(8,128)(2,1)S(1)}, bf16[4,56,768]{2,1,0:T(8,128)(2,1)}, u32[]{:S(2)}) copy-start(bf16[4,56,768]{2,1,0:T(8,128)(2,1)} %get-tuple-element.6549) | copy-start | bytes 1032196
  1596.4 95.2 %copy-start.164 = (bf16[3072]{0:T(1024)(128)(2,1)S(1)}, bf16[3072]{0:T(1024)(128)(2,1)}, u32[]{:S(2)}) copy-start(bf16[3072]{0:T(1024)(128)(2,1)} %copy-done.158) | copy-start | bytes 18436
  1596.5 95.2 %copy-start.192 = (bf16[768]{0:T(1024)(128)(2,1)S(1)}, bf16[768]{0:T(1024)(128)(2,1)}, u32[]{:S(2)}) copy-start(bf16[768]{0:T(1024)(128)(2,1)} %copy-done.186) | copy-start | bytes 4612
  1596.5 95.2 %copy-start.200 = (bf16[768]{0:T(1024)(128)(2,1)S(1)}, bf16[768]{0:T(1024)(128)(2,1)}, u32[]{:S(2)}) copy-start(bf16[768]{0:T(1024)(128)(2,1)} %reduce.399) | copy-start | bytes 4612
  1596.5 95.2 %copy-start.208 = (bf16[768]{0:T(1024)(128)(2,1)S(1)}, bf16[768]{0:T(1024)(128)(2,1)}, u32[]{:S(2)}) copy-start(bf16[768]{0:T(1024)(128)(2,1)} %reduce.401) | copy-start | bytes 4612
  1596.5 95.2 %copy-start.216 = (bf16[768]{0:T(1024)(128)(2,1)S(1)}, bf16[768]{0:T(1024)(128)(2,1)}, u32[]{:S(2)}) copy-start(bf16[768]{0:T(1024)(128)(2,1)} %reduce.403) | copy-start | bytes 4612
  1596.5 95.2 %copy-start.329 = (bf16[768]{0:T(1024)(128)(2,1)S(1)}, bf16[768]{0:T(1024)(128)(2,1)}, u32[]{:S(2)}) copy-start(bf16[768]{0:T(1024)(128)(2,1)} %reduce.405) | copy-start | bytes 4612
  1629.2 85.0 %collective-permute-start.11 = (bf16[4,56,768]{2,1,0:T(8,128)(2,1)}, bf16[4,56,768]{2,1,0:T(8,128)(2,1)}, u32[]{:S(2)}, u32[]{:S(2)}) collective-permute-start(bf16[4,56,768]{2,1,0:T(8,128)(2,1)} %get-tuple-element.4408), channel_id=1, source_target_pairs={{8,0},{16,8},{24,16},{9,1},{17,9},{25,17},{10,2},{18,10},{26,18},{... | collective-permute-start | bytes 1032200 | tf_op jit(solution)/shard_map/ppermute | solution.py:28
  1868.7 117.3 %all-to-all-start = ((bf16[16,56,768]{2,1,0:T(8,128)(2,1)}), bf16[16,56,768]{2,1,0:T(8,128)(2,1)S(1)}, u32[]{:S(2)}, u32[]{:S(2)}) async-start(bf16[16,56,768]{2,1,0:T(8,128)(2,1)} %select_dynamic-update-slice_fusion.7), calls=%async_computation | async-start | bytes 2752512 | tf_op jit(solution)/shard_map/all_to_all | solution.py:507
  1994.4 48.7 %all-to-all-start.1 = ((bf16[16,56,768]{2,1,0:T(8,128)(2,1)}), bf16[16,56,768]{2,1,0:T(8,128)(2,1)S(1)}, u32[]{:S(2)}, u32[]{:S(2)}) async-start(bf16[16,56,768]{2,1,0:T(8,128)(2,1)} %select_dynamic-update-slice_fusion), calls=%async_computation.1 | async-start | bytes 2752512 | tf_op jit(solution)/shard_map/all_to_all | solution.py:508
  (279 other events, 3118.8 us)
Sparse Core Ops, SparseCore 0:
  9.6 18.5 all-gather.2
  79.7 84.4 all-gather.4
  1848.7 538.3 all-reduce.193
where the time goes:
time: 2430 us; the launch traced here: 2410 us
  waiting for transfers between devices  521 us (21%)
  loops' own time  517 us (21%)
  local copies, waits for them, and re-layouts  481 us (20%)
  matrix products  348 us (14%)
  other arithmetic  296 us (12%)
  starting transfers between devices  190 us (8%)
  blocking collectives  40.9 us (2%)
    psum x1, waiting for transfers between devices, per_device(): lax.psum(sum_w_query.astype(jnp.bfloat16), 'dp').astype(jnp.float32)  343 us
    another operation x14, loops' own time, run_forward(): return lax.switch(branch, options)  241 us
    another operation x7, loops' own time, per_device(): grad_back, attn_terms = lax.switch(branch, attn_options)  170 us
    ppermute x12, waiting for transfers between devices, shifted_2(): lax.ppermute(value, axis, [(source, source + steps) for source in range(f...  165 us
    another operation x7, loops' own time, per_device(): grad_middle, ffn_terms = lax.switch(branch, ffn_options)  106 us
    all_to_all x1, starting transfers between devices, per_device(): lax.all_to_all(finished, 'section', split_axis=0, concat_axis=0, tiled=True)  101 us
    another operation x96, local copies, waits for them, and re-layouts  94.9 us
    broadcast_in_dim x19, other arithmetic, per_device(): outputs = tuple((total[None] for total in summed))  92.5 us
  transfers between devices with their start and end apart: 17, of which 10 were waited for; matrix products, arithmetic and copies ran while one was open for 16% of the time, Pallas kernels for 0%

commit v1 on v0

v1 whole, which is shorter than its diff:
```python
import jax
import jax.numpy as jnp
from jax import lax
from jax.experimental import pallas as pl
from jax.experimental.pallas import tpu as pltpu
from jax.sharding import PartitionSpec as P

HEADS = 12
HEAD_DIM = 64
OBJ = 36
PAIRS = HEADS // 2
EPS = 1e-06
NEG = -1000000000.0
F32 = jnp.float32
BF16 = jnp.bfloat16
LANES = 128
BLOCKS = 4
EXTRA = 32
VMEM = 60 * 1024 * 1024


def mm(a, b):
    return jnp.dot(a, b, preferred_element_type=F32)


def mm_nt(a, b):
    return lax.dot_general(a, b, (((1,), (1,)), ((), ())), preferred_element_type=F32)


def mm_tn(a, b):
    return lax.dot_general(a, b, (((0,), (0,)), ((), ())), preferred_element_type=F32)


def each_rows(count, step, body):
    def turn(i, carry):
        body(pl.ds(pl.multiple_of(i * step, step), step))
        return carry

    lax.fori_loop(0, count // step, turn, 0)


def folded(values):
    rows, width = values.shape
    return jnp.sum(values.reshape(rows // 8, 8, width), 0)


class Copies:
    def __init__(self, sems):
        self.sems, self.used, self.stores = sems, 0, []

    def next_sem(self):
        self.used += 1
        return self.sems.at[self.used - 1]

    def load(self, source, target):
        copy = pltpu.make_async_copy(source, target, self.next_sem())
        copy.start()
        return copy

    def load_either(self, first, own, other, target):
        sem = self.next_sem()
        mine = pltpu.make_async_copy(own, target, sem)

        @pl.when(first)
        def _():
            mine.start()

        @pl.when(jnp.logical_not(first))
        def _():
            pltpu.make_async_copy(other, target, sem).start()

        return mine

    def store(self, source, target):
        copy = pltpu.make_async_copy(source, target, self.next_sem())
        copy.start()
        self.stores.append(copy)

    def store_either(self, first, source, target, other):
        sem = self.next_sem()
        mine = pltpu.make_async_copy(source, target, sem)

        @pl.when(first)
        def _():
            mine.start()

        @pl.when(jnp.logical_not(first))
        def _():
            pltpu.make_async_copy(source, other, sem).start()

        self.stores.append(mine)

    def drain(self):
        for copy in self.stores:
            copy.wait()
        self.stores = []


def kernel_call(
    body, control, inputs, outs, scratch, sems, flops, moved, name, aliases=None, with_block=False
):
    n_in, n_out = len(inputs), len(outs)

    def kernel(control_ref, *refs):
        @pl.when(control_ref[0] == 1)
        def _():
            body(
                control_ref[1] == 1,
                *([control_ref[2]] if with_block else []),
                refs[:n_in],
                refs[n_in : n_in + n_out],
                refs[n_in + n_out : -1],
                Copies(refs[-1]),
            )

    return pl.pallas_call(
        kernel,
        out_shape=[jax.ShapeDtypeStruct(shape, kind) for shape, kind in outs],
        in_specs=[pl.BlockSpec(memory_space=pltpu.SMEM)]
        + [pl.BlockSpec(memory_space=pl.ANY)] * n_in,
        out_specs=[pl.BlockSpec(memory_space=pl.ANY)] * n_out,
        scratch_shapes=[pltpu.VMEM(shape, kind) for shape, kind in scratch]
        + [pltpu.SemaphoreType.DMA((sems,))],
        input_output_aliases=aliases or {},
        compiler_params=pltpu.CompilerParams(vmem_limit_bytes=VMEM),
        cost_estimate=pl.CostEstimate(flops=flops, bytes_accessed=moved, transcendentals=0),
        name=name,
    )(control, *inputs)


def norm_stats(values):
    centered = values - jnp.mean(values, -1, keepdims=True)
    inverse = lax.rsqrt(jnp.mean(centered * centered, -1, keepdims=True) + EPS)
    return centered * inverse, inverse


def norm_back(grad_out, normed, inverse, gain):
    scaled = grad_out * gain
    return inverse * (
        scaled
        - jnp.mean(scaled, -1, keepdims=True)
        - normed * jnp.mean(scaled * normed, -1, keepdims=True)
    )


def head_keep(pair, flags):
    lane = lax.broadcasted_iota(jnp.int32, flags.shape, 1)
    head = 2 * pair + jnp.where(lane >= HEAD_DIM, 1, 0)
    return jnp.where(lax.rem(head, 3).astype(F32) != flags, 1.0, 0.0)


def half_masks(rows):
    lane = lax.broadcasted_iota(jnp.int32, (rows, LANES), 1)
    low = jnp.where(lane < HEAD_DIM, 1.0, 0.0)
    return low.astype(BF16), (1.0 - low).astype(BF16), lane < HEAD_DIM


def stacked_halves(piece, low, high):
    return jnp.concatenate([piece * low, piece * high], 0)


def attn_forward(control, xs, flags, vecs, weights, blocks, final, name):
    rows = sum(x.shape[0] for x in xs)
    width = xs[0].shape[1]
    probs_shapes = [((PAIRS, 2 * nq, nk), BF16) for _, nq, _, _, nk, _ in blocks]
    narrow, wide = ((rows, width), BF16), ((rows, width), F32)
    tails = [((x.shape[0], width), BF16) for x in xs] if final else [wide, narrow]
    n_x, n_b, n_t = len(xs), len(blocks), len(tails)
    n_rest = 4

    def body(first, ins, outs, scr, copies):
        x_in, flags_in, vec_in, w_in = ins[:n_x], ins[n_x], ins[n_x + 1 : n_x + 3], ins[n_x + 3 :]
        x_s, flags_s, vec_s, w_s, q_s, k_s, v_s, ctx_s, before_s, tail_s = scr[:10]
        probs_s = scr[10:]
        at, x_loads = 0, []
        for piece in x_in:
            x_loads.append(copies.load(piece, x_s.at[pl.ds(at, piece.shape[0])]))
            at += piece.shape[0]
        vec_load = copies.load_either(first, vec_in[0], vec_in[1], vec_s)
        w_loads = [
            copies.load_either(first, w_in[2 * i], w_in[2 * i + 1], w_s.at[i]) for i in range(4)
        ]
        flags_load = copies.load(flags_in, flags_s)
        for load in x_loads:
            load.wait()
        vec_load.wait()
        vec = vec_s[...].astype(F32)
        for i, (target, bias) in enumerate(((q_s, 0), (k_s, None), (v_s, 1))):
            w_loads[i].wait()
            product = mm(x_s[...], w_s[i])
            if bias is not None:
                product = product + vec[bias : bias + 1]
            target[...] = product.astype(BF16)
        copies.store(q_s, outs[0])
        copies.store(k_s, outs[1])
        copies.store(v_s, outs[2])
        flags_load.wait()
        for index, (q0, nq, iq, k0, nk, ik) in enumerate(blocks):
            low, high, is_low = half_masks(nq)
            row = lax.broadcasted_iota(jnp.int32, (nq, nk), 0) // iq
            col = lax.broadcasted_iota(jnp.int32, (nq, nk), 1) // ik
            same = jnp.where(row == col, 0.0, 1.0)
            same = jnp.concatenate([same, same], 0)

            def pair_turn(pair, carry):
                lanes = pl.ds(pl.multiple_of(pair * LANES, LANES), LANES)
                q2 = stacked_halves(q_s[pl.ds(q0, nq), lanes], low, high)
                scores = mm_nt(q2, k_s[pl.ds(k0, nk), lanes]) * (HEAD_DIM ** (-0.5))
                scores = jnp.where(same > 0.0, NEG, scores)
                shifted = jnp.exp(scores - jnp.max(scores, -1, keepdims=True))
                probs = (shifted / jnp.sum(shifted, -1, keepdims=True)).astype(BF16)
                probs_s[index][pair] = probs
                mixed = mm(probs, v_s[pl.ds(k0, nk), lanes])
                keep = head_keep(pair, flags_s[pl.ds(q0, nq), :])
                ctx = jnp.where(is_low, mixed[:nq], mixed[nq:]) * keep
                ctx_s[pl.ds(q0, nq), lanes] = ctx.astype(BF16)
                return carry

            lax.fori_loop(0, PAIRS, pair_turn, 0, unroll=2)
            copies.store(probs_s[index], outs[5 + index])
        copies.store(ctx_s, outs[3])
        w_loads[3].wait()
        before_s[...] = mm(ctx_s[...], w_s[3])

        def finish(where):
            before = x_s[where, :].astype(F32) + (before_s[where, :] + vec[2:3])
            before_s[where, :] = before
            normed, _ = norm_stats(before)
            middle = normed * vec[3:4] + vec[4:5]
            tail_s[where, :] = middle.astype(tail_s.dtype)
            if not final:
                q_s[where, :] = middle.astype(BF16)

        if not final:
            copies.drain()
        each_rows(rows, 32, finish)
        copies.store(before_s, outs[4])
        if final:
            at = 0
            for target in outs[5 + n_b :]:
                copies.store(tail_s.at[pl.ds(at, target.shape[0])], target)
                at += target.shape[0]
        else:
            copies.store(tail_s, outs[5 + n_b])
            copies.store(q_s, outs[6 + n_b])
        copies.drain()

    outs = [narrow] * 4 + [wide] + probs_shapes + tails
    scratch = (
        [narrow, ((rows, LANES), F32), ((16, width), BF16), ((4, width, width), BF16)]
        + [narrow] * 4
        + [wide, ((rows, width), BF16 if final else F32)]
        + probs_shapes
    )
    flat = [w for pair in weights for w in pair]
    return kernel_call(
        body,
        control,
        list(xs) + [flags] + list(vecs) + flat,
        outs,
        scratch,
        n_x + 6 + n_rest + n_b + 1 + n_t,
        8 * rows * width * width,
        8 * width * width + 20 * rows * width,
        name,
    )


def ffn_forward(control, middle, vecs, w_inner, w_outer, name):
    rows, width = middle.shape
    narrow, wide = ((rows, width), BF16), ((rows, width), F32)
    hidden = ((BLOCKS, rows, width), BF16)

    def body(first, ins, outs, scr, copies):
        middle_in, vec_a, vec_b, wi_a, wi_b, wo_a, wo_b = ins
        mid_s, vec_s, wi_s, wo_s, mb_s, inner_s, acc_s, act_s, slope_s, out_s = scr
        mid_load = copies.load(middle_in, mid_s)
        vec_load = copies.load_either(first, vec_a, vec_b, vec_s)
        wi_loads, wo_loads = [], []
        for j in range(BLOCKS):
            part = pl.ds(j * width, width)
            wi_loads.append(
                copies.load_either(first, wi_a.at[:, part], wi_b.at[:, part], wi_s.at[j])
            )
            wo_loads.append(
                copies.load_either(first, wo_a.at[part, :], wo_b.at[part, :], wo_s.at[j])
            )
        mid_load.wait()
        vec_load.wait()
        vec = vec_s[...].astype(F32)
        mb_s[...] = mid_s[...].astype(BF16)
        for j in range(BLOCKS):
            wi_loads[j].wait()
            inner_s[...] = mm(mb_s[...], wi_s[j])

            def activate(where):
                inner = inner_s[where, :] + vec[8 + j : 9 + j]
                phi = 0.5 * (1.0 + lax.erf(inner * (0.5**0.5)))
                act_s[where, :] = (inner * phi).astype(BF16)
                density = jnp.exp(-0.5 * inner * inner) * 0.3989422804014327
                slope_s[j, where, :] = (phi + inner * density).astype(BF16)

            each_rows(rows, 16, activate)
            copies.store(slope_s.at[j], outs[0].at[j])
            wo_loads[j].wait()
            product = mm(act_s[...], wo_s[j])
            acc_s[...] = product if j == 0 else acc_s[...] + product

        def finish(where):
            after = mid_s[where, :] + (acc_s[where, :] + vec[5:6])
            acc_s[where, :] = after
            normed, _ = norm_stats(after)
            out_s[where, :] = (normed * vec[6:7] + vec[7:8]).astype(BF16)

        each_rows(rows, 32, finish)
        copies.store(acc_s, outs[1])
        copies.store(out_s, outs[2])
        copies.drain()

    weights = ((BLOCKS, width, width), BF16)
    return kernel_call(
        body,
        control,
        [middle] + list(vecs) + list(w_inner) + list(w_outer),
        [hidden, wide, narrow],
        [wide, ((16, width), BF16), weights, weights, narrow, wide, wide, narrow, hidden, narrow],
        2 + 4 * BLOCKS + 2,
        16 * rows * width * width,
        16 * width * width + 26 * rows * width,
        name,
    )


def ffn_backward(control, grad_out, middle, saved, vecs, w_inner, w_outer, buffer, name):
    slope, after = saved
    rows, width = grad_out.shape
    narrow, wide = ((rows, width), BF16), ((rows, width), F32)
    hidden = ((BLOCKS, rows, width), BF16)

    def body(first, ins, outs, scr, copies):
        g_in, mid_in, slope_in, after_in, vec_a, vec_b, wi_a, wi_b, wo_a, wo_b = ins[:10]
        gmid_out, extra_out, pair_out = outs
        g_s, mid_s, slope_s, after_s, vec_s, wi_s, wo_s, go_s, gi_s, acc_s, sums_s, extra_s = scr
        g_load = copies.load(g_in, g_s)
        after_load = copies.load(after_in, after_s)
        vec_load = copies.load_either(first, vec_a, vec_b, vec_s)
        loads = []
        for j in range(BLOCKS):
            part = pl.ds(j * width, width)
            loads.append(
                (
                    copies.load_either(first, wo_a.at[part, :], wo_b.at[part, :], wo_s.at[j]),
                    copies.load(slope_in.at[j], slope_s.at[j]),
                    copies.load_either(first, wi_a.at[:, part], wi_b.at[:, part], wi_s.at[j]),
                )
            )
        mid_load = copies.load(mid_in, mid_s)
        g_load.wait()
        after_load.wait()
        vec_load.wait()
        vec = vec_s[...].astype(F32)
        sums_s[...] = jnp.zeros_like(sums_s)

        def start(where):
            grad = g_s[where, :].astype(F32)
            normed, inverse = norm_stats(after_s[where, :])
            sums_s[0] += folded(grad * normed)
            sums_s[1] += folded(grad)
            grad_after = norm_back(grad, normed, inverse, vec[6:7])
            acc_s[where, :] = grad_after
            rounded = grad_after.astype(BF16)
            go_s[where, :] = rounded
            sums_s[2] += folded(rounded.astype(F32))

        each_rows(rows, 32, start)
        copies.store(go_s, pair_out.at[pl.ds(rows, rows)])
        extra_s[...] = jnp.zeros_like(extra_s)
        for i in range(3):
            extra_s[i : i + 1, :] = jnp.sum(sums_s[i], 0, keepdims=True)
        copies.store(extra_s, extra_out)
        for j in range(BLOCKS):
            for load in loads[j]:
                load.wait()
            gi_s[...] = (mm_nt(go_s[...], wo_s[j]) * slope_s[j].astype(F32)).astype(BF16)
            acc_s[...] += mm_nt(gi_s[...], wi_s[j])
        copies.store(acc_s, gmid_out)
        mid_load.wait()
        copies.store(mid_s, pair_out.at[pl.ds(0, rows)])
        copies.drain()

    weights = ((BLOCKS, width, width), BF16)
    inputs = [grad_out, middle, slope, after] + list(vecs) + list(w_inner) + list(w_outer)
    aliases = {}
    if buffer is not None:
        inputs = inputs + [buffer]
        aliases = {len(inputs): 2}
    return kernel_call(
        body,
        control,
        inputs,
        [wide, ((8, width), F32), ((2 * rows, width), BF16)],
        [
            narrow,
            narrow,
            hidden,
            wide,
            ((16, width), BF16),
            weights,
            weights,
            narrow,
            narrow,
            wide,
            ((8, 8, width), F32),
            ((8, width), F32),
        ],
        3 + 3 * BLOCKS + 1 + 4,
        16 * rows * width * width,
        16 * width * width + 30 * rows * width,
        name,
        aliases,
    )


def ffn_weight_grads(control, pieces, vecs, w_inner, w_outer, name):
    rows, width = pieces[0].shape[0] // 2, pieces[0].shape[1]
    count = len(pieces)
    narrow, wide = ((rows, width), BF16), ((rows, width), F32)
    tall = ((count * rows, width), BF16)

    def body(first, block, ins, outs, scr, copies):
        piece_in = ins[:count]
        vec_a, vec_b, wi_a, wi_b, wo_a, wo_b = ins[count : count + 6]
        mid_s, go_s, gi_s, act_s, vec_s, wi_s, wo_s, inner_s, back_s, gw_s, sums_s, extra_s = scr
        part = pl.ds(pl.multiple_of(block * width, width), width)
        vec_load = copies.load_either(first, vec_a, vec_b, vec_s)
        wi_load = copies.load_either(first, wi_a.at[:, part], wi_b.at[:, part], wi_s)
        wo_load = copies.load_either(first, wo_a.at[part, :], wo_b.at[part, :], wo_s)
        loads = []
        for i, piece in enumerate(piece_in):
            spot = pl.ds(i * rows, rows)
            loads.append(
                (
                    copies.load(piece.at[pl.ds(0, rows)], mid_s.at[spot]),
                    copies.load(piece.at[pl.ds(rows, rows)], go_s.at[spot]),
                )
            )
        vec_load.wait()
        wi_load.wait()
        wo_load.wait()
        extra_s[...] = vec_s[...].astype(F32)
        bias = extra_s[pl.ds(8 + block, 1), :]
        sums_s[...] = jnp.zeros_like(sums_s)
        for i in range(count):
            for load in loads[i]:
                load.wait()
            spot = slice(i * rows, (i + 1) * rows)
            inner_s[...] = mm(mid_s[spot, :], wi_s[...])
            back_s[...] = mm_nt(go_s[spot, :], wo_s[...])

            def turn(where, base=i * rows):
                inner = inner_s[where, :] + bias
                phi = 0.5 * (1.0 + lax.erf(inner * (0.5**0.5)))
                density = jnp.exp(-0.5 * inner * inner) * 0.3989422804014327
                target = pl.ds(pl.multiple_of(base + where.start, 16), where.size)
                act_s[target, :] = (inner * phi).astype(BF16)
                rounded = (back_s[where, :] * (phi + inner * density)).astype(BF16)
                gi_s[target, :] = rounded
                sums_s[...] += folded(rounded.astype(F32))

            each_rows(rows, 16, turn)
        gw_s[pl.ds(0, width), :] = mm_tn(mid_s[...], gi_s[...]).astype(BF16)
        copies.store(gw_s.at[pl.ds(0, width)], outs[0].at[pl.ds(0, width)])
        gw_s[pl.ds(width, width), :] = mm_tn(act_s[...], go_s[...]).astype(BF16)
        tail = jnp.concatenate(
            [jnp.sum(sums_s[...], 0, keepdims=True), jnp.zeros((EXTRA - 1, width), F32)], 0
        )
        gw_s[pl.ds(2 * width, EXTRA), :] = tail.astype(BF16)
        copies.store(gw_s.at[pl.ds(width, width + EXTRA)], outs[0].at[pl.ds(width, width + EXTRA)])
        copies.drain()

    square = ((width, width), BF16)
    return kernel_call(
        body,
        control,
        list(pieces) + list(vecs) + list(w_inner) + list(w_outer),
        [((2 * width + EXTRA, width), BF16)],
        [
            tall,
            tall,
            tall,
            tall,
            ((16, width), BF16),
            square,
            square,
            wide,
            wide,
            ((2 * width + EXTRA, width), BF16),
            ((8, width), F32),
            ((16, width), F32),
        ],
        3 + 2 * count + 2,
        8 * count * rows * width * width,
        4 * width * width + 4 * count * rows * width,
        name,
        with_block=True,
    )[0]


def attn_backward(control, grads, saved, xs, flags, vecs, weights, extra, blocks, buffers, name):
    query, key, value, ctx, before = saved[:5]
    probs = saved[5 : 5 + len(blocks)]
    rows, width = query.shape
    narrow, wide = ((rows, width), BF16), ((rows, width), F32)
    probs_shapes = [((PAIRS, 2 * nq, nk), BF16) for _, nq, _, _, nk, _ in blocks]
    n_x, n_b, n_g = len(xs), len(blocks), len(grads)
    kind = grads[0].dtype
    total_rows = 4 * width + EXTRA

    def body(first, ins, outs, scr, copies):
        g_in, x_in = ins[:n_g], ins[n_g : n_g + n_x]
        q_in, k_in, v_in, ctx_in, before_in = ins[n_g + n_x : n_g + n_x + 5]
        rest = ins[n_g + n_x + 5 :]
        probs_in, flags_in, vec_in, w_in = rest[:n_b], rest[n_b], rest[n_b + 1 : n_b + 3], rest[
            n_b + 3 : n_b + 11
        ]
        extra_in = rest[n_b + 11]
        (
            g_s,
            x_s,
            q_s,
            k_s,
            v_s,
            ctx_s,
            before_s,
            flags_s,
            vec_s,
            w_s,
            gb_s,
            gctx_s,
            gq_s,
            gk_s,
            gv_s,
            gx_s,
            gw_s,
            sums_s,
            extra_s,
        ) = scr[:19]
        probs_s = scr[19:]

        def load_rows(pieces, target):
            at, loads = 0, []
            for piece in pieces:
                loads.append(copies.load(piece, target.at[pl.ds(at, piece.shape[0])]))
                at += piece.shape[0]
            return loads

        g_loads = load_rows(g_in, g_s)
        early = [copies.load(before_in, before_s)]
        vec_load = copies.load_either(first, vec_in[0], vec_in[1], vec_s)
        wo_load = copies.load_either(first, w_in[6], w_in[7], w_s.at[3])
        flags_load = copies.load(flags_in, flags_s)
        heads = [copies.load(a, b) for a, b in ((q_in, q_s), (k_in, k_s), (v_in, v_s))]
        probs_loads = [copies.load(a, b) for a, b in zip(probs_in, probs_s)]
        w_loads = [
            copies.load_either(first, w_in[2 * i], w_in[2 * i + 1], w_s.at[i]) for i in range(3)
        ]
        ctx_load = copies.load(ctx_in, ctx_s)
        x_loads = load_rows(x_in, x_s)
        extra_s[...] = jnp.zeros_like(extra_s)
        extra_load = copies.load(extra_in, extra_s.at[pl.ds(8, 8)])
        for load in g_loads + early + [vec_load]:
            load.wait()
        vec = vec_s[...].astype(F32)
        sums_s[...] = jnp.zeros_like(sums_s)

        def start(where):
            grad = g_s[where, :].astype(F32)
            normed, inverse = norm_stats(before_s[where, :])
            sums_s[3] += folded(grad * normed)
            sums_s[4] += folded(grad)
            grad_before = norm_back(grad, normed, inverse, vec[3:4])
            before_s[where, :] = grad_before
            rounded = grad_before.astype(BF16)
            gb_s[where, :] = rounded
            sums_s[2] += folded(rounded.astype(F32))

        each_rows(rows, 32, start)
        wo_load.wait()
        gctx_s[...] = mm_nt(gb_s[...], w_s[3]).astype(BF16)
        flags_load.wait()
        for load in heads:
            load.wait()
        for index, (q0, nq, iq, k0, nk, ik) in enumerate(blocks):
            probs_loads[index].wait()
            low, high, is_low = half_masks(nq)

            def pair_turn(pair, carry):
                lanes = pl.ds(pl.multiple_of(pair * LANES, LANES), LANES)
                keep = head_keep(pair, flags_s[pl.ds(q0, nq), :]).astype(BF16)
                g2 = stacked_halves(gctx_s[pl.ds(q0, nq), lanes] * keep, low, high)
                q2 = stacked_halves(q_s[pl.ds(q0, nq), lanes], low, high)
                k_piece = k_s[pl.ds(k0, nk), lanes]
                kept = probs_s[index][pair]
                wide_probs = kept.astype(F32)
                g_probs = mm_nt(g2, v_s[pl.ds(k0, nk), lanes])
                inner = jnp.sum(wide_probs * g_probs, -1, keepdims=True)
                g_scores = (wide_probs * (g_probs - inner)).astype(BF16)
                scale = HEAD_DIM ** (-0.5)
                g_q = mm(g_scores, k_piece) * scale
                gq_s[pl.ds(q0, nq), lanes] = jnp.where(is_low, g_q[:nq], g_q[nq:]).astype(BF16)
                gk_s[pl.ds(k0, nk), lanes] = (mm_tn(g_scores, q2) * scale).astype(BF16)
                gv_s[pl.ds(k0, nk), lanes] = mm_tn(kept, g2).astype(BF16)
                return carry

            lax.fori_loop(0, PAIRS, pair_turn, 0, unroll=2)
        for load in w_loads:
            load.wait()
        grad_x = before_s[...] + mm_nt(gq_s[...], w_s[0])
        grad_x = grad_x + mm_nt(gk_s[...], w_s[1])
        grad_x = grad_x + mm_nt(gv_s[...], w_s[2])
        gx_s[...] = grad_x.astype(BF16)
        at = 0
        for target in outs[:n_x]:
            copies.store(gx_s.at[pl.ds(at, target.shape[0])], target)
            at += target.shape[0]
        keep_out, send_out = outs[n_x], outs[n_x + 1]
        for load in x_loads + [ctx_load]:
            load.wait()
        for i, (left, right) in enumerate(
            ((x_s, gq_s), (x_s, gk_s), (x_s, gv_s), (ctx_s, gb_s))
        ):
            spot = pl.ds(i * width, width)
            gw_s[spot, :] = mm_tn(left[...], right[...]).astype(BF16)
            copies.store_either(first, gw_s.at[spot], keep_out.at[spot], send_out.at[spot])

        def bias_sums(where):
            sums_s[0] += folded(gq_s[where, :].astype(F32))
            sums_s[1] += folded(gv_s[where, :].astype(F32))

        each_rows(rows, 32, bias_sums)
        extra_load.wait()
        for i in range(5):
            extra_s[i : i + 1, :] = jnp.sum(sums_s[i], 0, keepdims=True)
        spot = pl.ds(4 * width, EXTRA)
        gw_s[spot, :] = extra_s[...].astype(BF16)
        copies.store_either(first, gw_s.at[spot], keep_out.at[spot], send_out.at[spot])
        copies.drain()

    flat = [w for pair in weights for w in pair]
    inputs = (
        list(grads)
        + list(xs)
        + [query, key, value, ctx, before]
        + list(probs)
        + [flags]
        + list(vecs)
        + flat
        + [extra]
    )
    aliases = {}
    if buffers is not None:
        aliases = {len(inputs) + 1: n_x, len(inputs) + 2: n_x + 1}
        inputs = inputs + list(buffers)
    return kernel_call(
        body,
        control,
        inputs,
        [((x.shape[0], width), BF16) for x in xs] + [((total_rows, width), BF16)] * 2,
        [((rows, width), kind)]
        + [narrow] * 5
        + [wide, ((rows, LANES), F32), ((16, width), BF16), ((4, width, width), BF16)]
        + [narrow] * 6
        + [((total_rows, width), BF16), ((8, 8, width), F32), ((EXTRA, width), F32)]
        + probs_shapes,
        n_g + 2 * n_x + 1 + 1 + 4 + 1 + 3 + n_b + 1 + 4 + 1 + 1,
        16 * rows * width * width,
        16 * width * width + 30 * rows * width,
        name,
        aliases,
    )


def swapper(sections):
    n = lax.axis_size("dp")

    def swap(value, bit):
        pairs = [(s * n + i, s * n + (i ^ bit)) for s in sections for i in range(n)]
        return lax.ppermute(value, ("section", "dp"), pairs)

    return swap


def spread_sum(part, bits, swap):
    at = lax.axis_index("dp")
    for bit in bits:
        side = (at // bit) % 2
        half = part.shape[0] // 2
        keep = lax.dynamic_slice_in_dim(part, side * half, half, 0)
        send = lax.dynamic_slice_in_dim(part, (1 - side) * half, half, 0)
        part = keep + swap(send, bit)
    return part


def gather_back(part, bits, swap):
    at = lax.axis_index("dp")
    for bit in reversed(bits):
        side = (at // bit) % 2
        far = swap(part, bit)
        part = jnp.where(side == 0, jnp.concatenate([part, far]), jnp.concatenate([far, part]))
    return part


def per_device(
    tokens,
    cotangent,
    task_flags,
    w_query,
    w_key,
    w_value,
    w_attn_out,
    b_query,
    b_value,
    b_attn_out,
    norm1_gain,
    norm1_bias,
    w_inner,
    b_inner,
    w_outer,
    b_outer,
    norm2_gain,
    norm2_bias,
):
    section = lax.axis_index("section")
    stage, core = section // 2, section % 2
    items, seq_len, width = tokens.shape
    words = seq_len - OBJ
    n_visual, n_word = items * OBJ, items * words
    is_first = stage == 0

    def swap_stage(value):
        return lax.ppermute(value, "section", [(0, 2), (1, 3), (2, 0), (3, 1)])

    def swap_core(value):
        return lax.ppermute(value, "section", [(0, 1), (1, 0), (2, 3), (3, 2)])

    flags_far = swap_stage(task_flags)
    tokens_far = swap_stage(tokens)
    attn_w = [w[0] for w in (w_query, w_key, w_value, w_attn_out)]
    vec = jnp.concatenate(
        [
            b_query,
            b_value,
            b_attn_out,
            norm1_gain,
            norm1_bias,
            b_outer,
            norm2_gain,
            norm2_bias,
            b_inner.reshape(BLOCKS, width),
            jnp.zeros((4, width), BF16),
        ],
        0,
    )
    vecs = (vec, swap_core(vec))
    attn_w = [(w, swap_core(w)) for w in attn_w]
    inner_w = (w_inner[0], swap_core(w_inner[0]))
    outer_w = (w_outer[0], swap_core(w_outer[0]))
    cot_far = swap_stage(cotangent)

    flags = task_flags.astype(F32)
    far = flags_far.astype(F32)
    flags = jnp.where(
        is_first, jnp.concatenate([flags, far]), jnp.concatenate([far, flags])
    )
    flags_v = jnp.broadcast_to(jnp.repeat(flags, OBJ)[:, None], (2 * n_visual, LANES))
    flags_w = jnp.broadcast_to(jnp.repeat(flags, words)[:, None], (2 * n_word, LANES))
    flags_all = jnp.concatenate([flags_v, flags_w], 0)

    def split(first, second):
        visual = jnp.concatenate([first[:, :OBJ], second[:, :OBJ]], 0)
        word = jnp.concatenate([first[:, OBJ:], second[:, OBJ:]], 0)
        return visual.reshape(2 * n_visual, width), word.reshape(2 * n_word, width)

    place = lax.axis_index("dp")
    side = place % 2
    block = 2 * side + core

    def control(at, parity):
        return jnp.stack([stage == at, core == parity, block]).astype(jnp.int32)

    even_0, odd_0, even_1, odd_1 = control(0, 0), control(0, 1), control(1, 0), control(1, 1)
    even_any = jnp.stack([core >= 0, core == 0, block]).astype(jnp.int32)
    blocks_v = [(g * n_visual, n_visual, OBJ, g * n_visual, n_visual, OBJ) for g in (0, 1)]
    blocks_w = [(g * n_word, n_word, words, g * n_word, n_word, words) for g in (0, 1)]
    blocks_x = []
    for g in (0, 1):
        v_at, w_at = g * n_visual, 2 * n_visual + g * n_word
        blocks_x.append((v_at, n_visual, OBJ, w_at, n_word, words))
        blocks_x.append((w_at, n_word, words, v_at, n_visual, OBJ))

    visual_0, word_0 = split(tokens, tokens_far)
    grad_v4, grad_w4 = split(cot_far, cotangent)
    ffn_w = (vecs, inner_w, outer_w)

    *kept_0, middle_0, mid_0 = attn_forward(
        even_0, [visual_0], flags_v, vecs, attn_w, blocks_v, False, "s0_attn_f"
    )
    *ffn_0, visual_1 = ffn_forward(even_0, middle_0, *ffn_w, "s0_ffn_f")
    *kept_1, visual_2, word_2 = attn_forward(
        odd_0, [visual_1, word_0], flags_all, vecs, attn_w, blocks_x, True, "s1_attn_f"
    )
    word_2, visual_2 = swap_stage(word_2), swap_stage(visual_2)
    *kept_3, middle_3, mid_3 = attn_forward(
        odd_1, [word_2], flags_w, vecs, attn_w, blocks_w, False, "s3_attn_f"
    )
    *ffn_3, word_4 = ffn_forward(odd_1, middle_3, *ffn_w, "s3_ffn_f")
    gmid_3, extra_3, pair_3 = ffn_backward(odd_1, grad_w4, mid_3, ffn_3, *ffn_w, None, "s3_ffn_b")
    grad_w2, *sums = attn_backward(
        odd_1,
        [gmid_3],
        kept_3,
        [word_2],
        flags_w,
        vecs,
        attn_w,
        extra_3,
        blocks_w,
        None,
        "s3_attn_b",
    )
    *kept_2, middle_2, mid_2 = attn_forward(
        even_1, [visual_2], flags_v, vecs, attn_w, blocks_v, False, "s2_attn_f"
    )
    *ffn_2, visual_4 = ffn_forward(even_1, middle_2, *ffn_w, "s2_ffn_f")
    gmid_2, extra_2, pair_2 = ffn_backward(even_1, grad_v4, mid_2, ffn_2, *ffn_w, None, "s2_ffn_b")
    grad_v2, *sums = attn_backward(
        even_1,
        [gmid_2],
        kept_2,
        [visual_2],
        flags_v,
        vecs,
        attn_w,
        extra_2,
        blocks_v,
        sums,
        "s2_attn_b",
    )

    def join(visual, word):
        return jnp.concatenate(
            [visual.reshape(items, OBJ, width), word.reshape(items, words, width)], 1
        )

    grad_w2, grad_v2 = swap_stage(grad_w2), swap_stage(grad_v2)
    mixed_far = swap_stage(join(visual_4[:n_visual], word_4[:n_word]))
    mixed = jnp.where(is_first, mixed_far, join(visual_4[n_visual:], word_4[n_word:]))
    grad_v1, grad_w0, *sums = attn_backward(
        odd_0,
        [grad_v2, grad_w2],
        kept_1,
        [visual_1, word_0],
        flags_all,
        vecs,
        attn_w,
        jnp.zeros((8, width), F32),
        blocks_x,
        sums,
        "s1_attn_b",
    )
    gmid_0, extra_0, pair_0 = ffn_backward(
        even_0, grad_v1, mid_0, ffn_0, *ffn_w, pair_2, "s0_ffn_b"
    )
    grad_v0, keep, send = attn_backward(
        even_0,
        [gmid_0],
        kept_0,
        [visual_0],
        flags_v,
        vecs,
        attn_w,
        extra_0,
        blocks_v,
        sums,
        "s0_attn_b",
    )

    swap_all, swap_late = swapper(range(4)), swapper((2, 3))
    line = []
    while 2 ** (len(line) + 1) < lax.axis_size("dp"):
        line.append(2 ** (len(line) + 1))

    def ffn_sums(pair, control, swap, name):
        across = swap(pair, 1)
        pieces = [pair, across, swap_core(pair), swap_core(across)]
        sums = ffn_weight_grads(control, pieces, *ffn_w, name)
        parts = []
        for piece in (sums[:width], sums[width:]):
            piece = gather_back(spread_sum(piece, line, swap), [1] + line, swap)
            parts.append((piece, swap_core(piece)))
        return parts

    ffn_odd = ffn_sums(pair_3, odd_1, swap_late, "s3_ffn_w")
    ffn_even = ffn_sums(pair_0, even_any, swap_all, "even_ffn_w")
    attn = []
    for piece in (slice(0, 2 * width), slice(2 * width, None)):
        part = keep[piece] + swap_core(send[piece])
        attn.append(
            gather_back(spread_sum(part, [1] + line, swap_all), [1] + line, swap_all).astype(F32)
        )

    grad_v0, grad_w0, _ = lax.optimization_barrier((grad_v0, grad_w0, attn[1]))
    grad_far = swap_stage(join(grad_v0[n_visual:], grad_w0[n_word:]))
    tokens_grad = jnp.where(is_first, join(grad_v0[:n_visual], grad_w0[:n_word]), grad_far)

    is_even = core == 0
    unused = section == 1

    def pick(even, odd):
        return jnp.where(is_even, even, jnp.where(unused, jnp.zeros_like(odd), odd)).astype(F32)

    by_core = []
    for c in (0, 1):
        by_core.append([pick(ffn_even[h][c], ffn_odd[h][1 - c]) for h in (0, 1)])
    size = width + EXTRA
    inner, outer, inner_bias = [], [], []
    for x in (0, 1):
        for c in (0, 1):
            inner.append(by_core[c][0][x * width : (x + 1) * width])
            outer.append(by_core[c][1][x * size : x * size + width])
            inner_bias.append(by_core[c][1][x * size + width : x * size + width + 1])
    square = [attn[i // 2][(i % 2) * width : (i % 2 + 1) * width] for i in range(4)]
    small = attn[1][2 * width :]
    small = small * jnp.where(unused & (jnp.arange(EXTRA)[:, None] >= 8), 0.0, 1.0)
    return (
        mixed,
        tokens_grad,
        square[0][None],
        square[1][None],
        square[2][None],
        square[3][None],
        small[0:1],
        small[1:2],
        small[2:3],
        small[3:4],
        small[4:5],
        jnp.concatenate(inner, 1)[None],
        jnp.concatenate(inner_bias, 1),
        jnp.concatenate(outer, 0)[None],
        small[10:11],
        small[8:9],
        small[9:10],
    )


def solution(mesh):
    tokens = P(("section", "dp"), None, None)
    matrix = P("section", None, None)
    vector = P("section", None)
    placed = (
        (tokens, tokens, P(("section", "dp")))
        + (matrix,) * 4
        + (vector,) * 5
        + (matrix, vector, matrix)
        + (vector,) * 3
    )
    return jax.shard_map(
        per_device,
        mesh=mesh,
        in_specs=placed,
        out_specs=(tokens, tokens)
        + (matrix,) * 4
        + (vector,) * 5
        + (matrix, vector, matrix)
        + (vector,) * 3,
        check_vma=False,
    )
```

time: 2430 us -> 653 us (0.27)
  loops' own time: 517 us -> 0 us
  local copies, waits for them, and re-layouts: 481 us -> 56.7 us
  matrix products: 348 us -> 0 us
  waiting for transfers between devices: 521 us -> 282 us
  other arithmetic: 296 us -> 65 us
  Pallas kernels: 0 us -> 132 us
  starting transfers between devices: 190 us -> 105 us
  blocking collectives: 40.9 us -> 0 us
    another operation x28 -> x0, loops' own time: 517 us -> none  [the longest x14 241 us: run_forward(): return lax.switch(branch, options)]
    psum x1 -> x0, waiting for transfers between devices: 343 us -> none  [per_device(): lax.psum(sum_w_query.astype(jnp.bfloat16), 'dp').astype(jnp.float32)]
    dot_general x128 -> x0, matrix products: 338 us -> none  [the longest x8 67.7 us: window_forward(): jnp.dot(activated, w_outer, preferred_element_type=jnp.float32) + b_outer]
    pallas_call x0 -> x16, Pallas kernels: none -> 132 us  [kernel_call(): pl.pallas_call(kernel, out_shape=[jax.ShapeDtypeStruct(shape, kind) for s...]
    ppermute x12 -> x60, waiting for transfers between devices: 165 us -> 282 us  [the longest x34 253 us: swap(): return lax.ppermute(value, ('section', 'dp'), pairs)]
    all_to_all x2 -> x0, starting transfers between devices: 107 us -> none  [the longest x1 101 us: per_device(): lax.all_to_all(finished, 'section', split_axis=0, concat_axis=0, tiled=True)]
    cond x196 -> x0, local copies, waits for them, and re-layouts: 102 us -> none  [the longest x16 49.4 us: per_device(): grad_back, attn_terms = lax.switch(branch, attn_options)]
    reshape x104 -> x13, local copies, waits for them, and re-layouts: 109 us -> 7.33 us  [the longest x2 2.74 us: split(): visual.reshape(2 * n_visual, width)]
  transfers between devices with their start and end apart: 17 -> 60, of which waited for: 10 -> 30; matrix products, arithmetic and copies ran while one was open for 16% -> 16% of each run, Pallas kernels for 0% -> 19%
where the time goes in v1:
time: 653 us; the launch traced here: 644 us
  waiting for transfers between devices  282 us (43%)
  Pallas kernels  132 us (20%)
  starting transfers between devices  105 us (16%)
  other arithmetic  65 us (10%)
  local copies, waits for them, and re-layouts  56.7 us (9%)
    ppermute x34, waiting for transfers between devices, swap(): return lax.ppermute(value, ('section', 'dp'), pairs)  253 us
    pallas_call x16, Pallas kernels, kernel_call(): pl.pallas_call(kernel, out_shape=[jax.ShapeDtypeStruct(shape, kind) for s...  132 us
    ppermute x34, starting transfers between devices, swap(): return lax.ppermute(value, ('section', 'dp'), pairs)  53.9 us
    ppermute x9, starting transfers between devices, swap_stage(): return lax.ppermute(value, 'section', [(0, 2), (1, 3), (2, 0), (3, 1)])  48.5 us
    ppermute x9, waiting for transfers between devices, swap_stage(): return lax.ppermute(value, 'section', [(0, 2), (1, 3), (2, 0), (3, 1)])  23.6 us
    select_n x14, other arithmetic, gather_back(): jnp.where(side == 0, jnp.concatenate([part, far]), jnp.concatenate([far,...  16.6 us
  transfers between devices with their start and end apart: 60, of which 30 were waited for; matrix products, arithmetic and copies ran while one was open for 16% of the time, Pallas kernels for 19%

profile of v1, /device:TPU:30, one launch (start us, length us, event | category | flops | bytes accessed | tf_op | source)
XLA Modules:
  0.0 643.6 jit_solution(8821092388462659618)
XLA Ops:
  5.0 7.0 %collective-permute-done.1 = s32[4]{0:T(128)S(1)} collective-permute-done((s32[4]{0:T(128)}, s32[4]{0:T(128)S(1)}, u32[]{:S(2)}, u32[]{:S(2)}) %collective-permute-start.1) | collective-permute-done | bytes 48 | tf_op jit(solution)/shard_map/ppermute | solution.py:741
  12.0 5.1 collective-permute-done.2.refs_3_.refs_2_.refs_4_.refs_5_.refs_11_.refs_15_
  39.2 43.9 %collective-permute-start.10 = (bf16[160,768]{1,0:T(8,128)(2,1)}, bf16[160,768]{1,0:T(8,128)(2,1)S(1)}, u32[]{:S(2)}, u32[]{:S(2)}) collective-permute-start(bf16[160,768]{1,0:T(8,128)(2,1)} %get-tuple-element.93), channel_id=1, source_target_pairs={{0,16},{8,24},{16,0},{24,8},{1,17},{9,25},{17,1},{25,9},{2,18},{10... | collective-permute-start | bytes 737288 | tf_op jit(solution)/shard_map/ppermute | solution.py:741
  87.2 2.6 collective-permute-done.10.refs_0_.refs_1_
  90.5 10.6 %s3_attn_f.1 = (bf16[160,768]{1,0:T(8,128)(2,1)}, bf16[160,768]{1,0:T(8,128)(2,1)}, bf16[160,768]{1,0:T(8,128)(2,1)}, bf16[160,768]{1,0:T(8,128)(2,1)}, f32[160,...) custom-call(s32[3]{0:T(128)} %add_add_fusion.3.control_ref, ...), custom_call_target="tpu_custom_call" | custom-call | flops 754974720 | bytes 7176192 | tf_op jit(solution)/shard_map/s3_attn_f/pallas_call | solution.py:116
  101.1 8.3 %s3_ffn_f.1 = (bf16[4,160,768]{2,1,0:T(8,128)(2,1)}, f32[160,768]{1,0:T(8,128)}, bf16[160,768]{1,0:T(8,128)(2,1)}) custom-call(s32[3]{0:T(128)} %add_add_fusion.3.control_ref, f32[160,768]{1,0:T(8,128)} %get-tuple-element.94.refs_0_, bf16[16,768]{1,0:T(8,128)(2,1)} %copy-done.8, bf16[16,768]{1,0:T(8,128)(2,1)} %copy-done.9, bf16[768,3072]{1,0:T(8,128)(2,1)} %bitcast.26, ...), custom_call_target="tpu_custom_call" | custom-call | flops 1509949440 | bytes 12632064 | tf_op jit(solution)/shard_map/s3_ffn_f/pallas_call | solution.py:116
  109.4 7.8 %s3_ffn_b.1 = (f32[160,768]{1,0:T(8,128)}, f32[8,768]{1,0:T(8,128)}, bf16[320,768]{1,0:T(8,128)(2,1)}) custom-call(s32[3]{0:T(128)} %add_add_fusion.3.control_ref, bf16[160,768]{1,0:T(8,128)(2,1)} %reshape.92.refs_0_, bf16[160,768]{1,0:T(8,128)(2,1)} %get-tuple-element.108.refs_1_, bf16[4,160,768]{2,1,0:T(8,128)(2,1)} %get-tuple-element.109.refs_2_, ...), custom_call_target="tpu_custom_call" | custom-call | flops 1509949440 | bytes 13123584 | tf_op jit(solution)/shard_map/s3_ffn_b/pallas_call | solution.py:116
  117.2 2.4 collective-permute-start.38
  119.6 13.0 %s3_attn_b.1 = (bf16[160,768]{1,0:T(8,128)(2,1)}, bf16[3104,768]{1,0:T(8,128)(2,1)}, bf16[3104,768]{1,0:T(8,128)(2,1)}) custom-call(s32[3]{0:T(128)} %add_add_fusion.3.control_ref, f32[160,768]{1,0:T(8,128)} %get-tuple-element.111.refs_0_, bf16[160,768]{1,0:T(8,128)(2,1)} %copy-done.18, bf16[160,768]{1,0:T(8,128)(2,1)} %get-tuple-element.112.refs_2_, ...), custom_call_target="tpu_custom_call" | custom-call | flops 1509949440 | bytes 13123584 | tf_op jit(solution)/shard_map/s3_attn_b/pallas_call | solution.py:116
  133.4 24.2 %s2_attn_f.1 = (bf16[288,768]{1,0:T(8,128)(2,1)}, bf16[288,768]{1,0:T(8,128)(2,1)}, bf16[288,768]{1,0:T(8,128)(2,1)}, bf16[288,768]{1,0:T(8,128)(2,1)}, f32[288,...) custom-call(s32[3]{0:T(128)} %add_add_fusion.control_ref, ...), custom_call_target="tpu_custom_call" | custom-call | flops 1358954496 | bytes 9142272 | tf_op jit(solution)/shard_map/s2_attn_f/pallas_call | solution.py:116
  157.7 12.1 %s2_ffn_f.1 = (bf16[4,288,768]{2,1,0:T(8,128)(2,1)}, f32[288,768]{1,0:T(8,128)}, bf16[288,768]{1,0:T(8,128)(2,1)}) custom-call(s32[3]{0:T(128)} %add_add_fusion.control_ref, f32[288,768]{1,0:T(8,128)} %get-tuple-element.91.refs_0_, bf16[16,768]{1,0:T(8,128)(2,1)} %copy-done.8, bf16[16,768]{1,0:T(8,128)(2,1)} %copy-done.9, bf16[768,3072]{1,0:T(8,128)(2,1)} %bitcast.28, ...), custom_call_target="tpu_custom_call" | custom-call | flops 2717908992 | bytes 15187968 | tf_op jit(solution)/shard_map/s2_ffn_f/pallas_call | solution.py:116
  169.7 9.5 %s2_ffn_b.1 = (f32[288,768]{1,0:T(8,128)}, f32[8,768]{1,0:T(8,128)}, bf16[576,768]{1,0:T(8,128)(2,1)}) custom-call(s32[3]{0:T(128)} %add_add_fusion.control_ref, bf16[288,768]{1,0:T(8,128)(2,1)} %reshape.91.refs_0_, bf16[288,768]{1,0:T(8,128)(2,1)} %get-tuple-element.96.refs_1_, bf16[4,288,768]{2,1,0:T(8,128)(2,1)} %get-tuple-element.97.refs_2_, ...), custom_call_target="tpu_custom_call" | custom-call | flops 2717908992 | bytes 16072704 | tf_op jit(solution)/shard_map/s2_ffn_b/pallas_call | solution.py:116
  179.3 16.9 %s2_attn_b.1 = (bf16[288,768]{1,0:T(8,128)(2,1)}, bf16[3104,768]{1,0:T(8,128)(2,1)}, bf16[3104,768]{1,0:T(8,128)(2,1)}) custom-call(s32[3]{0:T(128)} %add_add_fusion.control_ref, f32[288,768]{1,0:T(8,128)} %get-tuple-element.99.refs_0_, bf16[288,768]{1,0:T(8,128)(2,1)} %copy-done.15, ...), custom_call_target="tpu_custom_call", output_to_operand_aliasing={{1}: (22, {}), {2}: (23, {})} | custom-call | flops 2717908992 | bytes 16072704 | tf_op jit(solution)/shard_map/s2_attn_b/pallas_call | solution.py:116
  199.4 13.0 %collective-permute-done.14.refs_1_ = bf16[160,768]{1,0:T(8,128)(2,1)S(1)} collective-permute-done((bf16[160,768]{1,0:T(8,128)(2,1)S(1)}, bf16[160,768]{1,0:T(8,128)(2,1)S(1)}, u32[]{:S(2)}, u32[]{:S(2)}) %collective-permute-start.14) | collective-permute-done | bytes 245792 | tf_op jit(solution)/shard_map/ppermute | solution.py:741
  216.1 10.5 %s3_ffn_w.1 = bf16[1568,768]{1,0:T(8,128)(2,1)} custom-call(s32[3]{0:T(128)} %add_add_fusion.3.control_ref, bf16[320,768]{1,0:T(8,128)(2,1)} %get-tuple-element.158.refs_0_, bf16[320,768]{1,0:T(8,128)(2,1)} %copy-done.20, bf16[320,768]{1,0:T(8,128)(2,1)} %copy-done.21, bf16[320,768]{1,0:T(8,128)(2,1)} %copy-done.22, bf16[16,768]{1,0:T(8,128)(2,1)} %copy-done.8, ...), custom_call_target="tpu_custom_call" | custom-call | flops 3019898880 | bytes 4325376 | tf_op jit(solution)/shard_map/s3_ffn_w/pallas_call | solution.py:116
  228.9 2.3 collective-permute-start.41
  233.9 3.5 collective-permute-start.53
  238.3 3.4 slice.166
  243.2 4.1 collective-permute-done.41
  249.4 2.4 collective-permute-start.42
  251.8 10.6 %collective-permute-done.53 = bf16[400,768]{1,0:T(8,128)(2,1)} collective-permute-done((bf16[400,768]{1,0:T(8,128)(2,1)}, bf16[400,768]{1,0:T(8,128)(2,1)}, u32[]{:S(2)}, u32[]{:S(2)}) %collective-permute-start.53) | collective-permute-done | bytes 614432 | tf_op jit(solution)/shard_map/ppermute | solution.py:688
  269.6 3.2 collective-permute-start.43
  272.9 15.8 %collective-permute-done.54 = bf16[200,768]{1,0:T(8,128)(2,1)S(1)} collective-permute-done((bf16[200,768]{1,0:T(8,128)(2,1)S(1)}, bf16[200,768]{1,0:T(8,128)(2,1)S(1)}, u32[]{:S(2)}, u32[]{:S(2)}) %collective-permute-start.54) | collective-permute-done | bytes 307232 | tf_op jit(solution)/shard_map/ppermute | solution.py:688
  292.2 3.4 slice.160
  295.6 2.7 collective-permute-done.43
  298.5 4.8 collective-permute-done.55
  306.5 3.9 collective-permute-start.56
  310.4 13.4 %even_ffn_w.1 = bf16[1568,768]{1,0:T(8,128)(2,1)} custom-call(s32[3]{0:T(128)} %add_add_fusion.4.control_ref, bf16[576,768]{1,0:T(8,128)(2,1)} %get-tuple-element.157.refs_0_, bf16[576,768]{1,0:T(8,128)(2,1)} %collective-permute-done.30.refs_1_, bf16[576,768]{1,0:T(8,128)(2,1)} %collective-permute-done.31.refs_2_, ...), custom_call_target="tpu_custom_call" | custom-call | flops 5435817984 | bytes 5898240 | tf_op jit(solution)/shard_map/even_ffn_w/pallas_call | solution.py:116
  328.8 2.7 slice_add_fusion.1
  331.6 15.7 %collective-permute-done.33 = bf16[384,768]{1,0:T(8,128)(2,1)S(1)} collective-permute-done((bf16[384,768]{1,0:T(8,128)(2,1)S(1)}, bf16[384,768]{1,0:T(8,128)(2,1)S(1)}, u32[]{:S(2)}, u32[]{:S(2)}) %collective-permute-start.33) | collective-permute-done | bytes 589856 | tf_op jit(solution)/shard_map/ppermute | solution.py:688
  348.9 8.9 %collective-permute-done.48 = bf16[400,768]{1,0:T(8,128)(2,1)S(1)} collective-permute-done((bf16[400,768]{1,0:T(8,128)(2,1)S(1)}, bf16[400,768]{1,0:T(8,128)(2,1)S(1)}, u32[]{:S(2)}, u32[]{:S(2)}) %collective-permute-start.48) | collective-permute-done | bytes 614432 | tf_op jit(solution)/shard_map/ppermute | solution.py:688
  358.0 3.0 collective-permute-start.49
  363.1 15.0 %collective-permute-done.34 = bf16[192,768]{1,0:T(8,128)(2,1)S(1)} collective-permute-done((bf16[192,768]{1,0:T(8,128)(2,1)S(1)}, bf16[192,768]{1,0:T(8,128)(2,1)S(1)}, u32[]{:S(2)}, u32[]{:S(2)}) %collective-permute-start.34) | collective-permute-done | bytes 294944 | tf_op jit(solution)/shard_map/ppermute | solution.py:688
  379.7 4.8 collective-permute-done.49
  384.7 3.0 collective-permute-start.50
  388.1 3.5 collective-permute-start.45
  392.1 12.0 %collective-permute-done.35 = bf16[192,768]{1,0:T(8,128)(2,1)S(1)} collective-permute-done((bf16[192,768]{1,0:T(8,128)(2,1)S(1)}, bf16[192,768]{1,0:T(8,128)(2,1)S(1)}, u32[]{:S(2)}, u32[]{:S(2)}) %collective-permute-start.35) | collective-permute-done | bytes 294944 | tf_op jit(solution)/shard_map/ppermute | solution.py:688
  404.3 6.3 collective-permute-done.50
  410.6 3.7 collective-permute-start.57
  417.5 15.3 %collective-permute-done.45 = bf16[768,768]{1,0:T(8,128)(2,1)S(1)} collective-permute-done((bf16[768,768]{1,0:T(8,128)(2,1)S(1)}, bf16[768,768]{1,0:T(8,128)(2,1)S(1)}, u32[]{:S(2)}, u32[]{:S(2)}) %collective-permute-start.45) | collective-permute-done | bytes 1179680 | tf_op jit(solution)/shard_map/ppermute | solution.py:688
  434.5 8.9 %collective-permute-done.25 = bf16[384,768]{1,0:T(8,128)(2,1)S(1)} collective-permute-done((bf16[384,768]{1,0:T(8,128)(2,1)S(1)}, bf16[384,768]{1,0:T(8,128)(2,1)S(1)}, u32[]{:S(2)}, u32[]{:S(2)}) %collective-permute-start.25) | collective-permute-done | bytes 589856 | tf_op jit(solution)/shard_map/ppermute | solution.py:688
  443.6 11.4 %collective-permute-done.17 = bf16[392,768]{1,0:T(8,128)(2,1)S(1)} collective-permute-done((bf16[392,768]{1,0:T(8,128)(2,1)S(1)}, bf16[392,768]{1,0:T(8,128)(2,1)S(1)}, u32[]{:S(2)}, u32[]{:S(2)}) %collective-permute-start.17) | collective-permute-done | bytes 602144 | tf_op jit(solution)/shard_map/ppermute | solution.py:688
  455.3 2.7 collective-permute-done.57
  459.0 17.8 %collective-permute-done.26 = bf16[192,768]{1,0:T(8,128)(2,1)S(1)} collective-permute-done((bf16[192,768]{1,0:T(8,128)(2,1)S(1)}, bf16[192,768]{1,0:T(8,128)(2,1)S(1)}, u32[]{:S(2)}, u32[]{:S(2)}) %collective-permute-start.26) | collective-permute-done | bytes 294944 | tf_op jit(solution)/shard_map/ppermute | solution.py:688
  476.9 6.4 %collective-permute-done.18 = bf16[196,768]{1,0:T(8,128)(2,1)S(1)} collective-permute-done((bf16[196,768]{1,0:T(8,128)(2,1)S(1)}, bf16[196,768]{1,0:T(8,128)(2,1)S(1)}, u32[]{:S(2)}, u32[]{:S(2)}) %collective-permute-start.18) | collective-permute-done | bytes 301088 | tf_op jit(solution)/shard_map/ppermute | solution.py:688
  483.6 3.0 collective-permute-start.19
  488.0 19.0 %collective-permute-done.27 = bf16[192,768]{1,0:T(8,128)(2,1)S(1)} collective-permute-done((bf16[192,768]{1,0:T(8,128)(2,1)S(1)}, bf16[192,768]{1,0:T(8,128)(2,1)S(1)}, u32[]{:S(2)}, u32[]{:S(2)}) %collective-permute-start.27) | collective-permute-done | bytes 294944 | tf_op jit(solution)/shard_map/ppermute | solution.py:688
  508.2 2.2 maximum_select_fusion.15
  510.5 2.2 collective-permute-done.19
  521.3 8.0 %collective-permute-done.28 = bf16[384,768]{1,0:T(8,128)(2,1)} collective-permute-done((bf16[384,768]{1,0:T(8,128)(2,1)}, bf16[384,768]{1,0:T(8,128)(2,1)}, u32[]{:S(2)}, u32[]{:S(2)}) %collective-permute-start.28) | collective-permute-done | bytes 589856 | tf_op jit(solution)/shard_map/ppermute | solution.py:688
  531.7 8.5 %collective-permute-done.20 = bf16[392,768]{1,0:T(8,128)(2,1)} collective-permute-done((bf16[392,768]{1,0:T(8,128)(2,1)}, bf16[392,768]{1,0:T(8,128)(2,1)}, u32[]{:S(2)}, u32[]{:S(2)}) %collective-permute-start.20) | collective-permute-done | bytes 602144 | tf_op jit(solution)/shard_map/ppermute | solution.py:688
  544.3 4.7 select_convert_fusion.3
  549.0 2.4 fusion.6
  551.4 11.8 %collective-permute-done.52 = bf16[800,768]{1,0:T(8,128)(2,1)S(1)} collective-permute-done((bf16[800,768]{1,0:T(8,128)(2,1)S(1)}, bf16[800,768]{1,0:T(8,128)(2,1)S(1)}, u32[]{:S(2)}, u32[]{:S(2)}) %collective-permute-start.52) | collective-permute-done | bytes 1228832 | tf_op jit(solution)/shard_map/ppermute | solution.py:688
  563.2 3.5 select_convert_fusion.1
  566.7 2.4 fusion.2
  569.1 19.3 %collective-permute-done.29 = bf16[768,768]{1,0:T(8,128)(2,1)S(1)} collective-permute-done((bf16[768,768]{1,0:T(8,128)(2,1)S(1)}, bf16[768,768]{1,0:T(8,128)(2,1)S(1)}, u32[]{:S(2)}, u32[]{:S(2)}) %collective-permute-start.29) | collective-permute-done | bytes 1179680 | tf_op jit(solution)/shard_map/ppermute | solution.py:688
  589.1 2.5 slice_bitcast_fusion.2
  591.6 19.8 %collective-permute-done.21 = bf16[784,768]{1,0:T(8,128)(2,1)S(1)} collective-permute-done((bf16[784,768]{1,0:T(8,128)(2,1)S(1)}, bf16[784,768]{1,0:T(8,128)(2,1)S(1)}, u32[]{:S(2)}, u32[]{:S(2)}) %collective-permute-start.21) | collective-permute-done | bytes 1204256 | tf_op jit(solution)/shard_map/ppermute | solution.py:688
  611.3 2.8 fusion
  617.8 4.9 slice_bitcast_fusion
  625.5 2.7 select_convert_fusion.2
  630.6 4.2 maximum_bitcast_fusion
  639.2 3.9 maximum_bitcast_fusion.1
  (268 shorter events, 112.2 us)
Async XLA Ops:
  0.7 36.4 %collective-permute-start.7 = (bf16[768,3072]{1,0:T(8,128)(2,1)}, bf16[768,3072]{1,0:T(8,128)(2,1)}, u32[]{:S(2)}, u32[]{:S(2)}) collective-permute-start(bf16[768,3072]{1,0:T(8,128)(2,1)} %bitcast.24), channel_id=1, source_target_pairs={{0,8},{8,0},{16,24},{24,16},{1,9},{9,1},{17,25},{25,17},{2,10},{10... | collective-permute-start | bytes 14155784 | tf_op jit(solution)/shard_map/ppermute | solution.py:744
  0.7 36.3 %collective-permute-start.8 = (bf16[3072,768]{1,0:T(8,128)(2,1)}, bf16[3072,768]{1,0:T(8,128)(2,1)}, u32[]{:S(2)}, u32[]{:S(2)}) collective-permute-start(bf16[3072,768]{1,0:T(8,128)(2,1)} %bitcast.33), channel_id=1, source_target_pairs={{0,8},{8,0},{16,24},{24,16},{1,9},{9,1},{17,25},{25,17},{2,10},{10... | collective-permute-start | bytes 14155784 | tf_op jit(solution)/shard_map/ppermute | solution.py:744
  1.2 17.1 %collective-permute-start.3 = (bf16[768,768]{1,0:T(8,128)(2,1)}, bf16[768,768]{1,0:T(8,128)(2,1)S(1)}, u32[]{:S(2)}, u32[]{:S(2)}) collective-permute-start(bf16[768,768]{1,0:T(8,128)(2,1)} %bitcast.44), channel_id=1, source_target_pairs={{0,8},{8,0},{16,24},{24,16},{1,9},{9,1},{17,25},{25,17},{2,10},{10... | collective-permute-start | bytes 3538952 | tf_op jit(solution)/shard_map/ppermute | solution.py:744
  1.3 15.9 %collective-permute-start = (bf16[4,56,768]{2,1,0:T(8,128)(2,1)}, bf16[4,56,768]{2,1,0:T(8,128)(2,1)S(1)}, u32[]{:S(2)}, u32[]{:S(2)}) collective-permute-start(bf16[4,56,768]{2,1,0:T(8,128)(2,1)} %param.18), channel_id=1, source_target_pairs={{0,16},{8,24},{16,0},{24,8},{1,17},{9,25},{17,1},{25,9},{2,18},{10... | collective-permute-start | bytes 1032200 | tf_op jit(solution)/shard_map/ppermute | solution.py:741
  1.8 10.2 %collective-permute-start.1 = (s32[4]{0:T(128)}, s32[4]{0:T(128)S(1)}, u32[]{:S(2)}, u32[]{:S(2)}) collective-permute-start(s32[4]{0:T(128)} %param.20), channel_id=1, source_target_pairs={{0,16},{8,24},{16,0},{24,8},{1,17},{9,25},{17,1},{25,9},{2,18},{10... | collective-permute-start | bytes 56 | tf_op jit(solution)/shard_map/ppermute | solution.py:741
  12.0 5.1 collective-permute-start.2
  17.1 17.6 %collective-permute-start.4 = (bf16[768,768]{1,0:T(8,128)(2,1)}, bf16[768,768]{1,0:T(8,128)(2,1)S(1)}, u32[]{:S(2)}, u32[]{:S(2)}) collective-permute-start(bf16[768,768]{1,0:T(8,128)(2,1)} %bitcast.53), channel_id=1, source_target_pairs={{0,8},{8,0},{16,24},{24,16},{1,9},{9,1},{17,25},{25,17},{2,10},{10... | collective-permute-start | bytes 3538952 | tf_op jit(solution)/shard_map/ppermute | solution.py:744
  18.0 17.2 %collective-permute-start.5 = (bf16[768,768]{1,0:T(8,128)(2,1)}, bf16[768,768]{1,0:T(8,128)(2,1)S(1)}, u32[]{:S(2)}, u32[]{:S(2)}) collective-permute-start(bf16[768,768]{1,0:T(8,128)(2,1)} %bitcast.62), channel_id=1, source_target_pairs={{0,8},{8,0},{16,24},{24,16},{1,9},{9,1},{17,25},{25,17},{2,10},{10... | collective-permute-start | bytes 3538952 | tf_op jit(solution)/shard_map/ppermute | solution.py:744
  18.4 16.9 %collective-permute-start.6 = (bf16[768,768]{1,0:T(8,128)(2,1)}, bf16[768,768]{1,0:T(8,128)(2,1)}, u32[]{:S(2)}, u32[]{:S(2)}) collective-permute-start(bf16[768,768]{1,0:T(8,128)(2,1)} %bitcast.71), channel_id=1, source_target_pairs={{0,8},{8,0},{16,24},{24,16},{1,9},{9,1},{17,25},{25,17},{2,10},{10... | collective-permute-start | bytes 3538952 | tf_op jit(solution)/shard_map/ppermute | solution.py:744
  34.7 49.1 %collective-permute-start.12 = (bf16[4,56,768]{2,1,0:T(8,128)(2,1)}, bf16[4,56,768]{2,1,0:T(8,128)(2,1)S(1)}, u32[]{:S(2)}, u32[]{:S(2)}) collective-permute-start(bf16[4,56,768]{2,1,0:T(8,128)(2,1)} %param.19), channel_id=1, source_target_pairs={{0,16},{8,24},{16,0},{24,8},{1,17},{9,25},{17,1},{25,9},{2,18},{10... | collective-permute-start | bytes 1032200 | tf_op jit(solution)/shard_map/ppermute | solution.py:741
  37.9 45.8 %copy-start.23 = (bf16[4,56,768]{2,1,0:T(8,128)(2,1)S(1)}, bf16[4,56,768]{2,1,0:T(8,128)(2,1)}, u32[]{:S(2)}) copy-start(bf16[4,56,768]{2,1,0:T(8,128)(2,1)} %param.19) | copy-start | bytes 1032196
  39.2 48.0 %copy-start.33 = (bf16[288,768]{1,0:T(8,128)(2,1)S(1)}, bf16[288,768]{1,0:T(8,128)(2,1)}, u32[]{:S(2)}) copy-start(bf16[288,768]{1,0:T(8,128)(2,1)} %get-tuple-element.90) | copy-start | bytes 1327108
  39.2 50.6 %collective-permute-start.10 = (bf16[160,768]{1,0:T(8,128)(2,1)}, bf16[160,768]{1,0:T(8,128)(2,1)S(1)}, u32[]{:S(2)}, u32[]{:S(2)}) collective-permute-start(bf16[160,768]{1,0:T(8,128)(2,1)} %get-tuple-element.93), channel_id=1, source_target_pairs={{0,16},{8,24},{16,0},{24,8},{1,17},{9,25},{17,1},{25,9},{2,18},{10... | collective-permute-start | bytes 737288 | tf_op jit(solution)/shard_map/ppermute | solution.py:741
  87.2 45.4 %collective-permute-start.9 = (bf16[288,768]{1,0:T(8,128)(2,1)S(1)}, bf16[288,768]{1,0:T(8,128)(2,1)S(1)}, u32[]{:S(2)}, u32[]{:S(2)}) collective-permute-start(bf16[288,768]{1,0:T(8,128)(2,1)S(1)} %copy-done.33), channel_id=1, source_target_pairs={{0,16},{8,24},{16,0},{24,8},{1,17},{9,25},{17,1},{25,9},{2,18},{10... | collective-permute-start | bytes 1327112 | tf_op jit(solution)/shard_map/ppermute | solution.py:741
  117.2 81.1 %collective-permute-start.38 = (bf16[320,768]{1,0:T(8,128)(2,1)}, bf16[320,768]{1,0:T(8,128)(2,1)S(1)}, u32[]{:S(2)}, u32[]{:S(2)}) collective-permute-start(bf16[320,768]{1,0:T(8,128)(2,1)} %get-tuple-element.158.refs_0_), channel_id=1, source_target_pairs={{16,17},{17,16},{18,19},{19,18},{20,21},{21,20},{22,23},{23,22},{2... | collective-permute-start | bytes 1474568 | tf_op jit(solution)/shard_map/ppermute | solution.py:688
  196.2 16.2 %collective-permute-start.13 = (bf16[288,768]{1,0:T(8,128)(2,1)}, bf16[288,768]{1,0:T(8,128)(2,1)S(1)}, u32[]{:S(2)}, u32[]{:S(2)}) collective-permute-start(bf16[288,768]{1,0:T(8,128)(2,1)} %get-tuple-element.122), channel_id=1, source_target_pairs={{0,16},{8,24},{16,0},{24,8},{1,17},{9,25},{17,1},{25,9},{2,18},{10... | collective-permute-start | bytes 1327112 | tf_op jit(solution)/shard_map/ppermute | solution.py:741
  196.3 16.1 %collective-permute-start.14 = (bf16[160,768]{1,0:T(8,128)(2,1)S(1)}, bf16[160,768]{1,0:T(8,128)(2,1)S(1)}, u32[]{:S(2)}, u32[]{:S(2)}) collective-permute-start(bf16[160,768]{1,0:T(8,128)(2,1)S(1)} %copy-done.34), channel_id=1, source_target_pairs={{0,16},{8,24},{16,0},{24,8},{1,17},{9,25},{17,1},{25,9},{2,18},{10... | collective-permute-start | bytes 737288 | tf_op jit(solution)/shard_map/ppermute | solution.py:741
  198.3 16.2 %collective-permute-start.39 = (bf16[320,768]{1,0:T(8,128)(2,1)S(1)}, bf16[320,768]{1,0:T(8,128)(2,1)S(1)}, u32[]{:S(2)}, u32[]{:S(2)}) collective-permute-start(bf16[320,768]{1,0:T(8,128)(2,1)S(1)} %copy-done.19), channel_id=1, source_target_pairs={{0,8},{8,0},{16,24},{24,16},{1,9},{9,1},{17,25},{25,17},{2,10},{10... | collective-permute-start | bytes 1474568 | tf_op jit(solution)/shard_map/ppermute | solution.py:744
  198.3 16.2 %collective-permute-start.40 = (bf16[320,768]{1,0:T(8,128)(2,1)S(1)}, bf16[320,768]{1,0:T(8,128)(2,1)S(1)}, u32[]{:S(2)}, u32[]{:S(2)}) collective-permute-start(bf16[320,768]{1,0:T(8,128)(2,1)S(1)} %collective-permute-done.38.refs_1_), channel_id=1, source_target_pairs={{0,8},{8,0},{16,24},{24,16},{1,9},{9,1},{17,25},{25,17},{2,10},{10... | collective-permute-start | bytes 1474568 | tf_op jit(solution)/shard_map/ppermute | solution.py:744
  228.9 18.5 %collective-permute-start.41 = (bf16[384,768]{1,0:T(8,128)(2,1)}, bf16[384,768]{1,0:T(8,128)(2,1)}, u32[]{:S(2)}, u32[]{:S(2)}) collective-permute-start(bf16[384,768]{1,0:T(8,128)(2,1)} %constant_dynamic-slice_fusion.5), channel_id=1, source_target_pairs={{16,18},{17,19},{18,16},{19,17},{20,22},{21,23},{22,20},{23,21},{2... | collective-permute-start | bytes 1769480 | tf_op jit(solution)/shard_map/ppermute | solution.py:688
  233.9 28.5 %collective-permute-start.53 = (bf16[400,768]{1,0:T(8,128)(2,1)}, bf16[400,768]{1,0:T(8,128)(2,1)}, u32[]{:S(2)}, u32[]{:S(2)}) collective-permute-start(bf16[400,768]{1,0:T(8,128)(2,1)} %constant_dynamic-slice_fusion.1), channel_id=1, source_target_pairs={{16,18},{17,19},{18,16},{19,17},{20,22},{21,23},{22,20},{23,21},{2... | collective-permute-start | bytes 1843208 | tf_op jit(solution)/shard_map/ppermute | solution.py:688
  241.7 85.1 %collective-permute-start.23 = (bf16[1536,768]{1,0:T(8,128)(2,1)}, bf16[1536,768]{1,0:T(8,128)(2,1)}, u32[]{:S(2)}, u32[]{:S(2)}) collective-permute-start(bf16[1536,768]{1,0:T(8,128)(2,1)} %slice.166), channel_id=1, source_target_pairs={{0,8},{8,0},{16,24},{24,16},{1,9},{9,1},{17,25},{25,17},{2,10},{10... | collective-permute-start | bytes 7077896 | tf_op jit(solution)/shard_map/ppermute | solution.py:744
  241.7 24.8 %collective-permute-start.30 = (bf16[576,768]{1,0:T(8,128)(2,1)S(1)}, bf16[576,768]{1,0:T(8,128)(2,1)}, u32[]{:S(2)}, u32[]{:S(2)}) collective-permute-start(bf16[576,768]{1,0:T(8,128)(2,1)S(1)} %copy-done.13), channel_id=1, source_target_pairs={{0,1},{1,0},{2,3},{3,2},{4,5},{5,4},{6,7},{7,6},{8,9},{9,8},{10,11... | collective-permute-start | bytes 2654216 | tf_op jit(solution)/shard_map/ppermute | solution.py:688
  249.4 41.3 %copy-start.26 = (bf16[288,768]{1,0:T(8,128)(2,1)S(1)}, bf16[288,768]{1,0:T(8,128)(2,1)}, u32[]{:S(2)}) copy-start(bf16[288,768]{1,0:T(8,128)(2,1)} %get-tuple-element.92) | copy-start | bytes 1327108
  249.4 19.1 %collective-permute-start.42 = (bf16[192,768]{1,0:T(8,128)(2,1)}, bf16[192,768]{1,0:T(8,128)(2,1)}, u32[]{:S(2)}, u32[]{:S(2)}) collective-permute-start(bf16[192,768]{1,0:T(8,128)(2,1)} %constant_dynamic-slice_fusion.4), channel_id=1, source_target_pairs={{16,20},{17,21},{18,22},{19,23},{20,16},{21,17},{22,18},{23,19},{2... | collective-permute-start | bytes 884744 | tf_op jit(solution)/shard_map/ppermute | solution.py:688
  263.7 25.0 %collective-permute-start.54 = (bf16[200,768]{1,0:T(8,128)(2,1)S(1)}, bf16[200,768]{1,0:T(8,128)(2,1)S(1)}, u32[]{:S(2)}, u32[]{:S(2)}) collective-permute-start(bf16[200,768]{1,0:T(8,128)(2,1)S(1)} %constant_dynamic-slice_fusion), channel_id=1, source_target_pairs={{16,20},{17,21},{18,22},{19,23},{20,16},{21,17},{22,18},{23,19},{2... | collective-permute-start | bytes 921608 | tf_op jit(solution)/shard_map/ppermute | solution.py:688
  266.3 40.1 %collective-permute-start.31 = (bf16[576,768]{1,0:T(8,128)(2,1)S(1)}, bf16[576,768]{1,0:T(8,128)(2,1)}, u32[]{:S(2)}, u32[]{:S(2)}) collective-permute-start(bf16[576,768]{1,0:T(8,128)(2,1)S(1)} %copy-done.13), channel_id=1, source_target_pairs={{0,8},{8,0},{16,24},{24,16},{1,9},{9,1},{17,25},{25,17},{2,10},{10... | collective-permute-start | bytes 2654216 | tf_op jit(solution)/shard_map/ppermute | solution.py:744
  266.4 44.0 %collective-permute-start.32 = (bf16[576,768]{1,0:T(8,128)(2,1)}, bf16[576,768]{1,0:T(8,128)(2,1)}, u32[]{:S(2)}, u32[]{:S(2)}) collective-permute-start(bf16[576,768]{1,0:T(8,128)(2,1)} %collective-permute-done.30.refs_1_), channel_id=1, source_target_pairs={{0,8},{8,0},{16,24},{24,16},{1,9},{9,1},{17,25},{25,17},{2,10},{10... | collective-permute-start | bytes 2654216 | tf_op jit(solution)/shard_map/ppermute | solution.py:744
  269.6 28.6 %collective-permute-start.43 = (bf16[192,768]{1,0:T(8,128)(2,1)S(1)}, bf16[192,768]{1,0:T(8,128)(2,1)S(1)}, u32[]{:S(2)}, u32[]{:S(2)}) collective-permute-start(bf16[192,768]{1,0:T(8,128)(2,1)S(1)} %dynamic-slice_add_fusion.11), channel_id=1, source_target_pairs={{16,20},{17,21},{18,22},{19,23},{20,16},{21,17},{22,18},{23,19},{2... | collective-permute-start | bytes 884744 | tf_op jit(solution)/shard_map/ppermute | solution.py:688
  288.7 14.5 %collective-permute-start.55 = (bf16[200,768]{1,0:T(8,128)(2,1)S(1)}, bf16[200,768]{1,0:T(8,128)(2,1)}, u32[]{:S(2)}, u32[]{:S(2)}) collective-permute-start(bf16[200,768]{1,0:T(8,128)(2,1)S(1)} %dynamic-slice_add_fusion.8), channel_id=1, source_target_pairs={{16,20},{17,21},{18,22},{19,23},{20,16},{21,17},{22,18},{23,19},{2... | collective-permute-start | bytes 921608 | tf_op jit(solution)/shard_map/ppermute | solution.py:688
  298.3 59.7 %collective-permute-start.15 = (bf16[1568,768]{1,0:T(8,128)(2,1)}, bf16[1568,768]{1,0:T(8,128)(2,1)}, u32[]{:S(2)}, u32[]{:S(2)}) collective-permute-start(bf16[1568,768]{1,0:T(8,128)(2,1)} %slice.160), channel_id=1, source_target_pairs={{0,8},{8,0},{16,24},{24,16},{1,9},{9,1},{17,25},{25,17},{2,10},{10... | collective-permute-start | bytes 7225352 | tf_op jit(solution)/shard_map/ppermute | solution.py:744
  303.3 81.4 %collective-permute-start.44 = (bf16[384,768]{1,0:T(8,128)(2,1)S(1)}, bf16[384,768]{1,0:T(8,128)(2,1)S(1)}, u32[]{:S(2)}, u32[]{:S(2)}) collective-permute-start(bf16[384,768]{1,0:T(8,128)(2,1)S(1)} %maximum_select_fusion.17), channel_id=1, source_target_pairs={{16,18},{17,19},{18,16},{19,17},{20,22},{21,23},{22,20},{23,21},{2... | collective-permute-start | bytes 1769480 | tf_op jit(solution)/shard_map/ppermute | solution.py:688
  306.5 81.7 %collective-permute-start.56 = (bf16[400,768]{1,0:T(8,128)(2,1)S(1)}, bf16[400,768]{1,0:T(8,128)(2,1)S(1)}, u32[]{:S(2)}, u32[]{:S(2)}) collective-permute-start(bf16[400,768]{1,0:T(8,128)(2,1)S(1)} %maximum_select_fusion.13), channel_id=1, source_target_pairs={{16,18},{17,19},{18,16},{19,17},{20,22},{21,23},{22,20},{23,21},{2... | collective-permute-start | bytes 1843208 | tf_op jit(solution)/shard_map/ppermute | solution.py:688
  326.6 20.6 %collective-permute-start.33 = (bf16[384,768]{1,0:T(8,128)(2,1)S(1)}, bf16[384,768]{1,0:T(8,128)(2,1)S(1)}, u32[]{:S(2)}, u32[]{:S(2)}) collective-permute-start(bf16[384,768]{1,0:T(8,128)(2,1)S(1)} %constant_dynamic-slice_fusion.7), channel_id=1, source_target_pairs={{0,2},{1,3},{2,0},{3,1},{4,6},{5,7},{6,4},{7,5},{8,10},{9,11},{10,... | collective-permute-start | bytes 1769480 | tf_op jit(solution)/shard_map/ppermute | solution.py:688
  326.7 34.3 %slice-start = ((s8[4767744]{0:T(1024)(128)(4,1)}), s8[4194304]{0:T(1024)(128)(4,1)S(1)}, s32[]{:S(2)}) async-start(s8[4767744]{0:T(1024)(128)(4,1)} %bitcast.42), calls=%async_computation | async-start | bytes 8388608
  326.7 31.0 %collective-permute-start.48 = (bf16[400,768]{1,0:T(8,128)(2,1)S(1)}, bf16[400,768]{1,0:T(8,128)(2,1)S(1)}, u32[]{:S(2)}, u32[]{:S(2)}) collective-permute-start(bf16[400,768]{1,0:T(8,128)(2,1)S(1)} %constant_dynamic-slice_fusion.3), channel_id=1, source_target_pairs={{0,2},{1,3},{2,0},{3,1},{4,6},{5,7},{6,4},{7,5},{8,10},{9,11},{10,... | collective-permute-start | bytes 1843208 | tf_op jit(solution)/shard_map/ppermute | solution.py:688
  347.2 67.3 %collective-permute-start.24 = (bf16[768,768]{1,0:T(8,128)(2,1)S(1)}, bf16[768,768]{1,0:T(8,128)(2,1)S(1)}, u32[]{:S(2)}, u32[]{:S(2)}) collective-permute-start(bf16[768,768]{1,0:T(8,128)(2,1)S(1)} %constant_dynamic-slice_fusion.10), channel_id=1, source_target_pairs={{0,1},{1,0},{2,3},{3,2},{4,5},{5,4},{6,7},{7,6},{8,9},{9,8},{10,11... | collective-permute-start | bytes 3538952 | tf_op jit(solution)/shard_map/ppermute | solution.py:688
  357.8 20.3 %collective-permute-start.34 = (bf16[192,768]{1,0:T(8,128)(2,1)S(1)}, bf16[192,768]{1,0:T(8,128)(2,1)S(1)}, u32[]{:S(2)}, u32[]{:S(2)}) collective-permute-start(bf16[192,768]{1,0:T(8,128)(2,1)S(1)} %constant_dynamic-slice_fusion.6), channel_id=1, source_target_pairs={{0,4},{1,5},{2,6},{3,7},{4,0},{5,1},{6,2},{7,3},{8,12},{9,13},{10,... | collective-permute-start | bytes 884744 | tf_op jit(solution)/shard_map/ppermute | solution.py:688
  358.0 26.6 %collective-permute-start.49 = (bf16[200,768]{1,0:T(8,128)(2,1)S(1)}, bf16[200,768]{1,0:T(8,128)(2,1)S(1)}, u32[]{:S(2)}, u32[]{:S(2)}) collective-permute-start(bf16[200,768]{1,0:T(8,128)(2,1)S(1)} %constant_dynamic-slice_fusion.2), channel_id=1, source_target_pairs={{0,4},{1,5},{2,6},{3,7},{4,0},{5,1},{6,2},{7,3},{8,12},{9,13},{10,... | collective-permute-start | bytes 921608 | tf_op jit(solution)/shard_map/ppermute | solution.py:688
  378.1 36.9 %collective-permute-start.16 = (bf16[784,768]{1,0:T(8,128)(2,1)S(1)}, bf16[784,768]{1,0:T(8,128)(2,1)S(1)}, u32[]{:S(2)}, u32[]{:S(2)}) collective-permute-start(bf16[784,768]{1,0:T(8,128)(2,1)S(1)} %constant_dynamic-slice_fusion.13), channel_id=1, source_target_pairs={{0,1},{1,0},{2,3},{3,2},{4,5},{5,4},{6,7},{7,6},{8,9},{9,8},{10,11... | collective-permute-start | bytes 3612680 | tf_op jit(solution)/shard_map/ppermute | solution.py:688
  384.6 19.5 %collective-permute-start.35 = (bf16[192,768]{1,0:T(8,128)(2,1)S(1)}, bf16[192,768]{1,0:T(8,128)(2,1)S(1)}, u32[]{:S(2)}, u32[]{:S(2)}) collective-permute-start(bf16[192,768]{1,0:T(8,128)(2,1)S(1)} %dynamic-slice_add_fusion.12), channel_id=1, source_target_pairs={{0,4},{1,5},{2,6},{3,7},{4,0},{5,1},{6,2},{7,3},{8,12},{9,13},{10,... | collective-permute-start | bytes 884744 | tf_op jit(solution)/shard_map/ppermute | solution.py:688
  384.7 25.9 %collective-permute-start.50 = (bf16[200,768]{1,0:T(8,128)(2,1)S(1)}, bf16[200,768]{1,0:T(8,128)(2,1)S(1)}, u32[]{:S(2)}, u32[]{:S(2)}) collective-permute-start(bf16[200,768]{1,0:T(8,128)(2,1)S(1)} %dynamic-slice_add_fusion.9), channel_id=1, source_target_pairs={{0,4},{1,5},{2,6},{3,7},{4,0},{5,1},{6,2},{7,3},{8,12},{9,13},{10,... | collective-permute-start | bytes 921608 | tf_op jit(solution)/shard_map/ppermute | solution.py:688
  388.1 44.6 %collective-permute-start.45 = (bf16[768,768]{1,0:T(8,128)(2,1)S(1)}, bf16[768,768]{1,0:T(8,128)(2,1)S(1)}, u32[]{:S(2)}, u32[]{:S(2)}) collective-permute-start(bf16[768,768]{1,0:T(8,128)(2,1)S(1)} %maximum_select_fusion.11), channel_id=1, source_target_pairs={{16,17},{17,16},{18,19},{19,18},{20,21},{21,20},{22,23},{23,22},{2... | collective-permute-start | bytes 3538952 | tf_op jit(solution)/shard_map/ppermute | solution.py:688
  404.1 79.4 %collective-permute-start.11 = (bf16[4,56,768]{2,1,0:T(8,128)(2,1)}, bf16[4,56,768]{2,1,0:T(8,128)(2,1)S(1)}, u32[]{:S(2)}, u32[]{:S(2)}) collective-permute-start(bf16[4,56,768]{2,1,0:T(8,128)(2,1)} %pad_maximum_fusion.2), channel_id=1, source_target_pairs={{0,16},{8,24},{16,0},{24,8},{1,17},{9,25},{17,1},{25,9},{2,18},{10... | collective-permute-start | bytes 1032200 | tf_op jit(solution)/shard_map/ppermute | solution.py:741
  410.6 47.4 %collective-permute-start.57 = (bf16[800,768]{1,0:T(8,128)(2,1)S(1)}, bf16[800,768]{1,0:T(8,128)(2,1)S(1)}, u32[]{:S(2)}, u32[]{:S(2)}) collective-permute-start(bf16[800,768]{1,0:T(8,128)(2,1)S(1)} %maximum_select_fusion.7), channel_id=1, source_target_pairs={{16,17},{17,16},{18,19},{19,18},{20,21},{21,20},{22,23},{23,22},{2... | collective-permute-start | bytes 3686408 | tf_op jit(solution)/shard_map/ppermute | solution.py:688
  414.5 69.1 %collective-permute-start.36 = (bf16[384,768]{1,0:T(8,128)(2,1)S(1)}, bf16[384,768]{1,0:T(8,128)(2,1)S(1)}, u32[]{:S(2)}, u32[]{:S(2)}) collective-permute-start(bf16[384,768]{1,0:T(8,128)(2,1)S(1)} %maximum_select_fusion.16), channel_id=1, source_target_pairs={{0,2},{1,3},{2,0},{3,1},{4,6},{5,7},{6,4},{7,5},{8,10},{9,11},{10,... | collective-permute-start | bytes 1769480 | tf_op jit(solution)/shard_map/ppermute | solution.py:688
  415.0 28.4 %collective-permute-start.25 = (bf16[384,768]{1,0:T(8,128)(2,1)S(1)}, bf16[384,768]{1,0:T(8,128)(2,1)S(1)}, u32[]{:S(2)}, u32[]{:S(2)}) collective-permute-start(bf16[384,768]{1,0:T(8,128)(2,1)S(1)} %constant_dynamic-slice_fusion.9), channel_id=1, source_target_pairs={{0,2},{1,3},{2,0},{3,1},{4,6},{5,7},{6,4},{7,5},{8,10},{9,11},{10,... | collective-permute-start | bytes 1769480 | tf_op jit(solution)/shard_map/ppermute | solution.py:688
  432.7 22.3 %collective-permute-start.17 = (bf16[392,768]{1,0:T(8,128)(2,1)S(1)}, bf16[392,768]{1,0:T(8,128)(2,1)S(1)}, u32[]{:S(2)}, u32[]{:S(2)}) collective-permute-start(bf16[392,768]{1,0:T(8,128)(2,1)S(1)} %constant_dynamic-slice_fusion.12), channel_id=1, source_target_pairs={{0,2},{1,3},{2,0},{3,1},{4,6},{5,7},{6,4},{7,5},{8,10},{9,11},{10,... | collective-permute-start | bytes 1806344 | tf_op jit(solution)/shard_map/ppermute | solution.py:688
  443.4 100.8 %collective-permute-start.46 = (bf16[1536,768]{1,0:T(8,128)(2,1)}, bf16[1536,768]{1,0:T(8,128)(2,1)}, u32[]{:S(2)}, u32[]{:S(2)}) collective-permute-start(bf16[1536,768]{1,0:T(8,128)(2,1)} %maximum_select_fusion.5), channel_id=1, source_target_pairs={{0,8},{8,0},{16,24},{24,16},{1,9},{9,1},{17,25},{25,17},{2,10},{10... | collective-permute-start | bytes 7077896 | tf_op jit(solution)/shard_map/ppermute | solution.py:744
  455.1 21.7 %collective-permute-start.26 = (bf16[192,768]{1,0:T(8,128)(2,1)S(1)}, bf16[192,768]{1,0:T(8,128)(2,1)S(1)}, u32[]{:S(2)}, u32[]{:S(2)}) collective-permute-start(bf16[192,768]{1,0:T(8,128)(2,1)S(1)} %constant_dynamic-slice_fusion.8), channel_id=1, source_target_pairs={{0,4},{1,5},{2,6},{3,7},{4,0},{5,1},{6,2},{7,3},{8,12},{9,13},{10,... | collective-permute-start | bytes 884744 | tf_op jit(solution)/shard_map/ppermute | solution.py:688
  458.0 25.3 %collective-permute-start.18 = (bf16[196,768]{1,0:T(8,128)(2,1)S(1)}, bf16[196,768]{1,0:T(8,128)(2,1)S(1)}, u32[]{:S(2)}, u32[]{:S(2)}) collective-permute-start(bf16[196,768]{1,0:T(8,128)(2,1)S(1)} %constant_dynamic-slice_fusion.11), channel_id=1, source_target_pairs={{0,4},{1,5},{2,6},{3,7},{4,0},{5,1},{6,2},{7,3},{8,12},{9,13},{10,... | collective-permute-start | bytes 903176 | tf_op jit(solution)/shard_map/ppermute | solution.py:688
  476.8 38.0 %collective-permute-start.51 = (bf16[400,768]{1,0:T(8,128)(2,1)S(1)}, bf16[400,768]{1,0:T(8,128)(2,1)}, u32[]{:S(2)}, u32[]{:S(2)}) collective-permute-start(bf16[400,768]{1,0:T(8,128)(2,1)S(1)} %maximum_select_fusion.12), channel_id=1, source_target_pairs={{0,2},{1,3},{2,0},{3,1},{4,6},{5,7},{6,4},{7,5},{8,10},{9,11},{10,... | collective-permute-start | bytes 1843208 | tf_op jit(solution)/shard_map/ppermute | solution.py:688
  483.3 23.7 %collective-permute-start.27 = (bf16[192,768]{1,0:T(8,128)(2,1)S(1)}, bf16[192,768]{1,0:T(8,128)(2,1)S(1)}, u32[]{:S(2)}, u32[]{:S(2)}) collective-permute-start(bf16[192,768]{1,0:T(8,128)(2,1)S(1)} %dynamic-slice_add_fusion.13), channel_id=1, source_target_pairs={{0,4},{1,5},{2,6},{3,7},{4,0},{5,1},{6,2},{7,3},{8,12},{9,13},{10,... | collective-permute-start | bytes 884744 | tf_op jit(solution)/shard_map/ppermute | solution.py:688
  483.5 79.7 %collective-permute-start.58 = (bf16[1600,768]{1,0:T(8,128)(2,1)S(1)}, bf16[1600,768]{1,0:T(8,128)(2,1)}, u32[]{:S(2)}, u32[]{:S(2)}) collective-permute-start(bf16[1600,768]{1,0:T(8,128)(2,1)S(1)} %maximum_select_fusion.1), channel_id=1, source_target_pairs={{0,8},{8,0},{16,24},{24,16},{1,9},{9,1},{17,25},{25,17},{2,10},{10... | collective-permute-start | bytes 7372808 | tf_op jit(solution)/shard_map/ppermute | solution.py:744
  483.6 29.1 %collective-permute-start.19 = (bf16[196,768]{1,0:T(8,128)(2,1)S(1)}, bf16[196,768]{1,0:T(8,128)(2,1)}, u32[]{:S(2)}, u32[]{:S(2)}) collective-permute-start(bf16[196,768]{1,0:T(8,128)(2,1)S(1)} %dynamic-slice_add_fusion.10), channel_id=1, source_target_pairs={{0,4},{1,5},{2,6},{3,7},{4,0},{5,1},{6,2},{7,3},{8,12},{9,13},{10,... | collective-permute-start | bytes 903176 | tf_op jit(solution)/shard_map/ppermute | solution.py:688
  507.7 34.9 %collective-permute-start.37 = (bf16[768,768]{1,0:T(8,128)(2,1)}, bf16[768,768]{1,0:T(8,128)(2,1)}, u32[]{:S(2)}, u32[]{:S(2)}) collective-permute-start(bf16[768,768]{1,0:T(8,128)(2,1)} %maximum_select_fusion.10), channel_id=1, source_target_pairs={{0,1},{1,0},{2,3},{3,2},{4,5},{5,4},{6,7},{7,6},{8,9},{9,8},{10,11... | collective-permute-start | bytes 3538952 | tf_op jit(solution)/shard_map/ppermute | solution.py:688
  512.7 16.6 %collective-permute-start.28 = (bf16[384,768]{1,0:T(8,128)(2,1)}, bf16[384,768]{1,0:T(8,128)(2,1)}, u32[]{:S(2)}, u32[]{:S(2)}) collective-permute-start(bf16[384,768]{1,0:T(8,128)(2,1)} %maximum_select_fusion.15), channel_id=1, source_target_pairs={{0,2},{1,3},{2,0},{3,1},{4,6},{5,7},{6,4},{7,5},{8,10},{9,11},{10,... | collective-permute-start | bytes 1769480 | tf_op jit(solution)/shard_map/ppermute | solution.py:688
  514.8 25.4 %collective-permute-start.20 = (bf16[392,768]{1,0:T(8,128)(2,1)}, bf16[392,768]{1,0:T(8,128)(2,1)}, u32[]{:S(2)}, u32[]{:S(2)}) collective-permute-start(bf16[392,768]{1,0:T(8,128)(2,1)} %maximum_select_fusion.14), channel_id=1, source_target_pairs={{0,2},{1,3},{2,0},{3,1},{4,6},{5,7},{6,4},{7,5},{8,10},{9,11},{10,... | collective-permute-start | bytes 1806344 | tf_op jit(solution)/shard_map/ppermute | solution.py:688
  529.3 33.9 %collective-permute-start.52 = (bf16[800,768]{1,0:T(8,128)(2,1)S(1)}, bf16[800,768]{1,0:T(8,128)(2,1)S(1)}, u32[]{:S(2)}, u32[]{:S(2)}) collective-permute-start(bf16[800,768]{1,0:T(8,128)(2,1)S(1)} %maximum_select_fusion.6), channel_id=1, source_target_pairs={{0,1},{1,0},{2,3},{3,2},{4,5},{5,4},{6,7},{7,6},{8,9},{9,8},{10,11... | collective-permute-start | bytes 3686408 | tf_op jit(solution)/shard_map/ppermute | solution.py:688
  540.3 48.2 %collective-permute-start.29 = (bf16[768,768]{1,0:T(8,128)(2,1)S(1)}, bf16[768,768]{1,0:T(8,128)(2,1)S(1)}, u32[]{:S(2)}, u32[]{:S(2)}) collective-permute-start(bf16[768,768]{1,0:T(8,128)(2,1)S(1)} %maximum_select_fusion.9), channel_id=1, source_target_pairs={{0,1},{1,0},{2,3},{3,2},{4,5},{5,4},{6,7},{7,6},{8,9},{9,8},{10,11... | collective-permute-start | bytes 3538952 | tf_op jit(solution)/shard_map/ppermute | solution.py:688
  542.6 68.7 %collective-permute-start.21 = (bf16[784,768]{1,0:T(8,128)(2,1)S(1)}, bf16[784,768]{1,0:T(8,128)(2,1)S(1)}, u32[]{:S(2)}, u32[]{:S(2)}) collective-permute-start(bf16[784,768]{1,0:T(8,128)(2,1)S(1)} %maximum_select_fusion.8), channel_id=1, source_target_pairs={{0,1},{1,0},{2,3},{3,2},{4,5},{5,4},{6,7},{7,6},{8,9},{9,8},{10,11... | collective-permute-start | bytes 3612680 | tf_op jit(solution)/shard_map/ppermute | solution.py:688
  548.9 76.6 %collective-permute-start.47 = (bf16[1536,768]{1,0:T(8,128)(2,1)}, bf16[1536,768]{1,0:T(8,128)(2,1)}, u32[]{:S(2)}, u32[]{:S(2)}) collective-permute-start(bf16[1536,768]{1,0:T(8,128)(2,1)} %get-tuple-element.162), channel_id=1, source_target_pairs={{0,8},{8,0},{16,24},{24,16},{1,9},{9,1},{17,25},{25,17},{2,10},{10... | collective-permute-start | bytes 7077896 | tf_op jit(solution)/shard_map/ppermute | solution.py:744
  566.7 68.0 %collective-permute-start.59 = (bf16[1600,768]{1,0:T(8,128)(2,1)}, bf16[1600,768]{1,0:T(8,128)(2,1)}, u32[]{:S(2)}, u32[]{:S(2)}) collective-permute-start(bf16[1600,768]{1,0:T(8,128)(2,1)} %get-tuple-element.160), channel_id=1, source_target_pairs={{0,8},{8,0},{16,24},{24,16},{1,9},{9,1},{17,25},{25,17},{2,10},{10... | collective-permute-start | bytes 7372808 | tf_op jit(solution)/shard_map/ppermute | solution.py:744
  616.1 7.6 %collective-permute-start.22 = (bf16[4,56,768]{2,1,0:T(8,128)(2,1)}, bf16[4,56,768]{2,1,0:T(8,128)(2,1)}, u32[]{:S(2)}, u32[]{:S(2)}) collective-permute-start(bf16[4,56,768]{2,1,0:T(8,128)(2,1)} %pad_maximum_fusion.3), channel_id=1, source_target_pairs={{0,16},{8,24},{16,0},{24,8},{1,17},{9,25},{17,1},{25,9},{2,18},{10... | collective-permute-start | bytes 1032200 | tf_op jit(solution)/shard_map/ppermute | solution.py:741
  (33 other events, 232.6 us)

commit v2 on v1

v2 whole, which is shorter than its diff:
```python
import jax
import jax.numpy as jnp
from jax import lax
from jax.experimental import pallas as pl
from jax.experimental.pallas import tpu as pltpu
from jax.sharding import PartitionSpec as P

HEADS = 12
HEAD_DIM = 64
OBJ = 36
PAIRS = HEADS // 2
EPS = 1e-06
NEG = -1000000000.0
F32 = jnp.float32
BF16 = jnp.bfloat16
LANES = 128
BLOCKS = 4
EXTRA = 32
GROUP = 8
VMEM = 60 * 1024 * 1024
FLOPS_PER_US = 1.15e9
PLAN = ("m2", "ce", "co", "ce", "m3", "B01", "co", "ce", "ce", "co", "B23", "co", "end", "ce")


def mm(a, b):
    return jnp.dot(a, b, preferred_element_type=F32)


def mm_nt(a, b):
    return lax.dot_general(a, b, (((1,), (1,)), ((), ())), preferred_element_type=F32)


def mm_tn(a, b):
    return lax.dot_general(a, b, (((0,), (0,)), ((), ())), preferred_element_type=F32)


def each_rows(count, step, body):
    def turn(i, carry):
        body(pl.ds(pl.multiple_of(i * step, step), step))
        return carry

    lax.fori_loop(0, count // step, turn, 0)


def folded(values):
    rows, width = values.shape
    return jnp.sum(values.reshape(rows // 8, 8, width), 0)


class Copies:
    def __init__(self, sems):
        self.sems, self.used, self.stores = sems, 0, []

    def next_sem(self):
        self.used += 1
        return self.sems.at[self.used - 1]

    def load(self, source, target):
        copy = pltpu.make_async_copy(source, target, self.next_sem())
        copy.start()
        return copy

    def load_either(self, first, own, other, target):
        sem = self.next_sem()
        mine = pltpu.make_async_copy(own, target, sem)

        @pl.when(first)
        def _():
            mine.start()

        @pl.when(jnp.logical_not(first))
        def _():
            pltpu.make_async_copy(other, target, sem).start()

        return mine

    def store(self, source, target, alone=False):
        copy = pltpu.make_async_copy(source, target, self.next_sem())
        copy.start()
        if not alone:
            self.stores.append(copy)
        return copy

    def store_either(self, first, source, target, other):
        sem = self.next_sem()
        mine = pltpu.make_async_copy(source, target, sem)

        @pl.when(first)
        def _():
            mine.start()

        @pl.when(jnp.logical_not(first))
        def _():
            pltpu.make_async_copy(source, other, sem).start()

        self.stores.append(mine)

    def drain(self):
        for copy in self.stores:
            copy.wait()
        self.stores = []


class Control:
    def __init__(self, scalars, order):
        self.scalars, self.order = jnp.stack(scalars).astype(jnp.int32), order


def kernel_call(body, control, inputs, outs, scratch, sems, micros, name, aliases=None, more=0):
    n_in, n_out = len(inputs), len(outs)
    after = control.order
    inputs = list(inputs) + list(after)
    outs = list(outs) + [((8, LANES), F32)]

    def kernel(control_ref, *refs):
        @pl.when(control_ref[0] == 1)
        def _():
            body(
                control_ref[1] == 1,
                control_ref[2],
                refs[:n_in],
                refs[len(inputs) : len(inputs) + n_out],
                refs[len(inputs) + n_out + 1 : -1],
                Copies(refs[-1]),
                *[control_ref[3 + i] for i in range(more)],
            )

    *results, token = pl.pallas_call(
        kernel,
        out_shape=[jax.ShapeDtypeStruct(shape, kind) for shape, kind in outs],
        in_specs=[pl.BlockSpec(memory_space=pltpu.SMEM)]
        + [pl.BlockSpec(memory_space=pl.ANY)] * len(inputs),
        out_specs=[pl.BlockSpec(memory_space=pl.ANY)] * len(outs),
        scratch_shapes=[pltpu.VMEM(shape, kind) for shape, kind in scratch]
        + [pltpu.SemaphoreType.DMA((sems,))],
        input_output_aliases=aliases or {},
        compiler_params=pltpu.CompilerParams(vmem_limit_bytes=VMEM),
        cost_estimate=pl.CostEstimate(
            flops=int(micros * FLOPS_PER_US), bytes_accessed=0, transcendentals=0
        ),
        name=name,
    )(control.scalars, *inputs)
    after[:] = [token]
    return results


def norm_stats(values):
    centered = values - jnp.mean(values, -1, keepdims=True)
    inverse = lax.rsqrt(jnp.mean(centered * centered, -1, keepdims=True) + EPS)
    return centered * inverse, inverse


def norm_back(grad_out, normed, inverse, gain):
    scaled = grad_out * gain
    return inverse * (
        scaled
        - jnp.mean(scaled, -1, keepdims=True)
        - normed * jnp.mean(scaled * normed, -1, keepdims=True)
    )


def head_keep(pair, flags):
    lane = lax.broadcasted_iota(jnp.int32, flags.shape, 1)
    head = 2 * pair + jnp.where(lane >= HEAD_DIM, 1, 0)
    return jnp.where(lax.rem(head, 3).astype(F32) != flags, 1.0, 0.0)


def half_masks(rows):
    lane = lax.broadcasted_iota(jnp.int32, (rows, LANES), 1)
    low = jnp.where(lane < HEAD_DIM, 1.0, 0.0)
    return low.astype(BF16), (1.0 - low).astype(BF16), lane < HEAD_DIM


def stacked_halves(piece, low, high):
    return jnp.concatenate([piece * low, piece * high], 0)


def project(x_s, vec, w_s, loads, q_s, k_s, v_s):
    for i, (target, bias) in enumerate(((q_s, 0), (k_s, None), (v_s, 1))):
        loads[i].wait()
        product = mm(x_s[...], w_s[i])
        if bias is not None:
            product = product + vec[bias : bias + 1]
        target[...] = product.astype(BF16)


def attend(blocks, flags_s, flags_at, q_s, k_s, v_s, ctx_s, probs_s):
    for index, (q0, nq, iq, k0, nk, ik) in enumerate(blocks):
        low, high, is_low = half_masks(nq)
        row = lax.broadcasted_iota(jnp.int32, (nq, nk), 0) // iq
        col = lax.broadcasted_iota(jnp.int32, (nq, nk), 1) // ik
        apart = jnp.where(row == col, 0.0, 1.0)
        apart = jnp.concatenate([apart, apart], 0) > 0.0

        def pair_turn(pair, carry):
            lanes = pl.ds(pl.multiple_of(pair * LANES, LANES), LANES)
            q2 = stacked_halves(q_s[pl.ds(q0, nq), lanes], low, high)
            scores = mm_nt(q2, k_s[pl.ds(k0, nk), lanes]) * (HEAD_DIM ** (-0.5))
            scores = jnp.where(apart, NEG, scores)
            shifted = jnp.exp(scores - jnp.max(scores, -1, keepdims=True))
            probs = (shifted / jnp.sum(shifted, -1, keepdims=True)).astype(BF16)
            probs_s[index][pair] = probs
            mixed = mm(probs, v_s[pl.ds(k0, nk), lanes])
            keep = head_keep(pair, flags_s[pl.ds(flags_at + q0, nq), :])
            ctx = jnp.where(is_low, mixed[:nq], mixed[nq:]) * keep
            ctx_s[pl.ds(q0, nq), lanes] = ctx.astype(BF16)
            return carry

        lax.fori_loop(0, PAIRS, pair_turn, 0, unroll=PAIRS)


def attn_finish(x_s, vec, before_s, targets):
    def finish(where):
        before = x_s[where, :].astype(F32) + (before_s[where, :] + vec[2:3])
        before_s[where, :] = before
        normed, _ = norm_stats(before)
        middle = normed * vec[3:4] + vec[4:5]
        for target in targets:
            target[where, :] = middle.astype(target.dtype)

    each_rows(x_s.shape[0], 32, finish)


def ffn_hidden(mid_s, vec, wi_s, wo_s, loads, inner_s, act_s, slope_s, acc_s):
    for j in range(BLOCKS):
        loads[2 * j].wait()
        inner_s[...] = mm(mid_s[...], wi_s[j])

        def activate(where):
            inner = inner_s[where, :] + vec[8 + j : 9 + j]
            phi = 0.5 * (1.0 + lax.erf(inner * (0.5**0.5)))
            act_s[where, :] = (inner * phi).astype(BF16)
            density = jnp.exp(-0.5 * inner * inner) * 0.3989422804014327
            slope_s[j, where, :] = (phi + inner * density).astype(BF16)

        each_rows(mid_s.shape[0], 32, activate)
        loads[2 * j + 1].wait()
        product = mm(act_s[...], wo_s[j])
        acc_s[...] = product if j == 0 else acc_s[...] + product


def ffn_finish(wide_s, acc_s, vec, out_s, at):
    def finish(where):
        after = wide_s[where, :] + (acc_s[where, :] + vec[5:6])
        acc_s[where, :] = after
        normed, _ = norm_stats(after)
        out_s[where, :] = (normed * vec[6:7] + vec[7:8]).astype(BF16)

    each_rows(wide_s.shape[0], 32, finish)


def ffn_back_start(g_s, after_s, vec, acc_s, go_s, sums_s):
    def start(where):
        grad = g_s[where, :].astype(F32)
        normed, inverse = norm_stats(after_s[where, :])
        sums_s[8] += folded(grad * normed)
        sums_s[9] += folded(grad)
        grad_after = norm_back(grad, normed, inverse, vec[6:7])
        acc_s[where, :] = grad_after
        rounded = grad_after.astype(BF16)
        go_s[where, :] = rounded
        sums_s[10] += folded(rounded.astype(F32))

    each_rows(g_s.shape[0], 32, start)


def ffn_back(go_s, slope_s, wi_s, wo_s, loads, gi_s, acc_s):
    for j in range(BLOCKS):
        for load in loads[j]:
            load.wait()
        gi_s[...] = (mm_nt(go_s[...], wo_s[j]) * slope_s[j].astype(F32)).astype(BF16)
        acc_s[...] += mm_nt(gi_s[...], wi_s[j])


def sum_rows(sums_s, extra_s, count):
    extra_s[...] = jnp.zeros_like(extra_s)
    for i in range(count):
        extra_s[i : i + 1, :] = jnp.sum(sums_s[i], 0, keepdims=True)


def load_attn_weights(copies, first, w_in, w_s):
    return [copies.load_either(first, w_in[2 * i], w_in[2 * i + 1], w_s.at[i]) for i in range(4)]


def load_ffn_weights(copies, first, w_in, wi_s, wo_s):
    wi_a, wi_b, wo_a, wo_b = w_in
    width = wi_s.shape[1]
    loads = []
    for j in range(BLOCKS):
        part = pl.ds(j * width, width)
        loads.append(copies.load_either(first, wi_a.at[:, part], wi_b.at[:, part], wi_s.at[j]))
        loads.append(copies.load_either(first, wo_a.at[part, :], wo_b.at[part, :], wo_s.at[j]))
    return loads


def probs_of(blocks):
    return [((PAIRS, 2 * nq, nk), BF16) for _, nq, _, _, nk, _ in blocks]


def first_stage_forward(control, visual, word, flags, weights, blocks_0, blocks_1, name):
    vecs, attn_w, inner_w, outer_w = weights
    rows, width = visual.shape
    total = rows + word.shape[0]
    narrow, wide = ((rows, width), BF16), ((rows, width), F32)
    tall, tall_wide = ((total, width), BF16), ((total, width), F32)
    hidden = ((BLOCKS, rows, width), BF16)
    square = ((4, width, width), BF16)
    flat = [w for pair in attn_w for w in pair]
    probs_0, probs_1 = probs_of(blocks_0), probs_of(blocks_1)

    def body(first, block, ins, outs, scr, copies):
        visual_in, word_in, flags_in, vec_a, vec_b = ins[:5]
        attn_in, ffn_in = ins[5:13], ins[13:17]
        x_s, flags_s, vec0_s, vec1_s, w0_s, w1_s, wi_s, wo_s = scr[:8]
        q_s, k_s, v_s, ctx_s, before_s, wide_s, mid_s, inner_s, acc_s, act_s, slope_s = scr[8:19]
        x1_s, q1_s, k1_s, v1_s, ctx1_s, before1_s, out_s = scr[19:26]
        p0_s, p1_s = scr[26 : 26 + len(probs_0)], scr[26 + len(probs_0) :]
        other = jnp.logical_not(first)
        x_load = copies.load(visual_in, x_s)
        vec0_load = copies.load_either(first, vec_a, vec_b, vec0_s)
        w0_loads = load_attn_weights(copies, first, attn_in, w0_s)
        flags_load = copies.load(flags_in, flags_s)
        ffn_loads = load_ffn_weights(copies, first, ffn_in, wi_s, wo_s)
        word_load = copies.load(word_in, x1_s.at[pl.ds(rows, total - rows)])
        vec1_load = copies.load_either(other, vec_a, vec_b, vec1_s)
        w1_loads = load_attn_weights(copies, other, attn_in, w1_s)
        x_load.wait()
        vec0_load.wait()
        vec = vec0_s[...].astype(F32)
        project(x_s, vec, w0_s, w0_loads, q_s, k_s, v_s)
        flags_load.wait()
        attend(blocks_0, flags_s, 0, q_s, k_s, v_s, ctx_s, p0_s)
        for i, source in enumerate((q_s, k_s, v_s, ctx_s)):
            copies.store(source, outs[i])
        for i, source in enumerate(p0_s):
            copies.store(source, outs[5 + i])
        w0_loads[3].wait()
        before_s[...] = mm(ctx_s[...], w0_s[3])
        attn_finish(x_s, vec, before_s, (wide_s, mid_s))
        copies.store(before_s, outs[4])
        at = 5 + len(p0_s)
        copies.store(mid_s, outs[at])
        ffn_hidden(mid_s, vec, wi_s, wo_s, ffn_loads, inner_s, act_s, slope_s, acc_s)
        copies.store(slope_s, outs[at + 1])
        ffn_finish(wide_s, acc_s, vec, x1_s, 0)
        copies.store(acc_s, outs[at + 2])
        copies.store(x1_s.at[pl.ds(0, rows)], outs[at + 3])
        at += 4
        word_load.wait()
        vec1_load.wait()
        vec = vec1_s[...].astype(F32)
        project(x1_s, vec, w1_s, w1_loads, q1_s, k1_s, v1_s)
        attend(blocks_1, flags_s, 0, q1_s, k1_s, v1_s, ctx1_s, p1_s)
        for i, source in enumerate((q1_s, k1_s, v1_s, ctx1_s)):
            copies.store(source, outs[at + i])
        for i, source in enumerate(p1_s):
            copies.store(source, outs[at + 5 + i])
        w1_loads[3].wait()
        before1_s[...] = mm(ctx1_s[...], w1_s[3])
        attn_finish(x1_s, vec, before1_s, (out_s,))
        copies.store(before1_s, outs[at + 4])
        at += 5 + len(p1_s)
        copies.store(out_s.at[pl.ds(0, rows)], outs[at])
        copies.store(out_s.at[pl.ds(rows, total - rows)], outs[at + 1])
        copies.drain()

    outs = [narrow] * 4 + [wide] + probs_0 + [narrow, hidden, wide, narrow]
    outs += [tall] * 4 + [tall_wide] + probs_1 + [narrow, ((total - rows, width), BF16)]
    scratch = [narrow, ((total, LANES), F32)] + [((16, width), BF16)] * 2
    scratch += [square, square, square, square]
    scratch += [narrow] * 4 + [wide, wide, narrow, wide, wide, narrow, hidden]
    scratch += [tall] * 5 + [tall_wide, tall] + probs_0 + probs_1
    results = kernel_call(
        body,
        control,
        [visual, word, flags] + list(vecs) + flat + list(inner_w) + list(outer_w),
        outs,
        scratch,
        len(outs) + 5 + 8 + 2 * BLOCKS,
        4 + rows / 20 + total / 50,
        name,
    )
    n_0, n_1 = 5 + len(probs_0), 5 + len(probs_1)
    kept_0, rest = results[:n_0], results[n_0:]
    mid_0, slope_0, after_0, visual_1 = rest[:4]
    kept_1, out = rest[4 : 4 + n_1], rest[4 + n_1 :]
    return kept_0, mid_0, (slope_0, after_0), visual_1, kept_1, out[0], out[1]


SECTION = (
    ("x", "g", "vec", "w", "wi", "wo", "q", "k", "v", "ctx", "before", "wide", "mid", "inner", "acc")
    + ("act", "slope", "out", "go", "gb", "gctx", "gq", "gk", "gv", "sums", "extra")
)


class Refs:
    def __init__(self, names, refs):
        for name, ref in zip(names, refs):
            setattr(self, name, ref)
        self.probs = refs[len(names) :]


def section_scratch(rows, width, blocks):
    narrow, wide = ((rows, width), BF16), ((rows, width), F32)
    hidden, square = ((BLOCKS, rows, width), BF16), ((4, width, width), BF16)
    kinds = {
        "vec": ((16, width), BF16),
        "slope": hidden,
        "sums": ((16, 8, width), F32),
        "extra": ((16, width), F32),
    }
    kinds.update({name: wide for name in ("before", "wide", "inner", "acc")})
    kinds.update({name: square for name in ("w", "wi", "wo")})
    return [kinds.get(name, narrow) for name in SECTION] + probs_of(blocks)


def attn_back_start(g_s, before_s, vec, gb_s, sums_s):
    def start(where):
        grad = g_s[where, :].astype(F32)
        normed, inverse = norm_stats(before_s[where, :])
        sums_s[3] += folded(grad * normed)
        sums_s[4] += folded(grad)
        grad_before = norm_back(grad, normed, inverse, vec[3:4])
        before_s[where, :] = grad_before
        rounded = grad_before.astype(BF16)
        gb_s[where, :] = rounded
        sums_s[2] += folded(rounded.astype(F32))

    each_rows(g_s.shape[0], 32, start)


def attend_back(blocks, flags_s, flags_at, gctx_s, q_s, k_s, v_s, probs_s, gq_s, gk_s, gv_s):
    for index, (q0, nq, iq, k0, nk, ik) in enumerate(blocks):
        low, high, is_low = half_masks(nq)

        def pair_turn(pair, carry):
            lanes = pl.ds(pl.multiple_of(pair * LANES, LANES), LANES)
            keep = head_keep(pair, flags_s[pl.ds(flags_at + q0, nq), :]).astype(BF16)
            g2 = stacked_halves(gctx_s[pl.ds(q0, nq), lanes] * keep, low, high)
            q2 = stacked_halves(q_s[pl.ds(q0, nq), lanes], low, high)
            k_piece = k_s[pl.ds(k0, nk), lanes]
            kept = probs_s[index][pair]
            wide_probs = kept.astype(F32)
            g_probs = mm_nt(g2, v_s[pl.ds(k0, nk), lanes])
            inner = jnp.sum(wide_probs * g_probs, -1, keepdims=True)
            g_scores = (wide_probs * (g_probs - inner)).astype(BF16)
            scale = HEAD_DIM ** (-0.5)
            g_q = mm(g_scores, k_piece) * scale
            gq_s[pl.ds(q0, nq), lanes] = jnp.where(is_low, g_q[:nq], g_q[nq:]).astype(BF16)
            gk_s[pl.ds(k0, nk), lanes] = (mm_tn(g_scores, q2) * scale).astype(BF16)
            gv_s[pl.ds(k0, nk), lanes] = mm_tn(kept, g2).astype(BF16)
            return carry

        lax.fori_loop(0, PAIRS, pair_turn, 0, unroll=PAIRS)


def input_grad(before_s, gq_s, gk_s, gv_s, w_s):
    grad_x = before_s[...] + mm_nt(gq_s[...], w_s[0])
    grad_x = grad_x + mm_nt(gk_s[...], w_s[1])
    return (grad_x + mm_nt(gv_s[...], w_s[2])).astype(BF16)


def section_round(first, r, x_in, g_in, weights_in, flags_s, flags_at, flags_load, blocks, copies, outs):
    vec_in, attn_in, ffn_in = weights_in
    out_out, mid_out, go_out, grad_out, kept_out, extra_out = outs
    x_load = copies.load(x_in, r.x)
    vec_load = copies.load_either(first, vec_in[0], vec_in[1], r.vec)
    w_loads = load_attn_weights(copies, first, attn_in, r.w)
    ffn_loads = load_ffn_weights(copies, first, ffn_in, r.wi, r.wo)
    g_load = copies.load(g_in, r.g)

    def run():
        x_load.wait()
        vec_load.wait()
        vec = r.vec[...].astype(F32)
        project(r.x, vec, r.w, w_loads, r.q, r.k, r.v)
        if flags_load:
            flags_load.pop().wait()
        attend(blocks, flags_s, flags_at, r.q, r.k, r.v, r.ctx, r.probs)
        copies.store(r.ctx, kept_out.at[0])
        w_loads[3].wait()
        r.before[...] = mm(r.ctx[...], r.w[3])
        attn_finish(r.x, vec, r.before, (r.wide, r.mid))
        copies.store(r.mid, mid_out)
        ffn_hidden(r.mid, vec, r.wi, r.wo, ffn_loads, r.inner, r.act, r.slope, r.acc)
        ffn_finish(r.wide, r.acc, vec, r.out, 0)
        copies.store(r.out, out_out)
        g_load.wait()
        r.sums[...] = jnp.zeros_like(r.sums)
        ffn_back_start(r.g, r.acc, vec, r.inner, r.go, r.sums)
        copies.store(r.go, go_out)
        ffn_back(r.go, r.slope, r.wi, r.wo, [()] * BLOCKS, r.act, r.inner)
        attn_back_start(r.inner, r.before, vec, r.gb, r.sums)
        copies.store(r.gb, kept_out.at[4])
        r.gctx[...] = mm_nt(r.gb[...], r.w[3]).astype(BF16)
        attend_back(
            blocks, flags_s, flags_at, r.gctx, r.q, r.k, r.v, r.probs, r.gq, r.gk, r.gv
        )
        for i, source in enumerate((r.gq, r.gk, r.gv)):
            copies.store(source, kept_out.at[1 + i])
        r.gctx[...] = input_grad(r.before, r.gq, r.gk, r.gv, r.w)
        copies.store(r.gctx, grad_out)
        sum_rows(r.sums, r.extra, 11)
        copies.store(r.extra, extra_out)

    return run


def second_stage(
    control, word, cot_word, visual, cot_visual, flags, at_word, weights, blocks_w, blocks_v, name
):
    vecs, attn_w, inner_w, outer_w = weights
    width = word.shape[1]
    flat = [w for pair in attn_w for w in pair]
    scratch_w = section_scratch(word.shape[0], width, blocks_w)
    scratch_v = section_scratch(visual.shape[0], width, blocks_v)

    def body(first, block, ins, outs, scr, copies):
        word_in, cot_w_in, visual_in, cot_v_in, flags_in = ins[:5]
        weights_in = (ins[5:7], ins[7:15], ins[15:19])
        flags_s = scr[0]
        word_s = Refs(SECTION, scr[1 : 1 + len(scratch_w)])
        visual_s = Refs(SECTION, scr[1 + len(scratch_w) :])
        flags_load = [copies.load(flags_in, flags_s)]
        n_word = word_in.shape[0]
        pair = outs[1]
        n_visual = visual_in.shape[0]
        grad_out = outs[7]
        outs_w = (
            outs[0],
            pair.at[pl.ds(0, n_word)],
            pair.at[pl.ds(n_word, n_word)],
            grad_out.at[pl.ds(n_visual, n_word)],
            *outs[2:4],
        )
        outs_v = (*outs[4:7], grad_out.at[pl.ds(0, n_visual)], *outs[8:])
        run_w = section_round(
            first, word_s, word_in, cot_w_in, weights_in, flags_s, at_word, flags_load, blocks_w, copies, outs_w
        )
        run_v = section_round(
            jnp.logical_not(first), visual_s, visual_in, cot_v_in, weights_in, flags_s, 0, [], blocks_v, copies, outs_v
        )
        run_w()
        run_v()
        copies.drain()

    outs = []
    for piece, pairs in ((word, [2]), (visual, [1, 1])):
        rows = piece.shape[0]
        outs += [((rows, width), BF16)]
        outs += [((count * rows, width), BF16) for count in pairs]
        if piece is visual:
            outs += [((rows + word.shape[0], width), BF16)]
        outs += [((5, rows, width), BF16), ((16, width), F32)]
    inputs = [word, cot_word, visual, cot_visual, flags] + list(vecs) + flat
    inputs = inputs + list(inner_w) + list(outer_w)
    results = kernel_call(
        body,
        control,
        inputs,
        outs,
        [(flags.shape, F32)] + scratch_w + scratch_v,
        1 + 2 * (3 + 4 + 2 * BLOCKS) + 2 * 10,
        60,
        name,
    )
    return results[:4], results[4:]


def first_stage_back(
    control, grad, kept_1, ffn_0, flags, weights, blocks_1, buffer, name
):
    vecs, attn_w, inner_w, outer_w = weights
    slope_0, after_0 = ffn_0
    rows, width = after_0.shape
    total = kept_1[0].shape[0]
    n_word = total - rows
    flat = [w for pair in attn_w for w in pair]
    n_1 = len(blocks_1)
    narrow, wide = ((rows, width), BF16), ((rows, width), F32)
    tall, tall_wide = ((total, width), BF16), ((total, width), F32)
    hidden, square = ((BLOCKS, rows, width), BF16), ((4, width, width), BF16)

    def body(first, block, ins, outs, scr, copies):
        grad_in, rest = ins[0], ins[1:]
        kept_1_in, rest = rest[: 5 + n_1], rest[5 + n_1 :]
        (slope_in, after_in, flags_in), rest = rest[:3], rest[3:]
        vec_in, attn_in, ffn_in = rest[:2], rest[2:10], rest[10:14]
        kept_1_out, extra_1_out, word_out, go_out, gmid_out, extra_0_out = outs
        g1, q1, k1, v1, ctx1, before1, gb1, gctx1, gq1, gk1, gv1, flags_s = scr[:12]
        vec1, w1, sums1, extra1 = scr[12:16]
        vec0, wi, wo, slope, after, go, gi, acc, sums0, extra0 = scr[16:26]
        probs1 = scr[26:]
        other = jnp.logical_not(first)
        g_loads = [copies.load(grad_in, g1)]
        before_load = copies.load(kept_1_in[4], before1)
        vec1_load = copies.load_either(first, vec_in[0], vec_in[1], vec1)
        w1_load = copies.load_either(first, attn_in[6], attn_in[7], w1.at[3])
        flags_load = copies.load(flags_in, flags_s)
        loads1 = [copies.load(a, b) for a, b in zip(kept_1_in[:3], (q1, k1, v1))]
        loads1 += [copies.load(a, b) for a, b in zip(kept_1_in[5:], probs1)]
        w1_loads = [
            copies.load_either(first, attn_in[2 * i], attn_in[2 * i + 1], w1.at[i])
            for i in range(3)
        ]
        after_load = copies.load(after_in, after)
        vec0_load = copies.load_either(other, vec_in[0], vec_in[1], vec0)
        ffn_loads = load_ffn_weights(copies, other, ffn_in, wi, wo)
        slope_load = copies.load(slope_in, slope)
        for load in g_loads + [before_load, vec1_load]:
            load.wait()
        vec = vec1[...].astype(F32)
        sums1[...] = jnp.zeros_like(sums1)
        sums0[...] = jnp.zeros_like(sums0)
        attn_back_start(g1, before1, vec, gb1, sums1)
        copies.store(gb1, kept_1_out.at[4])
        w1_load.wait()
        gctx1[...] = mm_nt(gb1[...], w1[3]).astype(BF16)
        flags_load.wait()
        for load in loads1:
            load.wait()
        attend_back(blocks_1, flags_s, 0, gctx1, q1, k1, v1, probs1, gq1, gk1, gv1)
        for i, source in enumerate((gq1, gk1, gv1)):
            copies.store(source, kept_1_out.at[1 + i])
        for load in w1_loads:
            load.wait()
        gctx1[...] = input_grad(before1, gq1, gk1, gv1, w1)
        copies.store(gctx1.at[pl.ds(rows, n_word)], word_out)
        sum_rows(sums1, extra1, 11)
        copies.store(extra1, extra_1_out)
        after_load.wait()
        vec0_load.wait()
        vec = vec0[...].astype(F32)
        ffn_back_start(gctx1.at[pl.ds(0, rows)], after, vec, acc, go, sums0)
        copies.store(go, go_out)
        sum_rows(sums0, extra0, 11)
        copies.store(extra0, extra_0_out)
        slope_load.wait()
        for load in ffn_loads:
            load.wait()
        ffn_back(go, slope, wi, wo, [()] * BLOCKS, gi, acc)
        copies.store(acc, gmid_out)
        copies.drain()

    inputs = (
        [grad]
        + list(kept_1)
        + [slope_0, after_0, flags]
        + list(vecs)
        + flat
        + list(inner_w)
        + list(outer_w)
        + [buffer]
    )
    return kernel_call(
        body,
        control,
        inputs,
        [
            ((5, total, width), BF16),
            ((16, width), F32),
            ((n_word, width), BF16),
            narrow,
            wide,
            ((16, width), F32),
        ],
        [tall] * 5
        + [tall_wide]
        + [tall] * 5
        + [(flags.shape, F32), ((16, width), BF16), square, ((16, 8, width), F32), ((16, width), F32)]
        + [((16, width), BF16), square, square, hidden, wide, narrow, narrow, wide]
        + [((16, 8, width), F32), ((16, width), F32)]
        + probs_of(blocks_1),
        2 + 1 + 1 + 1 + 1 + 3 + n_1 + 3 + 1 + 1 + 2 * BLOCKS + 2 + 14,
        8,
        name,
        {len(inputs): 3},
    )


def first_section_back(control, gmid, kept, flags, weights, extra, blocks, name):
    vecs, attn_w, _, _ = weights
    rows, width = gmid.shape
    flat = [w for pair in attn_w for w in pair]
    n_b = len(blocks)
    narrow, wide = ((rows, width), BF16), ((rows, width), F32)

    def body(first, block, ins, outs, scr, copies):
        gmid_in, kept_in, rest = ins[0], ins[1 : 6 + n_b], ins[6 + n_b :]
        flags_in, extra_in, vec_in, attn_in = rest[0], rest[1], rest[2:4], rest[4:12]
        grad_out, kept_out, extra_out = outs
        g, q, k, v, before, gb, gctx, gq, gk, gv, flags_s, vec_s, w, sums, extra_s, more = scr[:16]
        probs = scr[16:]
        early = [copies.load(gmid_in, g), copies.load(kept_in[4], before)]
        early.append(copies.load_either(first, vec_in[0], vec_in[1], vec_s))
        wo_load = copies.load_either(first, attn_in[6], attn_in[7], w.at[3])
        loads = [copies.load(flags_in, flags_s), copies.load(extra_in, more)]
        loads += [copies.load(a, b) for a, b in zip(kept_in[:3], (q, k, v))]
        loads += [copies.load(a, b) for a, b in zip(kept_in[5:], probs)]
        w_loads = [
            copies.load_either(first, attn_in[2 * i], attn_in[2 * i + 1], w.at[i])
            for i in range(3)
        ]
        for load in early:
            load.wait()
        vec = vec_s[...].astype(F32)
        sums[...] = jnp.zeros_like(sums)
        attn_back_start(g, before, vec, gb, sums)
        copies.store(gb, kept_out.at[4])
        wo_load.wait()
        gctx[...] = mm_nt(gb[...], w[3]).astype(BF16)
        for load in loads:
            load.wait()
        attend_back(blocks, flags_s, 0, gctx, q, k, v, probs, gq, gk, gv)
        for i, source in enumerate((gq, gk, gv)):
            copies.store(source, kept_out.at[1 + i])
        sum_rows(sums, extra_s, 5)
        extra_s[...] += more[...]
        copies.store(extra_s, extra_out)
        for load in w_loads:
            load.wait()
        gctx[...] = input_grad(before, gq, gk, gv, w)
        copies.store(gctx, grad_out)
        copies.drain()

    return kernel_call(
        body,
        control,
        [gmid] + list(kept) + [flags, extra] + list(vecs) + flat,
        [narrow, ((5, rows, width), BF16), ((16, width), F32)],
        [wide, narrow, narrow, narrow, wide]
        + [narrow] * 5
        + [(flags.shape, F32), ((16, width), BF16), ((4, width, width), BF16)]
        + [((16, 8, width), F32), ((16, width), F32), ((16, width), F32)]
        + probs_of(blocks),
        3 + 1 + 2 + 3 + n_b + 3 + 6,
        0.01,
        name,
    )


def spare_rows(width):
    unit = 32 * lax.axis_size("dp")
    return -(4 * width + 16) % unit + 16


def attn_weight_grads(control, xs, ctx, kept, extra, buffers, name):
    rows, width = kept.shape[1:]
    n_x = len(xs)
    spare = spare_rows(width)
    total = 4 * width + spare
    half = total // 2
    narrow = ((rows, width), BF16)

    def body(first, block, ins, outs, scr, copies):
        x_in, (kept_in, extra_in) = ins[:n_x], ins[n_x : n_x + 2]
        ctx_in = kept_in.at[0] if ctx is None else ins[n_x + 2]
        x_s, ctx_s, gq_s, gk_s, gv_s, gb_s, extra_s, gw_s, sums_s = scr
        at, x_loads = 0, []
        for piece in x_in:
            x_loads.append(copies.load(piece, x_s.at[pl.ds(at, piece.shape[0])]))
            at += piece.shape[0]
        loads = [copies.load(kept_in.at[1 + i], b) for i, b in enumerate((gq_s, gk_s, gv_s, gb_s))]
        ctx_load = copies.load(ctx_in, ctx_s)
        extra_load = copies.load(extra_in, extra_s)
        for load in x_loads:
            load.wait()
        for i, (left, right) in enumerate(((x_s, gq_s), (x_s, gk_s), (x_s, gv_s), (ctx_s, gb_s))):
            loads[i].wait()
            if i == 3:
                ctx_load.wait()
            gw_s[pl.ds(i * width, width), :] = mm_tn(left[...], right[...]).astype(BF16)
        sums_s[...] = jnp.zeros_like(sums_s)

        def bias_sums(where):
            sums_s[0] += folded(gq_s[where, :].astype(F32))
            sums_s[1] += folded(gv_s[where, :].astype(F32))

        each_rows(rows, 32, bias_sums)
        extra_load.wait()
        for i in range(2):
            extra_s[i : i + 1, :] = jnp.sum(sums_s[i], 0, keepdims=True)
        tail = jnp.concatenate([extra_s[...], jnp.zeros((spare - 16, width), F32)], 0)
        gw_s[pl.ds(4 * width, spare), :] = tail.astype(BF16)
        lower = lax.rem(block, 2) == 0
        keep_out, send_out = outs
        copies.store_either(lower, gw_s.at[pl.ds(0, half)], keep_out, send_out)
        copies.store_either(lower, gw_s.at[pl.ds(half, half)], send_out, keep_out)
        copies.drain()

    inputs = list(xs) + [kept, extra] + ([] if ctx is None else [ctx])
    aliases = {}
    if buffers is not None:
        aliases = {len(inputs) + 1: 0, len(inputs) + 2: 1}
        inputs = inputs + list(buffers)
    return kernel_call(
        body,
        control,
        inputs,
        [((half, width), BF16)] * 2,
        [narrow] * 6
        + [((16, width), F32), ((total, width), BF16), ((2, 8, width), F32)],
        n_x + 4 + 2 + 2,
        2,
        name,
        aliases,
    )


def assemble_ffn(control, evens, odds, name):
    rows, width = evens[0][0].shape

    def body(first, block, ins, outs, scr, copies, core, unused):
        groups = (ins[: 2 * BLOCKS], ins[2 * BLOCKS :])
        inner_out, outer_out, bias_out = outs
        own_s, far_s, out_s, bias_s = scr

        def fetch(j):
            slot, waits = j % 2, []
            for k, target in ((0, own_s), (1, far_s)):
                mine = groups[0][2 * j + k]
                waits.append(
                    copies.load_either(core == 0, mine, groups[1][2 * j + k], target.at[slot])
                )
            return waits

        loads = {0: fetch(0)}
        pending = []
        for j in range(BLOCKS):
            if j + 1 < BLOCKS:
                loads[j + 1] = fetch(j + 1)
            for load in loads[j]:
                load.wait()
            if j >= 2:
                for copy in pending[j - 2]:
                    copy.wait()
            slot = j % 2

            def turn(where):
                value = own_s[slot, where, :].astype(F32) + far_s[slot, where, :].astype(F32)
                out_s[slot, where, :] = jnp.where(unused == 1, 0.0, value)

            each_rows(rows, 32, turn)
            bias_s[j : j + 1, :] = out_s[slot, 2 * width : 2 * width + 1, :]
            part = pl.ds(j * width, width)
            pending.append(
                [
                    copies.store(out_s.at[slot, pl.ds(0, width)], inner_out.at[:, part], True),
                    copies.store(out_s.at[slot, pl.ds(width, width)], outer_out.at[part, :], True),
                ]
            )
        bias = copies.store(bias_s, bias_out, True)
        for copy in pending[-2] + pending[-1] + [bias]:
            copy.wait()

    return kernel_call(
        body,
        control,
        [piece for pair in evens for piece in pair] + [piece for pair in odds for piece in pair],
        [
            ((width, BLOCKS * width), F32),
            ((BLOCKS * width, width), F32),
            ((8, width), F32),
        ],
        [((2, rows, width), BF16)] * 2 + [((2, rows, width), F32), ((8, width), F32)],
        4 * BLOCKS + 1,
        0.01,
        name,
        more=2,
    )


def assemble_attn(control, even, odd, name):
    half, width = even[0].shape
    spare = spare_rows(width)

    def body(first, block, ins, outs, scr, copies, core, unused):
        in_s, out_s = scr
        loads = []
        for h in (0, 1):
            sem = copies.next_sem()
            for p, group in enumerate((ins[:2], ins[2:4])):
                source = group[0 if h == p else 1]

                @pl.when(core == p)
                def _(source=source):
                    pltpu.make_async_copy(source, in_s.at[pl.ds(h * half, half)], sem).start()

            loads.append(pltpu.make_async_copy(ins[0], in_s.at[pl.ds(h * half, half)], sem))

        def turn(where):
            out_s[where, :] = in_s[where, :].astype(F32)

        pieces = [(i * width, width) for i in range(4)] + [(4 * width, spare)]
        waited = 0
        for i, (at, size) in enumerate(pieces):
            while waited < 2 and waited * half < at + size:
                loads[waited].wait()
                waited += 1

            def shifted(where, at=at):
                turn(pl.ds(pl.multiple_of(at + where.start, 32), where.size))

            each_rows(size, 32, shifted)
            copies.store(out_s.at[pl.ds(at, size)], outs[i])
        copies.drain()

    total = 4 * width + spare
    return kernel_call(
        body,
        control,
        list(even) + list(odd),
        [((width, width), F32)] * 4 + [((spare, width), F32)],
        [((total, width), BF16), ((total, width), F32)],
        2 + 5,
        7,
        name,
        more=2,
    )


def ffn_weight_grads(
    control, mids, gos, which, group, vecs, w_inner, w_outer, name, others, first_piece
):
    rows, width = mids[0][1], w_inner[0].shape[0]
    count, n_j = len(mids), len(which)
    together = rows * group
    wide = ((together, width), F32)
    tall = ((count * rows, width), BF16)
    arrays = [array for array, _, _ in mids] + [array for array, _, _ in gos]
    n_others = len(others)
    starts = [start for _, _, start in mids] + [start for _, _, start in gos]

    def body(first, block, ins, outs, scr, copies, early, place):
        vec_a, vec_b, wi_a, wi_b, wo_a, wo_b = ins[2 * count : 2 * count + 6]
        others_in = ins[2 * count + 6 :]
        mid_s, go_s, gi_s, act_s, vec_s, wi_s, wo_s, inner_s, back_s, gw_s, sums_s = scr
        vec_load = copies.load_either(first, vec_a, vec_b, vec_s)
        w_loads = []
        for at, j in enumerate(which):
            part = pl.ds(j * width, width)
            w_loads.append(copies.load_either(first, wi_a.at[:, part], wi_b.at[:, part], wi_s.at[at]))
            w_loads.append(copies.load_either(first, wo_a.at[part, :], wo_b.at[part, :], wo_s.at[at]))
        base = copies.used
        for i in range(count):
            piece = first_piece + i
            slot = jnp.where(early == 1, i, i ^ lax.rem(place, GROUP))
            owner = jnp.where(early == 1, piece, piece ^ place)
            spot = pl.ds(pl.multiple_of(slot * rows, 32), rows)
            mid_sem, go_sem = copies.sems.at[base + slot], copies.sems.at[base + count + slot]
            source = ins[i].at[pl.ds(starts[i], rows)]
            if n_others:

                @pl.when(early == 1)
                def _(source=source, spot=spot, sem=mid_sem):
                    pltpu.make_async_copy(source, mid_s.at[spot], sem).start()

                @pl.when(early != 1)
                def _(source=others_in[i], spot=spot, sem=mid_sem):
                    pltpu.make_async_copy(source, mid_s.at[spot], sem).start()

                at = pl.multiple_of(owner * rows, 32)
            else:
                pltpu.make_async_copy(source, mid_s.at[spot], mid_sem).start()
                at = starts[count + i]
            source = ins[count + i].at[pl.ds(at, rows)]
            pltpu.make_async_copy(source, go_s.at[spot], go_sem).start()

        def wait_for(i):
            spot = pl.ds(i * rows, rows)
            for k, target in enumerate((mid_s, go_s)):
                source, sem = ins[0].at[pl.ds(0, rows)], copies.sems.at[base + k * count + i]
                pltpu.make_async_copy(source, target.at[spot], sem).wait()

        copies.used += 2 * count
        vec_load.wait()
        for at, j in enumerate(which):
            w_loads[2 * at].wait()
            w_loads[2 * at + 1].wait()
            bias = vec_s[8 + j : 9 + j, :].astype(F32)
            sums_s[...] = jnp.zeros_like(sums_s)
            for i in range(count // group):
                if at == 0:
                    for k in range(group * i, group * (i + 1)):
                        wait_for(k)
                spot = slice(i * together, (i + 1) * together)
                inner_s[...] = mm(mid_s[spot, :], wi_s[at])
                back_s[...] = mm_nt(go_s[spot, :], wo_s[at])

                def turn(where, base=i * together):
                    inner = inner_s[where, :] + bias
                    phi = 0.5 * (1.0 + lax.erf(inner * (0.5**0.5)))
                    density = jnp.exp(-0.5 * inner * inner) * 0.3989422804014327
                    target = pl.ds(pl.multiple_of(base + where.start, 32), where.size)
                    act_s[target, :] = (inner * phi).astype(BF16)
                    rounded = (back_s[where, :] * (phi + inner * density)).astype(BF16)
                    gi_s[target, :] = rounded
                    sums_s[...] += folded(rounded.astype(F32))

                each_rows(together, 32, turn)
            out, gw = outs[at], gw_s.at[at]
            gw[pl.ds(0, width), :] = mm_tn(mid_s[...], gi_s[...]).astype(BF16)
            copies.store(gw.at[pl.ds(0, width)], out.at[pl.ds(0, width)])
            gw[pl.ds(width, width), :] = mm_tn(act_s[...], go_s[...]).astype(BF16)
            tail = jnp.concatenate(
                [jnp.sum(sums_s[...], 0, keepdims=True), jnp.zeros((EXTRA - 1, width), F32)], 0
            )
            gw[pl.ds(2 * width, EXTRA), :] = tail.astype(BF16)
            copies.store(gw.at[pl.ds(width, width + EXTRA)], out.at[pl.ds(width, width + EXTRA)])
        copies.drain()

    square = ((n_j, width, width), BF16)
    return kernel_call(
        body,
        control,
        arrays + list(vecs) + list(w_inner) + list(w_outer) + list(others),
        [((2 * width + EXTRA, width), BF16)] * n_j,
        [
            tall,
            tall,
            tall,
            tall,
            ((16, width), BF16),
            square,
            square,
            wide,
            wide,
            ((n_j, 2 * width + EXTRA, width), BF16),
            ((8, width), F32),
        ],
        1 + 4 * n_j + 2 * count,
        0.01,
        name,
        more=2,
    )


def swapper(sections):
    n = lax.axis_size("dp")

    def swap(value, bit):
        pairs = [(s * n + i, s * n + (i ^ bit)) for s in sections for i in range(n)]
        return lax.ppermute(value, ("section", "dp"), pairs)

    return swap


def fold(control, parts, cuts, name):
    rows, width = parts[0].shape
    piece = rows // cuts
    n_parts = len(parts)

    def body(first, kept, ins, outs, scr, copies):
        total, more = scr[0], scr[1:]
        loads = [copies.load(a, b) for a, b in zip(ins, scr)]
        for load in loads:
            load.wait()

        def add(where):
            value = total[where, :].astype(F32)
            for other in more:
                value = value + other[where, :].astype(F32)
            total[where, :] = value.astype(BF16)

        each_rows(rows, 16, add)
        for i in list(range(1, cuts)) + [0]:
            at = pl.multiple_of((kept ^ i) * piece, 16) if cuts > 1 else 0
            copies.store(total.at[pl.ds(at, piece)], outs[i])
        copies.drain()

    shape = ((rows, width), BF16)
    outs = [((piece, width), BF16)] * cuts
    return kernel_call(body, control, parts, outs, [shape] * n_parts, n_parts + cuts, 0.01, name)


def join(control, parts, name):
    rows, width = parts[0].shape

    def body(first, own, ins, outs, scr, copies):
        loads = []
        for i, source in enumerate(ins):
            spot = pl.ds(pl.multiple_of((own ^ i) * rows, 16), rows)
            loads.append(copies.load(source, scr[0].at[spot]))
        for load in loads:
            load.wait()
        copies.store(scr[0], outs[0])
        copies.drain()

    whole = ((len(parts) * rows, width), BF16)
    return kernel_call(body, control, parts, [whole], [whole], len(parts) + 1, 0.01, name)[0]


def tied(value, *others):
    return lax.optimization_barrier((value, others))[0]


def per_device(
    tokens,
    cotangent,
    task_flags,
    w_query,
    w_key,
    w_value,
    w_attn_out,
    b_query,
    b_value,
    b_attn_out,
    norm1_gain,
    norm1_bias,
    w_inner,
    b_inner,
    w_outer,
    b_outer,
    norm2_gain,
    norm2_bias,
):
    section = lax.axis_index("section")
    stage, core = section // 2, section % 2
    items, seq_len, width = tokens.shape
    words = seq_len - OBJ
    n_visual, n_word = items * OBJ, items * words
    is_first = stage == 0

    def swap_stage(value):
        return lax.ppermute(value, "section", [(0, 2), (1, 3), (2, 0), (3, 1)])

    def swap_core(value):
        return lax.ppermute(value, "section", [(0, 1), (1, 0), (2, 3), (3, 2)])

    flags_far = swap_stage(task_flags)
    tokens_far = swap_stage(tokens)
    attn_w = [w[0] for w in (w_query, w_key, w_value, w_attn_out)]
    vec = jnp.concatenate(
        [
            b_query,
            b_value,
            b_attn_out,
            norm1_gain,
            norm1_bias,
            b_outer,
            norm2_gain,
            norm2_bias,
            b_inner.reshape(BLOCKS, width),
            jnp.zeros((4, width), BF16),
        ],
        0,
    )
    vecs = (vec, swap_core(vec))
    attn_w = [(w, swap_core(w)) for w in attn_w]
    inner_w = (w_inner[0], swap_core(w_inner[0]))
    outer_w = (w_outer[0], swap_core(w_outer[0]))
    cot_far = swap_stage(cotangent)

    flags = task_flags.astype(F32)
    far = flags_far.astype(F32)
    flags = jnp.where(
        is_first, jnp.concatenate([flags, far]), jnp.concatenate([far, flags])
    )
    every = jnp.concatenate([jnp.repeat(flags, OBJ), jnp.repeat(flags, words)])
    flags = jnp.broadcast_to(every[:, None], (every.shape[0], LANES))

    def split(first, second):
        visual = jnp.concatenate([first[:, :OBJ], second[:, :OBJ]], 0)
        word = jnp.concatenate([first[:, OBJ:], second[:, OBJ:]], 0)
        return visual.reshape(2 * n_visual, width), word.reshape(2 * n_word, width)

    place = lax.axis_index("dp")
    side = place % 2
    block = 2 * side + core

    order = []

    def control(at, parity):
        return Control([stage == at, core == parity, block], order)

    even_0, odd_0, even_1, odd_1 = control(0, 0), control(0, 1), control(1, 0), control(1, 1)
    even_any = Control([core >= 0, core == 0, block, stage == 0, place], order)
    odd_late = Control([stage == 1, core == 1, block, stage < 0, place], order)
    blocks_v = [(g * n_visual, n_visual, OBJ, g * n_visual, n_visual, OBJ) for g in (0, 1)]
    blocks_w = [(g * n_word, n_word, words, g * n_word, n_word, words) for g in (0, 1)]
    blocks_x = []
    for g in (0, 1):
        v_at, w_at = g * n_visual, 2 * n_visual + g * n_word
        blocks_x.append((v_at, n_visual, OBJ, w_at, n_word, words))
        blocks_x.append((w_at, n_word, words, v_at, n_visual, OBJ))

    visual_0, word_0 = split(tokens, tokens_far)
    grad_v4, grad_w4 = split(cot_far, cotangent)
    ffn_w = (vecs, inner_w, outer_w)
    weights = (vecs, attn_w, inner_w, outer_w)
    at_word = 2 * n_visual

    kept_0, mid_0, ffn_0, visual_1, kept_1, visual_2, word_2 = first_stage_forward(
        even_0, visual_0, word_0, flags, weights, blocks_v, blocks_x, "s01_f"
    )
    swap_all, swap_early, swap_late = swapper(range(4)), swapper((0, 1)), swapper((2, 3))
    line = []
    while 2 ** (len(line) + 1) < lax.axis_size("dp"):
        line.append(2 ** (len(line) + 1))
    by_size = [2**i for i in reversed(range(len(line) + 1))]
    side_early = by_size[:1] + [1] + by_size[1:-1]

    def spread(value, swap, bits):
        pieces = [value]
        for mask in range(1, lax.axis_size("dp")):
            bit = [bit for bit in bits if mask & bit][-1]
            pieces.append((mask, bit))
        for turn in range(1, len(bits) + 1):
            for mask in range(1, len(pieces)):
                if bin(mask).count("1") == turn:
                    bit = pieces[mask][1]
                    pieces[mask] = swap(pieces[mask ^ bit], bit)
        return pieces

    def turn_of(pieces, turn):
        return [piece for mask, piece in enumerate(pieces) if bin(mask).count("1") == turn]

    def held(pieces, turn, value):
        value, now = lax.optimization_barrier((value, turn_of(pieces, turn)))
        now = iter(now)
        return value, [
            next(now) if bin(mask).count("1") == turn else piece
            for mask, piece in enumerate(pieces)
        ]

    def items_of(visual, word):
        return jnp.concatenate(
            [visual.reshape(items, OBJ, width), word.reshape(items, words, width)], 1
        )

    word_2, visual_2 = swap_stage(word_2), swap_stage(visual_2)
    mids_0 = lax.all_gather(mid_0, "dp", axis=0, tiled=True)
    of_word, of_visual = second_stage(
        odd_1,
        word_2,
        grad_w4,
        visual_2,
        grad_v4,
        flags,
        at_word,
        weights,
        blocks_w,
        blocks_v,
        "s23",
    )
    word_4, pair_3, kept_3, extra_3 = of_word
    visual_4, mid_2, go_2, grad_2, kept_2, extra_2 = of_visual
    pairs = spread(pair_3, swap_late, by_size)
    mids_2 = spread(mid_2, swap_late, side_early)
    grad_2, order[0] = lax.optimization_barrier((swap_stage(grad_2), order[0]))
    odd_c = attn_weight_grads(odd_1, [word_2], None, kept_3, extra_3, None, "s3_attn_w")
    even_c = attn_weight_grads(even_1, [visual_2], None, kept_2, extra_2, None, "s2_attn_w")
    order[0], pairs = held(pairs, 1, order[0])
    rows_v, rows_w = 2 * n_visual, 2 * n_word
    blocks = {"odd": [], "even": []}

    def multiply(key, which):
        if key == "odd":
            block_mids = [(piece, rows_w, 0) for piece in pairs]
            block_gos = [(piece, rows_w, rows_w) for piece in pairs]
        else:
            count = lax.axis_size("dp")
            block_mids = [(mids_0, rows_v, i * rows_v) for i in range(count)]
            block_gos = [(gos, rows_v, i * rows_v) for i in range(count)]
        control, group = (odd_late, 2) if key == "odd" else (even_any, 2)
        name = f"{key}_ffn_w{which[0]}"
        others = mids_2 if key == "even" else ()
        results = None
        for at in range(0, len(block_mids), GROUP):
            some = slice(at, at + GROUP)
            more = ffn_weight_grads(
                control, block_mids[some], block_gos[some], which, group, *ffn_w, name, others[some], at
            )
            results = [a + b for a, b in zip(results, more)] if results else more
        for result in results:
            blocks[key].append((result, swap_core(result)))

    visual_4, grad_2 = lax.optimization_barrier((visual_4, grad_2))
    mixed_own = items_of(visual_4[n_visual:], word_4[n_word:])
    mixed_far = items_of(visual_4[:n_visual], word_4[:n_word])
    back_1, extra_1, grad_w0, go_even, gmid_0, extra_0 = first_stage_back(
        odd_0, grad_2, kept_1, ffn_0, flags, weights, blocks_x, go_2, "s10_b"
    )
    gos = lax.all_gather(go_even, "dp", axis=0, tiled=True)
    order[0], pairs = held(pairs, 2, order[0])
    order[0], mids_2 = held(mids_2, 1, order[0])
    order[0], mids_0 = lax.optimization_barrier((order[0], mids_0))
    odd_c = attn_weight_grads(
        odd_0, [visual_1, word_0], kept_1[3], back_1, extra_1, odd_c, "s1_attn_w"
    )
    odd_c_core = swap_core(odd_c[1])
    n_line = lax.axis_size("dp") // 2
    far_side = place // 2
    at_side = Control([core >= 0, core >= 0, side], order)
    at_line = Control([core >= 0, core >= 0, far_side], order)

    def chain(key, keep, core_far):
        kept, sent = fold(at_side, [keep, core_far], 2, f"{key}_fold_core")
        far = swap_all(sent, 1)
        yield
        kept, *sent = fold(at_line, [kept, far], n_line, f"{key}_fold_side")
        far = [swap_all(part, 2 * (i + 1)) for i, part in enumerate(sent)]
        yield
        kept = fold(at_line, [kept] + far, 1, f"{key}_fold_line")[0]
        far = [swap_all(kept, 2 * (i + 1)) for i in range(n_line - 1)]
        yield
        kept = join(at_line, [kept] + far, f"{key}_join_line")
        far = swap_all(kept, 1)
        yield
        yield join(at_side, [kept, far], f"{key}_join_side")

    chains = {"co": chain("odd", odd_c[0], odd_c_core)}
    next(chains["co"])
    grad_v0, back_0, extra_0 = first_section_back(
        even_0, gmid_0, kept_0, flags, weights, extra_0, blocks_v, "s0_b"
    )
    order[0], pairs = held(pairs, 3, order[0])
    multiply("odd", (0, 1))
    even_c = attn_weight_grads(
        even_0, [visual_0], kept_0[3], back_0, extra_0, even_c, "s0_attn_w"
    )
    chains["ce"] = chain("even", even_c[0], swap_core(even_c[1]))
    multiply("odd", (2, 3))
    control_end = Control([core >= 0, core >= 0, block, core, section == 1], order)
    ffn_out, far_grad = None, None
    sums = {}
    for item in PLAN:
        if item in chains:
            sums[item] = next(chains[item])
        elif item[0] == "m":
            order[0], mids_2 = held(mids_2, int(item[1]), order[0])
        elif item == "end":
            grad_far = items_of(grad_v0[n_visual:], grad_w0[n_word:])
            mixed_far, grad_far, order[0] = lax.optimization_barrier(
                (mixed_far, grad_far, order[0])
            )
            mixed_far, grad_far = swap_stage(mixed_far), swap_stage(grad_far)
            odd_c_far = swap_core(sums["co"])
            ffn_out = assemble_ffn(control_end, blocks["even"], blocks["odd"], "ffn_out")
            order[0], mixed_far, grad_far, odd_c_far = lax.optimization_barrier(
                (order[0], mixed_far, grad_far, odd_c_far)
            )
        else:
            multiply("even", tuple(int(j) for j in item[1:]))
    grad_inner, grad_outer, inner_bias = ffn_out
    odd_c, even_c = sums["co"], sums["ce"]
    *square, small = assemble_attn(
        control_end, [even_c, swap_core(even_c)], [odd_c, odd_c_far], "attn_out"
    )
    mixed = jnp.where(is_first, mixed_far, mixed_own)
    tokens_grad = jnp.where(is_first, items_of(grad_v0[:n_visual], grad_w0[:n_word]), grad_far)
    return (
        mixed,
        tokens_grad,
        square[0][None],
        square[1][None],
        square[2][None],
        square[3][None],
        small[0:1],
        small[1:2],
        small[2:3],
        small[3:4],
        small[4:5],
        grad_inner[None],
        inner_bias[:BLOCKS].reshape(1, BLOCKS * width),
        grad_outer[None],
        small[10:11],
        small[8:9],
        small[9:10],
    )


def solution(mesh):
    tokens = P(("section", "dp"), None, None)
    matrix = P("section", None, None)
    vector = P("section", None)
    placed = (
        (tokens, tokens, P(("section", "dp")))
        + (matrix,) * 4
        + (vector,) * 5
        + (matrix, vector, matrix)
        + (vector,) * 3
    )
    return jax.shard_map(
        per_device,
        mesh=mesh,
        in_specs=placed,
        out_specs=(tokens, tokens)
        + (matrix,) * 4
        + (vector,) * 5
        + (matrix, vector, matrix)
        + (vector,) * 3,
        check_vma=False,
    )
```

time: 653 us -> 567 us (0.87)
  the two profiles are of different devices: /device:TPU:30 before, /device:TPU:13 now
where the time goes in v2:
time: 567 us; the launch traced here: 556 us
  Pallas kernels  265 us (47%)
  starting transfers between devices  121 us (21%)
  waiting for transfers between devices  108 us (19%)
  local copies, waits for them, and re-layouts  33.6 us (6%)
  between operations  15.3 us (3%)
  other arithmetic  12.3 us (2%)
    pallas_call x24, Pallas kernels, kernel_call(): pl.pallas_call(kernel, out_shape=[jax.ShapeDtypeStruct(shape, kind) for s...  265 us
    ppermute x30, waiting for transfers between devices, swap(): return lax.ppermute(value, ('section', 'dp'), pairs)  83.4 us
    ppermute x30, starting transfers between devices, swap(): return lax.ppermute(value, ('section', 'dp'), pairs)  67.5 us
    ppermute x8, starting transfers between devices, swap_stage(): return lax.ppermute(value, 'section', [(0, 2), (1, 3), (2, 0), (3, 1)])  29.9 us
    ppermute x19, starting transfers between devices, swap_core(): return lax.ppermute(value, 'section', [(0, 1), (1, 0), (2, 3), (3, 2)])  24 us
    ppermute x8, waiting for transfers between devices, swap_stage(): return lax.ppermute(value, 'section', [(0, 2), (1, 3), (2, 0), (3, 1)])  16.1 us
  transfers between devices with their start and end apart: 59, of which 18 were waited for; matrix products, arithmetic and copies ran while one was open for 6% of the time, Pallas kernels for 46%

profile of v2, /device:TPU:13, one launch (start us, length us, event | category | flops | bytes accessed | tf_op | source)
XLA Modules:
  0.0 555.7 jit_solution(10762809376470279413)
XLA Ops:
  11.6 6.7 %collective-permute-done.1 = s32[4]{0:T(128)S(1)} collective-permute-done((s32[4]{0:T(128)}, s32[4]{0:T(128)S(1)}, u32[]{:S(2)}, u32[]{:S(2)}) %collective-permute-start.1) | collective-permute-done | bytes 48 | tf_op jit(solution)/shard_map/ppermute | solution.py:1125
  19.3 4.7 collective-permute-done.2.refs_4_.refs_6_.refs_14_.refs_11_.refs_17_
  26.3 1.7 slice.75
  31.7 1.8 pad_maximum_fusion
  33.4 1.9 reshape.83.refs_0_
  36.3 1.7 pad_maximum_fusion.4
  38.0 1.7 reshape.84.refs_1_
  42.9 26.6 %collective-permute-start.11 = (bf16[288,768]{1,0:T(8,128)(2,1)}, bf16[288,768]{1,0:T(8,128)(2,1)S(1)}, u32[]{:S(2)}, u32[]{:S(2)}) collective-permute-start(bf16[288,768]{1,0:T(8,128)(2,1)} %get-tuple-element.157), channel_id=1, source_target_pairs={{0,16},{8,24},{16,0},{24,8},{1,17},{9,25},{17,1},{25,9},{2,18},{10... | collective-permute-start | bytes 1327112 | tf_op jit(solution)/shard_map/ppermute | solution.py:1125
  75.7 9.3 %collective-permute-done.9.refs_0_ = bf16[160,768]{1,0:T(8,128)(2,1)S(1)} collective-permute-done((bf16[160,768]{1,0:T(8,128)(2,1)}, bf16[160,768]{1,0:T(8,128)(2,1)S(1)}, u32[]{:S(2)}, u32[]{:S(2)}) %collective-permute-start.9) | collective-permute-done | bytes 245792 | tf_op jit(solution)/shard_map/ppermute | solution.py:1125
  85.9 53.8 %s23.1 = (bf16[160,768]{1,0:T(8,128)(2,1)}, bf16[320,768]{1,0:T(8,128)(2,1)}, bf16[5,160,768]{2,1,0:T(8,128)(2,1)}, f32[16,768]{1,0:T(8,128)}, bf16[288,768]{1,0...) custom-call(s32[3]{0:T(128)} %get-tuple-element.312.control_ref, ...), custom_call_target="tpu_custom_call" | custom-call | flops 69000003584 | tf_op jit(solution)/shard_map/s23/pallas_call | solution.py:128
  139.8 2.1 collective-permute-start.14
  141.9 3.1 collective-permute-start.13
  145.1 4.2 collective-permute-start.15
  149.2 7.8 %collective-permute-done.14.refs_2_.refs_10_ = bf16[320,768]{1,0:T(8,128)(2,1)S(1)} collective-permute-done((bf16[320,768]{1,0:T(8,128)(2,1)}, bf16[320,768]{1,0:T(8,128)(2,1)S(1)}, u32[]{:S(2)}, u32[]{:S(2)}) %collective-permute-start.14) | collective-permute-done | bytes 491552 | tf_op jit(solution)/shard_map/ppermute | solution.py:1043
  157.1 4.2 collective-permute-start.16
  161.9 1.9 collective-permute-start.19
  163.9 4.0 collective-permute-start.20
  167.9 6.7 %s3_attn_w.1 = (bf16[1664,768]{1,0:T(8,128)(2,1)}, bf16[1664,768]{1,0:T(8,128)(2,1)}, f32[8,128]{1,0:T(8,128)}) custom-call(s32[3]{0:T(128)} %get-tuple-element.312.control_ref, bf16[160,768]{1,0:T(8,128)(2,1)} %copy-done.38, bf16[5,160,768]{2,1,0:T(8,128)(2,1)} %get-tuple-element.178.refs_1_, f32[16,768]{1,0:T(8,128)} %get-tuple-element.179.refs_2_, ...), custom_call_target="tpu_custom_call" | custom-call | flops 2300000000 | tf_op jit(solution)/shard_map/s3_attn_w/pallas_call | solution.py:128
  174.6 8.5 %s2_attn_w.1 = (bf16[1664,768]{1,0:T(8,128)(2,1)}, bf16[1664,768]{1,0:T(8,128)(2,1)}, f32[8,128]{1,0:T(8,128)}) custom-call(s32[3]{0:T(128)} %add_add_fusion.3.control_ref, bf16[288,768]{1,0:T(8,128)(2,1)} %copy-done.37, bf16[5,288,768]{2,1,0:T(8,128)(2,1)} %get-tuple-element.176.refs_1_, f32[16,768]{1,0:T(8,128)} %get-tuple-element.177.refs_2_, ...), custom_call_target="tpu_custom_call" | custom-call | flops 2300000000 | tf_op jit(solution)/shard_map/s2_attn_w/pallas_call | solution.py:128
  183.1 2.8 collective-permute-start.21
  186.0 3.4 collective-permute-start.17
  189.4 3.4 collective-permute-start.18
  194.1 4.1 collective-permute-done.17.refs_5_.refs_13_
  198.2 11.3 %collective-permute-done.18.refs_6_.refs_14_ = bf16[320,768]{1,0:T(8,128)(2,1)S(1)} collective-permute-done((bf16[320,768]{1,0:T(8,128)(2,1)S(1)}, bf16[320,768]{1,0:T(8,128)(2,1)S(1)}, u32[]{:S(2)}, u32[]{:S(2)}) %collective-permute-start.18) | collective-permute-done | bytes 491552 | tf_op jit(solution)/shard_map/ppermute | solution.py:1043
  210.6 3.0 collective-permute-start.22
  213.6 1.9 collective-permute-start.23
  219.7 6.2 %odd_fold_core.1 = (bf16[832,768]{1,0:T(8,128)(2,1)}, bf16[832,768]{1,0:T(8,128)(2,1)}, f32[8,128]{1,0:T(8,128)}) custom-call(s32[3]{0:T(128)} %pad_add_fusion.control_ref, bf16[1664,768]{1,0:T(8,128)(2,1)} %get-tuple-element.215.refs_0_, bf16[1664,768]{1,0:T(8,128)(2,1)} %copy-done.11, f32[8,128]{1,0:T(8,128)} %get-tuple-element.217.refs_2_), custom_call_target="tpu_custom_call" | custom-call | flops 11500000 | tf_op jit(solution)/shard_map/odd_fold_core/pallas_call | solution.py:128
  226.7 5.6 %collective-permute-done.23.refs_7_.refs_15_ = bf16[320,768]{1,0:T(8,128)(2,1)S(1)} collective-permute-done((bf16[320,768]{1,0:T(8,128)(2,1)S(1)}, bf16[320,768]{1,0:T(8,128)(2,1)S(1)}, u32[]{:S(2)}, u32[]{:S(2)}) %collective-permute-start.23) | collective-permute-done | bytes 491552 | tf_op jit(solution)/shard_map/ppermute | solution.py:1043
  233.1 24.4 %odd_ffn_w0.1 = (bf16[1568,768]{1,0:T(8,128)(2,1)}, bf16[1568,768]{1,0:T(8,128)(2,1)}, f32[8,128]{1,0:T(8,128)}) custom-call(s32[5]{0:T(128)} %stack.128.control_ref, bf16[320,768]{1,0:T(8,128)(2,1)} %get-tuple-element.183.refs_0_.refs_8_, bf16[320,768]{1,0:T(8,128)(2,1)} %copy-done.1, bf16[320,768]{1,0:T(8,128)(2,1)} %copy-done, ...), custom_call_target="tpu_custom_call" | custom-call | flops 11500000 | tf_op jit(solution)/shard_map/odd_ffn_w0/pallas_call | solution.py:128
  260.1 3.9 collective-permute-start.24
  264.0 1.9 collective-permute-start.25
  265.9 1.9 collective-permute-start.26
  269.4 24.1 %odd_ffn_w2.1 = (bf16[1568,768]{1,0:T(8,128)(2,1)}, bf16[1568,768]{1,0:T(8,128)(2,1)}, f32[8,128]{1,0:T(8,128)}) custom-call(s32[5]{0:T(128)} %stack.128.control_ref, bf16[320,768]{1,0:T(8,128)(2,1)} %get-tuple-element.183.refs_0_.refs_8_, bf16[320,768]{1,0:T(8,128)(2,1)} %copy-done.1, bf16[320,768]{1,0:T(8,128)(2,1)} %copy-done, ...), custom_call_target="tpu_custom_call" | custom-call | flops 11500000 | tf_op jit(solution)/shard_map/odd_ffn_w2/pallas_call | solution.py:128
  293.5 2.4 collective-permute-done.26.refs_28_
  297.4 5.9 %even_fold_core.1 = (bf16[832,768]{1,0:T(8,128)(2,1)}, bf16[832,768]{1,0:T(8,128)(2,1)}, f32[8,128]{1,0:T(8,128)}) custom-call(s32[3]{0:T(128)} %pad_add_fusion.control_ref, bf16[1664,768]{1,0:T(8,128)(2,1)} %get-tuple-element.233.refs_0_, bf16[1664,768]{1,0:T(8,128)(2,1)} %copy-done.10, f32[8,128]{1,0:T(8,128)} %get-tuple-element.235.refs_2_), custom_call_target="tpu_custom_call" | custom-call | flops 11500000 | tf_op jit(solution)/shard_map/even_fold_core/pallas_call | solution.py:128
  305.0 3.1 collective-permute-start.30
  308.7 4.1 odd_fold_side.1
  313.1 2.1 collective-permute-start.34
  315.3 17.7 %collective-permute-done.28.refs_1_ = bf16[832,768]{1,0:T(8,128)(2,1)S(1)} collective-permute-done((bf16[832,768]{1,0:T(8,128)(2,1)}, bf16[832,768]{1,0:T(8,128)(2,1)S(1)}, u32[]{:S(2)}, u32[]{:S(2)}) %collective-permute-start.28) | collective-permute-done | bytes 1277984 | tf_op jit(solution)/shard_map/ppermute | solution.py:1043
  332.9 1.7 collective-permute-start.35
  334.6 4.1 even_fold_side.1
  342.2 41.8 %even_ffn_w0.1 = (bf16[1568,768]{1,0:T(8,128)(2,1)}, bf16[1568,768]{1,0:T(8,128)(2,1)}, f32[8,128]{1,0:T(8,128)}) custom-call(s32[5]{0:T(128)} %stack.117.control_ref, bf16[2304,768]{1,0:T(8,128)(2,1)} %all-gather.3.cloned.1.call-done.refs_0_.refs_1_.refs_2_.refs_3_.refs_4_.refs_5_.refs_6_.refs_7_, ...), custom_call_target="tpu_custom_call" | custom-call | flops 11500000 | tf_op jit(solution)/shard_map/even_ffn_w0/pallas_call | solution.py:128
  384.0 3.1 odd_fold_line.1
  390.2 2.7 collective-permute-start.50
  393.0 2.9 even_fold_line.1
  395.9 1.7 collective-permute-start.42
  397.6 3.8 collective-permute-done.36.refs_1_
  401.4 2.8 collective-permute-start.43
  404.2 4.5 collective-permute-start.47
  408.7 4.0 collective-permute-done.42.refs_1_
  412.7 3.0 collective-permute-start.48
  416.9 11.4 %collective-permute-done.44.refs_3_ = bf16[208,768]{1,0:T(8,128)(2,1)} collective-permute-done((bf16[208,768]{1,0:T(8,128)(2,1)}, bf16[208,768]{1,0:T(8,128)(2,1)}, u32[]{:S(2)}, u32[]{:S(2)}) %collective-permute-start.44) | collective-permute-done | bytes 319520 | tf_op jit(solution)/shard_map/ppermute | solution.py:1043
  428.3 3.0 even_join_line.1
  431.3 9.8 %collective-permute-done.38.refs_3_ = bf16[208,768]{1,0:T(8,128)(2,1)S(1)} collective-permute-done((bf16[208,768]{1,0:T(8,128)(2,1)}, bf16[208,768]{1,0:T(8,128)(2,1)S(1)}, u32[]{:S(2)}, u32[]{:S(2)}) %collective-permute-start.38) | collective-permute-done | bytes 319520 | tf_op jit(solution)/shard_map/ppermute | solution.py:1043
  441.8 3.0 odd_join_line.1
  444.8 8.0 %collective-permute-start.51 = (bf16[832,768]{1,0:T(8,128)(2,1)}, bf16[832,768]{1,0:T(8,128)(2,1)S(1)}, u32[]{:S(2)}, u32[]{:S(2)}) collective-permute-start(bf16[832,768]{1,0:T(8,128)(2,1)} %get-tuple-element.272.refs_0_), channel_id=1, source_target_pairs={{0,1},{1,0},{2,3},{3,2},{4,5},{5,4},{6,7},{7,6},{8,9},{9,8},{10,11... | collective-permute-start | bytes 3833864 | tf_op jit(solution)/shard_map/ppermute | solution.py:1043
  452.8 2.7 collective-permute-start.31
  455.5 38.9 %even_ffn_w2.1 = (bf16[1568,768]{1,0:T(8,128)(2,1)}, bf16[1568,768]{1,0:T(8,128)(2,1)}, f32[8,128]{1,0:T(8,128)}) custom-call(s32[5]{0:T(128)} %stack.117.control_ref, bf16[2304,768]{1,0:T(8,128)(2,1)} %all-gather.3.cloned.1.call-done.refs_0_.refs_1_.refs_2_.refs_3_.refs_4_.refs_5_.refs_6_.refs_7_, ...), custom_call_target="tpu_custom_call" | custom-call | flops 11500000 | tf_op jit(solution)/shard_map/even_ffn_w2/pallas_call | solution.py:128
  495.6 3.8 odd_join_side.1
  511.2 14.4 %ffn_out.1 = (f32[768,3072]{1,0:T(8,128)}, f32[3072,768]{1,0:T(8,128)}, f32[8,768]{1,0:T(8,128)}, f32[8,128]{1,0:T(8,128)}) custom-call(s32[5]{0:T(128)} %stack.111.control_ref, bf16[1568,768]{1,0:T(8,128)(2,1)} %get-tuple-element.245.refs_0_, bf16[1568,768]{1,0:T(8,128)(2,1)} %collective-permute-done.31.refs_1_, ...), custom_call_target="tpu_custom_call" | custom-call | flops 11500000 | tf_op jit(solution)/shard_map/ffn_out/pallas_call | solution.py:128
  525.7 4.7 collective-permute-done.55.refs_1_
  530.4 3.9 even_join_side.1
  536.5 1.8 maximum_select_fusion.1
  540.4 6.6 %attn_out.1 = (f32[768,768]{1,0:T(8,128)}, f32[768,768]{1,0:T(8,128)}, f32[768,768]{1,0:T(8,128)}, f32[768,768]{1,0:T(8,128)}, f32[256,768]{1,0:T(8,128)}, /*index=5*/f32[8,128]{1,0:T(8,128)}) custom-call(s32[5]{0:T(128)} %stack.111.control_ref, bf16[1664,768]{1,0:T(8,128)(2,1)} %get-tuple-element.284.refs_0_, ...), custom_call_target="tpu_custom_call" | custom-call | flops 8049999872 | tf_op jit(solution)/shard_map/attn_out/pallas_call | solution.py:128
  (214 shorter events, 66.7 us)
Async XLA Ops:
  7.2 202.4 %all-gather.3.cloned.1.call-start = ((), (), s32[]{:S(2)}) async-start(), calls=%async_computation | async-start | bytes 3981312 | tf_op jit(solution)/shard_map/all_gather | solution.py:1232
  7.2 32.7 %collective-permute-start.7 = (bf16[768,3072]{1,0:T(8,128)(2,1)}, bf16[768,3072]{1,0:T(8,128)(2,1)}, u32[]{:S(2)}, u32[]{:S(2)}) collective-permute-start(bf16[768,3072]{1,0:T(8,128)(2,1)} %bitcast.28), channel_id=1, source_target_pairs={{0,8},{8,0},{16,24},{24,16},{1,9},{9,1},{17,25},{25,17},{2,10},{10... | collective-permute-start | bytes 14155784 | tf_op jit(solution)/shard_map/ppermute | solution.py:1128
  8.0 31.9 %collective-permute-start.8 = (bf16[3072,768]{1,0:T(8,128)(2,1)}, bf16[3072,768]{1,0:T(8,128)(2,1)}, u32[]{:S(2)}, u32[]{:S(2)}) collective-permute-start(bf16[3072,768]{1,0:T(8,128)(2,1)} %bitcast.36), channel_id=1, source_target_pairs={{0,8},{8,0},{16,24},{24,16},{1,9},{9,1},{17,25},{25,17},{2,10},{10... | collective-permute-start | bytes 14155784 | tf_op jit(solution)/shard_map/ppermute | solution.py:1128
  8.1 17.2 %collective-permute-start.3 = (bf16[768,768]{1,0:T(8,128)(2,1)}, bf16[768,768]{1,0:T(8,128)(2,1)S(1)}, u32[]{:S(2)}, u32[]{:S(2)}) collective-permute-start(bf16[768,768]{1,0:T(8,128)(2,1)} %bitcast.44), channel_id=1, source_target_pairs={{0,8},{8,0},{16,24},{24,16},{1,9},{9,1},{17,25},{25,17},{2,10},{10... | collective-permute-start | bytes 3538952 | tf_op jit(solution)/shard_map/ppermute | solution.py:1128
  8.5 15.9 %collective-permute-start = (bf16[4,56,768]{2,1,0:T(8,128)(2,1)}, bf16[4,56,768]{2,1,0:T(8,128)(2,1)S(1)}, u32[]{:S(2)}, u32[]{:S(2)}) collective-permute-start(bf16[4,56,768]{2,1,0:T(8,128)(2,1)} %param.18), channel_id=1, source_target_pairs={{0,16},{8,24},{16,0},{24,8},{1,17},{9,25},{17,1},{25,9},{2,18},{10... | collective-permute-start | bytes 1032200 | tf_op jit(solution)/shard_map/ppermute | solution.py:1125
  8.7 9.6 %collective-permute-start.1 = (s32[4]{0:T(128)}, s32[4]{0:T(128)S(1)}, u32[]{:S(2)}, u32[]{:S(2)}) collective-permute-start(s32[4]{0:T(128)} %param.20), channel_id=1, source_target_pairs={{0,16},{8,24},{16,0},{24,8},{1,17},{9,25},{17,1},{25,9},{2,18},{10... | collective-permute-start | bytes 56 | tf_op jit(solution)/shard_map/ppermute | solution.py:1125
  18.3 5.7 %collective-permute-start.2 = (bf16[16,768]{1,0:T(8,128)(2,1)S(1)}, bf16[16,768]{1,0:T(8,128)(2,1)S(1)}, u32[]{:S(2)}, u32[]{:S(2)}) collective-permute-start(bf16[16,768]{1,0:T(8,128)(2,1)S(1)} %concatenate.41.refs_3_.refs_5_.refs_13_.refs_10_.refs_16_), channel_id=1, source_target_pairs={{0,8},{8,0},{16,24},{24,16},{1,9},{9,1},{17,25},{25,17},{2,10},{10... | collective-permute-start | bytes 73736 | tf_op jit(solution)/shard_map/ppermute | solution.py:1128
  24.0 15.7 %collective-permute-start.4 = (bf16[768,768]{1,0:T(8,128)(2,1)}, bf16[768,768]{1,0:T(8,128)(2,1)S(1)}, u32[]{:S(2)}, u32[]{:S(2)}) collective-permute-start(bf16[768,768]{1,0:T(8,128)(2,1)} %bitcast.49), channel_id=1, source_target_pairs={{0,8},{8,0},{16,24},{24,16},{1,9},{9,1},{17,25},{25,17},{2,10},{10... | collective-permute-start | bytes 3538952 | tf_op jit(solution)/shard_map/ppermute | solution.py:1128
  25.1 14.8 %collective-permute-start.5 = (bf16[768,768]{1,0:T(8,128)(2,1)}, bf16[768,768]{1,0:T(8,128)(2,1)S(1)}, u32[]{:S(2)}, u32[]{:S(2)}) collective-permute-start(bf16[768,768]{1,0:T(8,128)(2,1)} %bitcast.54), channel_id=1, source_target_pairs={{0,8},{8,0},{16,24},{24,16},{1,9},{9,1},{17,25},{25,17},{2,10},{10... | collective-permute-start | bytes 3538952 | tf_op jit(solution)/shard_map/ppermute | solution.py:1128
  25.2 14.7 %collective-permute-start.6 = (bf16[768,768]{1,0:T(8,128)(2,1)}, bf16[768,768]{1,0:T(8,128)(2,1)}, u32[]{:S(2)}, u32[]{:S(2)}) collective-permute-start(bf16[768,768]{1,0:T(8,128)(2,1)} %bitcast.59), channel_id=1, source_target_pairs={{0,8},{8,0},{16,24},{24,16},{1,9},{9,1},{17,25},{25,17},{2,10},{10... | collective-permute-start | bytes 3538952 | tf_op jit(solution)/shard_map/ppermute | solution.py:1128
  39.7 32.4 %collective-permute-start.10 = (bf16[4,56,768]{2,1,0:T(8,128)(2,1)}, bf16[4,56,768]{2,1,0:T(8,128)(2,1)}, u32[]{:S(2)}, u32[]{:S(2)}) collective-permute-start(bf16[4,56,768]{2,1,0:T(8,128)(2,1)} %param.19), channel_id=1, source_target_pairs={{0,16},{8,24},{16,0},{24,8},{1,17},{9,25},{17,1},{25,9},{2,18},{10... | collective-permute-start | bytes 1032200 | tf_op jit(solution)/shard_map/ppermute | solution.py:1125
  42.9 42.2 %collective-permute-start.11 = (bf16[288,768]{1,0:T(8,128)(2,1)}, bf16[288,768]{1,0:T(8,128)(2,1)S(1)}, u32[]{:S(2)}, u32[]{:S(2)}) collective-permute-start(bf16[288,768]{1,0:T(8,128)(2,1)} %get-tuple-element.157), channel_id=1, source_target_pairs={{0,16},{8,24},{16,0},{24,8},{1,17},{9,25},{17,1},{25,9},{2,18},{10... | collective-permute-start | bytes 1327112 | tf_op jit(solution)/shard_map/ppermute | solution.py:1125
  69.4 15.6 %collective-permute-start.9 = (bf16[160,768]{1,0:T(8,128)(2,1)}, bf16[160,768]{1,0:T(8,128)(2,1)S(1)}, u32[]{:S(2)}, u32[]{:S(2)}) collective-permute-start(bf16[160,768]{1,0:T(8,128)(2,1)} %get-tuple-element.156), channel_id=1, source_target_pairs={{0,16},{8,24},{16,0},{24,8},{1,17},{9,25},{17,1},{25,9},{2,18},{10... | collective-permute-start | bytes 737288 | tf_op jit(solution)/shard_map/ppermute | solution.py:1125
  75.7 266.4 %all-gather.5.cloned.1.call-start = ((), (), s32[]{:S(2)}) async-start(), calls=%async_computation.1 | async-start | bytes 3981312 | tf_op jit(solution)/shard_map/all_gather | solution.py:1284
  139.7 24.1 %collective-permute-start.12 = (bf16[448,768]{1,0:T(8,128)(2,1)}, bf16[448,768]{1,0:T(8,128)(2,1)S(1)}, u32[]{:S(2)}, u32[]{:S(2)}) collective-permute-start(bf16[448,768]{1,0:T(8,128)(2,1)} %get-tuple-element.160), channel_id=1, source_target_pairs={{0,16},{8,24},{16,0},{24,8},{1,17},{9,25},{17,1},{25,9},{2,18},{10... | collective-permute-start | bytes 2064392 | tf_op jit(solution)/shard_map/ppermute | solution.py:1125
  139.8 17.2 %collective-permute-start.14 = (bf16[320,768]{1,0:T(8,128)(2,1)}, bf16[320,768]{1,0:T(8,128)(2,1)S(1)}, u32[]{:S(2)}, u32[]{:S(2)}) collective-permute-start(bf16[320,768]{1,0:T(8,128)(2,1)} %get-tuple-element.183.refs_0_.refs_8_), channel_id=1, source_target_pairs={{16,18},{17,19},{18,16},{19,17},{20,22},{21,23},{22,20},{23,21},{2... | collective-permute-start | bytes 1474568 | tf_op jit(solution)/shard_map/ppermute | solution.py:1043
  141.9 41.2 %collective-permute-start.13 = (bf16[320,768]{1,0:T(8,128)(2,1)}, bf16[320,768]{1,0:T(8,128)(2,1)S(1)}, u32[]{:S(2)}, u32[]{:S(2)}) collective-permute-start(bf16[320,768]{1,0:T(8,128)(2,1)} %get-tuple-element.183.refs_0_.refs_8_), channel_id=1, source_target_pairs={{16,17},{17,16},{18,19},{19,18},{20,21},{21,20},{22,23},{23,22},{2... | collective-permute-start | bytes 1474568 | tf_op jit(solution)/shard_map/ppermute | solution.py:1043
  145.1 40.9 %collective-permute-start.15 = (bf16[320,768]{1,0:T(8,128)(2,1)}, bf16[320,768]{1,0:T(8,128)(2,1)S(1)}, u32[]{:S(2)}, u32[]{:S(2)}) collective-permute-start(bf16[320,768]{1,0:T(8,128)(2,1)} %get-tuple-element.183.refs_0_.refs_8_), channel_id=1, source_target_pairs={{16,20},{17,21},{18,22},{19,23},{20,16},{21,17},{22,18},{23,19},{2... | collective-permute-start | bytes 1474568 | tf_op jit(solution)/shard_map/ppermute | solution.py:1043
  157.1 32.3 %collective-permute-start.16 = (bf16[320,768]{1,0:T(8,128)(2,1)S(1)}, bf16[320,768]{1,0:T(8,128)(2,1)S(1)}, u32[]{:S(2)}, u32[]{:S(2)}) collective-permute-start(bf16[320,768]{1,0:T(8,128)(2,1)S(1)} %collective-permute-done.14.refs_2_.refs_10_), channel_id=1, source_target_pairs={{16,17},{17,16},{18,19},{19,18},{20,21},{21,20},{22,23},{23,22},{2... | collective-permute-start | bytes 1474568 | tf_op jit(solution)/shard_map/ppermute | solution.py:1043
  161.9 47.6 %collective-permute-start.19 = (bf16[288,768]{1,0:T(8,128)(2,1)}, bf16[288,768]{1,0:T(8,128)(2,1)S(1)}, u32[]{:S(2)}, u32[]{:S(2)}) collective-permute-start(bf16[288,768]{1,0:T(8,128)(2,1)} %get-tuple-element.187.refs_22_), channel_id=1, source_target_pairs={{16,17},{17,16},{18,19},{19,18},{20,21},{21,20},{22,23},{23,22},{2... | collective-permute-start | bytes 1327112 | tf_op jit(solution)/shard_map/ppermute | solution.py:1043
  163.9 45.7 %collective-permute-start.20 = (bf16[288,768]{1,0:T(8,128)(2,1)}, bf16[288,768]{1,0:T(8,128)(2,1)S(1)}, u32[]{:S(2)}, u32[]{:S(2)}) collective-permute-start(bf16[288,768]{1,0:T(8,128)(2,1)} %get-tuple-element.187.refs_22_), channel_id=1, source_target_pairs={{16,18},{17,19},{18,16},{19,17},{20,22},{21,23},{22,20},{23,21},{2... | collective-permute-start | bytes 1327112 | tf_op jit(solution)/shard_map/ppermute | solution.py:1043
  183.1 26.4 %collective-permute-start.21 = (bf16[288,768]{1,0:T(8,128)(2,1)S(1)}, bf16[288,768]{1,0:T(8,128)(2,1)}, u32[]{:S(2)}, u32[]{:S(2)}) collective-permute-start(bf16[288,768]{1,0:T(8,128)(2,1)S(1)} %copy-done.14), channel_id=1, source_target_pairs={{16,20},{17,21},{18,22},{19,23},{20,16},{21,17},{22,18},{23,19},{2... | collective-permute-start | bytes 1327112 | tf_op jit(solution)/shard_map/ppermute | solution.py:1043
  186.0 12.2 %collective-permute-start.17 = (bf16[320,768]{1,0:T(8,128)(2,1)S(1)}, bf16[320,768]{1,0:T(8,128)(2,1)S(1)}, u32[]{:S(2)}, u32[]{:S(2)}) collective-permute-start(bf16[320,768]{1,0:T(8,128)(2,1)S(1)} %collective-permute-done.15.refs_4_.refs_12_), channel_id=1, source_target_pairs={{16,17},{17,16},{18,19},{19,18},{20,21},{21,20},{22,23},{23,22},{2... | collective-permute-start | bytes 1474568 | tf_op jit(solution)/shard_map/ppermute | solution.py:1043
  189.4 20.1 %collective-permute-start.18 = (bf16[320,768]{1,0:T(8,128)(2,1)S(1)}, bf16[320,768]{1,0:T(8,128)(2,1)S(1)}, u32[]{:S(2)}, u32[]{:S(2)}) collective-permute-start(bf16[320,768]{1,0:T(8,128)(2,1)S(1)} %collective-permute-done.15.refs_4_.refs_12_), channel_id=1, source_target_pairs={{16,18},{17,19},{18,16},{19,17},{20,22},{21,23},{22,20},{23,21},{2... | collective-permute-start | bytes 1474568 | tf_op jit(solution)/shard_map/ppermute | solution.py:1043
  210.6 7.6 %collective-permute-start.22 = (bf16[1664,768]{1,0:T(8,128)(2,1)}, bf16[1664,768]{1,0:T(8,128)(2,1)S(1)}, u32[]{:S(2)}, u32[]{:S(2)}) collective-permute-start(bf16[1664,768]{1,0:T(8,128)(2,1)} %get-tuple-element.216), channel_id=1, source_target_pairs={{0,8},{8,0},{16,24},{24,16},{1,9},{9,1},{17,25},{25,17},{2,10},{10... | collective-permute-start | bytes 7667720 | tf_op jit(solution)/shard_map/ppermute | solution.py:1128
  213.6 18.8 %collective-permute-start.23 = (bf16[320,768]{1,0:T(8,128)(2,1)S(1)}, bf16[320,768]{1,0:T(8,128)(2,1)S(1)}, u32[]{:S(2)}, u32[]{:S(2)}) collective-permute-start(bf16[320,768]{1,0:T(8,128)(2,1)S(1)} %collective-permute-done.18.refs_6_.refs_14_), channel_id=1, source_target_pairs={{16,17},{17,16},{18,19},{19,18},{20,21},{21,20},{22,23},{23,22},{2... | collective-permute-start | bytes 1474568 | tf_op jit(solution)/shard_map/ppermute | solution.py:1043
  258.5 37.5 %collective-permute-start.27 = (bf16[1664,768]{1,0:T(8,128)(2,1)}, bf16[1664,768]{1,0:T(8,128)(2,1)S(1)}, u32[]{:S(2)}, u32[]{:S(2)}) collective-permute-start(bf16[1664,768]{1,0:T(8,128)(2,1)} %get-tuple-element.234), channel_id=1, source_target_pairs={{0,8},{8,0},{16,24},{24,16},{1,9},{9,1},{17,25},{25,17},{2,10},{10... | collective-permute-start | bytes 7667720 | tf_op jit(solution)/shard_map/ppermute | solution.py:1128
  260.1 33.4 %collective-permute-start.24 = (bf16[288,768]{1,0:T(8,128)(2,1)S(1)}, bf16[288,768]{1,0:T(8,128)(2,1)S(1)}, u32[]{:S(2)}, u32[]{:S(2)}) collective-permute-start(bf16[288,768]{1,0:T(8,128)(2,1)S(1)} %copy-done.16), channel_id=1, source_target_pairs={{16,18},{17,19},{18,16},{19,17},{20,22},{21,23},{22,20},{23,21},{2... | collective-permute-start | bytes 1327112 | tf_op jit(solution)/shard_map/ppermute | solution.py:1043
  264.0 29.5 %collective-permute-start.25 = (bf16[288,768]{1,0:T(8,128)(2,1)}, bf16[288,768]{1,0:T(8,128)(2,1)S(1)}, u32[]{:S(2)}, u32[]{:S(2)}) collective-permute-start(bf16[288,768]{1,0:T(8,128)(2,1)} %collective-permute-done.21.refs_26_), channel_id=1, source_target_pairs={{16,17},{17,16},{18,19},{19,18},{20,21},{21,20},{22,23},{23,22},{2... | collective-permute-start | bytes 1327112 | tf_op jit(solution)/shard_map/ppermute | solution.py:1043
  265.9 30.0 %collective-permute-start.26 = (bf16[288,768]{1,0:T(8,128)(2,1)}, bf16[288,768]{1,0:T(8,128)(2,1)}, u32[]{:S(2)}, u32[]{:S(2)}) collective-permute-start(bf16[288,768]{1,0:T(8,128)(2,1)} %collective-permute-done.21.refs_26_), channel_id=1, source_target_pairs={{16,18},{17,19},{18,16},{19,17},{20,22},{21,23},{22,20},{23,21},{2... | collective-permute-start | bytes 1327112 | tf_op jit(solution)/shard_map/ppermute | solution.py:1043
  267.8 40.9 %collective-permute-start.29 = (bf16[832,768]{1,0:T(8,128)(2,1)}, bf16[832,768]{1,0:T(8,128)(2,1)}, u32[]{:S(2)}, u32[]{:S(2)}) collective-permute-start(bf16[832,768]{1,0:T(8,128)(2,1)} %get-tuple-element.239), channel_id=1, source_target_pairs={{0,1},{1,0},{2,3},{3,2},{4,5},{5,4},{6,7},{7,6},{8,9},{9,8},{10,11... | collective-permute-start | bytes 3833864 | tf_op jit(solution)/shard_map/ppermute | solution.py:1043
  293.5 48.7 %copy-start.18 = (bf16[288,768]{1,0:T(8,128)(2,1)}, bf16[288,768]{1,0:T(8,128)(2,1)S(1)}, u32[]{:S(2)}) copy-start(bf16[288,768]{1,0:T(8,128)(2,1)S(1)} %collective-permute-done.24.refs_25_) | copy-start | bytes 1327108
  293.5 48.7 %copy-start.19 = (bf16[288,768]{1,0:T(8,128)(2,1)}, bf16[288,768]{1,0:T(8,128)(2,1)S(1)}, u32[]{:S(2)}) copy-start(bf16[288,768]{1,0:T(8,128)(2,1)S(1)} %collective-permute-done.25.refs_27_) | copy-start | bytes 1327108
  303.3 29.6 %collective-permute-start.28 = (bf16[832,768]{1,0:T(8,128)(2,1)}, bf16[832,768]{1,0:T(8,128)(2,1)S(1)}, u32[]{:S(2)}, u32[]{:S(2)}) collective-permute-start(bf16[832,768]{1,0:T(8,128)(2,1)} %get-tuple-element.237), channel_id=1, source_target_pairs={{0,1},{1,0},{2,3},{3,2},{4,5},{5,4},{6,7},{7,6},{8,9},{9,8},{10,11... | collective-permute-start | bytes 3833864 | tf_op jit(solution)/shard_map/ppermute | solution.py:1043
  304.3 148.6 %collective-permute-start.49 = (bf16[1568,768]{1,0:T(8,128)(2,1)}, bf16[1568,768]{1,0:T(8,128)(2,1)}, u32[]{:S(2)}, u32[]{:S(2)}) collective-permute-start(bf16[1568,768]{1,0:T(8,128)(2,1)} %get-tuple-element.266.refs_12_), channel_id=1, source_target_pairs={{0,8},{8,0},{16,24},{24,16},{1,9},{9,1},{17,25},{25,17},{2,10},{10... | collective-permute-start | bytes 7225352 | tf_op jit(solution)/shard_map/ppermute | solution.py:1128
  305.0 33.7 %collective-permute-start.30 = (bf16[288,768]{1,0:T(8,128)(2,1)S(1)}, bf16[288,768]{1,0:T(8,128)(2,1)S(1)}, u32[]{:S(2)}, u32[]{:S(2)}) collective-permute-start(bf16[288,768]{1,0:T(8,128)(2,1)S(1)} %collective-permute-done.25.refs_27_), channel_id=1, source_target_pairs={{16,18},{17,19},{18,16},{19,17},{20,22},{21,23},{22,20},{23,21},{2... | collective-permute-start | bytes 1327112 | tf_op jit(solution)/shard_map/ppermute | solution.py:1043
  312.8 27.4 %collective-permute-start.33 = (bf16[208,768]{1,0:T(8,128)(2,1)}, bf16[208,768]{1,0:T(8,128)(2,1)S(1)}, u32[]{:S(2)}, u32[]{:S(2)}) collective-permute-start(bf16[208,768]{1,0:T(8,128)(2,1)} %get-tuple-element.248), channel_id=1, source_target_pairs={{0,2},{1,3},{2,0},{3,1},{4,6},{5,7},{6,4},{7,5},{8,10},{9,11},{10,... | collective-permute-start | bytes 958472 | tf_op jit(solution)/shard_map/ppermute | solution.py:1043
  313.1 27.9 %collective-permute-start.34 = (bf16[208,768]{1,0:T(8,128)(2,1)}, bf16[208,768]{1,0:T(8,128)(2,1)}, u32[]{:S(2)}, u32[]{:S(2)}) collective-permute-start(bf16[208,768]{1,0:T(8,128)(2,1)} %get-tuple-element.249), channel_id=1, source_target_pairs={{0,4},{1,5},{2,6},{3,7},{4,0},{5,1},{6,2},{7,3},{8,12},{9,13},{10,... | collective-permute-start | bytes 958472 | tf_op jit(solution)/shard_map/ppermute | solution.py:1043
  332.9 51.1 %collective-permute-start.35 = (bf16[208,768]{1,0:T(8,128)(2,1)}, bf16[208,768]{1,0:T(8,128)(2,1)}, u32[]{:S(2)}, u32[]{:S(2)}) collective-permute-start(bf16[208,768]{1,0:T(8,128)(2,1)} %get-tuple-element.250), channel_id=1, source_target_pairs={{0,6},{1,7},{2,4},{3,5},{4,2},{5,3},{6,0},{7,1},{8,14},{9,15},{10,... | collective-permute-start | bytes 958472 | tf_op jit(solution)/shard_map/ppermute | solution.py:1043
  338.7 50.0 %collective-permute-start.39 = (bf16[208,768]{1,0:T(8,128)(2,1)}, bf16[208,768]{1,0:T(8,128)(2,1)}, u32[]{:S(2)}, u32[]{:S(2)}) collective-permute-start(bf16[208,768]{1,0:T(8,128)(2,1)} %get-tuple-element.254), channel_id=1, source_target_pairs={{0,2},{1,3},{2,0},{3,1},{4,6},{5,7},{6,4},{7,5},{8,10},{9,11},{10,... | collective-permute-start | bytes 958472 | tf_op jit(solution)/shard_map/ppermute | solution.py:1043
  340.3 50.0 %collective-permute-start.40 = (bf16[208,768]{1,0:T(8,128)(2,1)}, bf16[208,768]{1,0:T(8,128)(2,1)}, u32[]{:S(2)}, u32[]{:S(2)}) collective-permute-start(bf16[208,768]{1,0:T(8,128)(2,1)} %get-tuple-element.255), channel_id=1, source_target_pairs={{0,4},{1,5},{2,6},{3,7},{4,0},{5,1},{6,2},{7,3},{8,12},{9,13},{10,... | collective-permute-start | bytes 958472 | tf_op jit(solution)/shard_map/ppermute | solution.py:1043
  341.0 52.0 %collective-permute-start.41 = (bf16[208,768]{1,0:T(8,128)(2,1)}, bf16[208,768]{1,0:T(8,128)(2,1)}, u32[]{:S(2)}, u32[]{:S(2)}) collective-permute-start(bf16[208,768]{1,0:T(8,128)(2,1)} %get-tuple-element.256), channel_id=1, source_target_pairs={{0,6},{1,7},{2,4},{3,5},{4,2},{5,3},{6,0},{7,1},{8,14},{9,15},{10,... | collective-permute-start | bytes 958472 | tf_op jit(solution)/shard_map/ppermute | solution.py:1043
  384.0 20.2 %copy-start.12 = (bf16[1568,768]{1,0:T(8,128)(2,1)S(1)}, bf16[1568,768]{1,0:T(8,128)(2,1)}, u32[]{:S(2)}) copy-start(bf16[1568,768]{1,0:T(8,128)(2,1)} %get-tuple-element.264.refs_8_) | copy-start | bytes 7225348
  387.1 14.3 %collective-permute-start.36 = (bf16[208,768]{1,0:T(8,128)(2,1)}, bf16[208,768]{1,0:T(8,128)(2,1)S(1)}, u32[]{:S(2)}, u32[]{:S(2)}) collective-permute-start(bf16[208,768]{1,0:T(8,128)(2,1)} %get-tuple-element.252.refs_0_), channel_id=1, source_target_pairs={{0,2},{1,3},{2,0},{3,1},{4,6},{5,7},{6,4},{7,5},{8,10},{9,11},{10,... | collective-permute-start | bytes 958472 | tf_op jit(solution)/shard_map/ppermute | solution.py:1043
  388.8 15.4 %collective-permute-start.37 = (bf16[208,768]{1,0:T(8,128)(2,1)}, bf16[208,768]{1,0:T(8,128)(2,1)S(1)}, u32[]{:S(2)}, u32[]{:S(2)}) collective-permute-start(bf16[208,768]{1,0:T(8,128)(2,1)} %get-tuple-element.252.refs_0_), channel_id=1, source_target_pairs={{0,4},{1,5},{2,6},{3,7},{4,0},{5,1},{6,2},{7,3},{8,12},{9,13},{10,... | collective-permute-start | bytes 958472 | tf_op jit(solution)/shard_map/ppermute | solution.py:1043
  390.2 104.2 %collective-permute-start.50 = (bf16[1568,768]{1,0:T(8,128)(2,1)}, bf16[1568,768]{1,0:T(8,128)(2,1)}, u32[]{:S(2)}, u32[]{:S(2)}) collective-permute-start(bf16[1568,768]{1,0:T(8,128)(2,1)} %get-tuple-element.267.refs_14_), channel_id=1, source_target_pairs={{0,8},{8,0},{16,24},{24,16},{1,9},{9,1},{17,25},{25,17},{2,10},{10... | collective-permute-start | bytes 7225352 | tf_op jit(solution)/shard_map/ppermute | solution.py:1128
  395.9 16.8 %collective-permute-start.42 = (bf16[208,768]{1,0:T(8,128)(2,1)}, bf16[208,768]{1,0:T(8,128)(2,1)S(1)}, u32[]{:S(2)}, u32[]{:S(2)}) collective-permute-start(bf16[208,768]{1,0:T(8,128)(2,1)} %get-tuple-element.258.refs_0_), channel_id=1, source_target_pairs={{0,2},{1,3},{2,0},{3,1},{4,6},{5,7},{6,4},{7,5},{8,10},{9,11},{10,... | collective-permute-start | bytes 958472 | tf_op jit(solution)/shard_map/ppermute | solution.py:1043
  401.4 39.7 %copy-start.29 = (bf16[208,768]{1,0:T(8,128)(2,1)}, bf16[208,768]{1,0:T(8,128)(2,1)S(1)}, u32[]{:S(2)}) copy-start(bf16[208,768]{1,0:T(8,128)(2,1)S(1)} %collective-permute-done.36.refs_1_) | copy-start | bytes 958468
  401.4 15.0 %collective-permute-start.43 = (bf16[208,768]{1,0:T(8,128)(2,1)}, bf16[208,768]{1,0:T(8,128)(2,1)S(1)}, u32[]{:S(2)}, u32[]{:S(2)}) collective-permute-start(bf16[208,768]{1,0:T(8,128)(2,1)} %get-tuple-element.258.refs_0_), channel_id=1, source_target_pairs={{0,4},{1,5},{2,6},{3,7},{4,0},{5,1},{6,2},{7,3},{8,12},{9,13},{10,... | collective-permute-start | bytes 958472 | tf_op jit(solution)/shard_map/ppermute | solution.py:1043
  404.2 36.9 %copy-start.30 = (bf16[208,768]{1,0:T(8,128)(2,1)}, bf16[208,768]{1,0:T(8,128)(2,1)S(1)}, u32[]{:S(2)}) copy-start(bf16[208,768]{1,0:T(8,128)(2,1)S(1)} %collective-permute-done.37.refs_2_) | copy-start | bytes 958468
  404.2 95.3 %collective-permute-start.47 = (bf16[1568,768]{1,0:T(8,128)(2,1)S(1)}, bf16[1568,768]{1,0:T(8,128)(2,1)}, u32[]{:S(2)}, u32[]{:S(2)}) collective-permute-start(bf16[1568,768]{1,0:T(8,128)(2,1)S(1)} %copy-done.12), channel_id=1, source_target_pairs={{0,8},{8,0},{16,24},{24,16},{1,9},{9,1},{17,25},{25,17},{2,10},{10... | collective-permute-start | bytes 7225352 | tf_op jit(solution)/shard_map/ppermute | solution.py:1128
  412.7 87.3 %collective-permute-start.48 = (bf16[1568,768]{1,0:T(8,128)(2,1)}, bf16[1568,768]{1,0:T(8,128)(2,1)}, u32[]{:S(2)}, u32[]{:S(2)}) collective-permute-start(bf16[1568,768]{1,0:T(8,128)(2,1)} %get-tuple-element.265.refs_10_), channel_id=1, source_target_pairs={{0,8},{8,0},{16,24},{24,16},{1,9},{9,1},{17,25},{25,17},{2,10},{10... | collective-permute-start | bytes 7225352 | tf_op jit(solution)/shard_map/ppermute | solution.py:1128
  416.4 11.9 %collective-permute-start.44 = (bf16[208,768]{1,0:T(8,128)(2,1)}, bf16[208,768]{1,0:T(8,128)(2,1)}, u32[]{:S(2)}, u32[]{:S(2)}) collective-permute-start(bf16[208,768]{1,0:T(8,128)(2,1)} %get-tuple-element.258.refs_0_), channel_id=1, source_target_pairs={{0,6},{1,7},{2,4},{3,5},{4,2},{5,3},{6,0},{7,1},{8,14},{9,15},{10,... | collective-permute-start | bytes 958472 | tf_op jit(solution)/shard_map/ppermute | solution.py:1043
  428.3 12.8 %collective-permute-start.38 = (bf16[208,768]{1,0:T(8,128)(2,1)}, bf16[208,768]{1,0:T(8,128)(2,1)S(1)}, u32[]{:S(2)}, u32[]{:S(2)}) collective-permute-start(bf16[208,768]{1,0:T(8,128)(2,1)} %get-tuple-element.252.refs_0_), channel_id=1, source_target_pairs={{0,6},{1,7},{2,4},{3,5},{4,2},{5,3},{6,0},{7,1},{8,14},{9,15},{10,... | collective-permute-start | bytes 958472 | tf_op jit(solution)/shard_map/ppermute | solution.py:1043
  444.8 49.7 %collective-permute-start.51 = (bf16[832,768]{1,0:T(8,128)(2,1)}, bf16[832,768]{1,0:T(8,128)(2,1)S(1)}, u32[]{:S(2)}, u32[]{:S(2)}) collective-permute-start(bf16[832,768]{1,0:T(8,128)(2,1)} %get-tuple-element.272.refs_0_), channel_id=1, source_target_pairs={{0,1},{1,0},{2,3},{3,2},{4,5},{5,4},{6,7},{7,6},{8,9},{9,8},{10,11... | collective-permute-start | bytes 3833864 | tf_op jit(solution)/shard_map/ppermute | solution.py:1043
  452.8 47.9 %collective-permute-start.31 = (bf16[1568,768]{1,0:T(8,128)(2,1)}, bf16[1568,768]{1,0:T(8,128)(2,1)}, u32[]{:S(2)}, u32[]{:S(2)}) collective-permute-start(bf16[1568,768]{1,0:T(8,128)(2,1)} %get-tuple-element.245.refs_0_), channel_id=1, source_target_pairs={{0,8},{8,0},{16,24},{24,16},{1,9},{9,1},{17,25},{25,17},{2,10},{10... | collective-permute-start | bytes 7225352 | tf_op jit(solution)/shard_map/ppermute | solution.py:1128
  494.4 11.9 %collective-permute-start.32 = (bf16[1568,768]{1,0:T(8,128)(2,1)}, bf16[1568,768]{1,0:T(8,128)(2,1)}, u32[]{:S(2)}, u32[]{:S(2)}) collective-permute-start(bf16[1568,768]{1,0:T(8,128)(2,1)} %get-tuple-element.246.refs_2_), channel_id=1, source_target_pairs={{0,8},{8,0},{16,24},{24,16},{1,9},{9,1},{17,25},{25,17},{2,10},{10... | collective-permute-start | bytes 7225352 | tf_op jit(solution)/shard_map/ppermute | solution.py:1128
  494.5 11.8 %collective-permute-start.45 = (bf16[1568,768]{1,0:T(8,128)(2,1)}, bf16[1568,768]{1,0:T(8,128)(2,1)}, u32[]{:S(2)}, u32[]{:S(2)}) collective-permute-start(bf16[1568,768]{1,0:T(8,128)(2,1)} %get-tuple-element.262.refs_4_), channel_id=1, source_target_pairs={{0,8},{8,0},{16,24},{24,16},{1,9},{9,1},{17,25},{25,17},{2,10},{10... | collective-permute-start | bytes 7225352 | tf_op jit(solution)/shard_map/ppermute | solution.py:1128
  499.4 26.2 %collective-permute-start.54 = (bf16[1664,768]{1,0:T(8,128)(2,1)}, bf16[1664,768]{1,0:T(8,128)(2,1)}, u32[]{:S(2)}, u32[]{:S(2)}) collective-permute-start(bf16[1664,768]{1,0:T(8,128)(2,1)} %get-tuple-element.279.refs_2_), channel_id=1, source_target_pairs={{0,8},{8,0},{16,24},{24,16},{1,9},{9,1},{17,25},{25,17},{2,10},{10... | collective-permute-start | bytes 7667720 | tf_op jit(solution)/shard_map/ppermute | solution.py:1128
  500.0 9.7 %collective-permute-start.46 = (bf16[1568,768]{1,0:T(8,128)(2,1)}, bf16[1568,768]{1,0:T(8,128)(2,1)S(1)}, u32[]{:S(2)}, u32[]{:S(2)}) collective-permute-start(bf16[1568,768]{1,0:T(8,128)(2,1)} %get-tuple-element.263.refs_6_), channel_id=1, source_target_pairs={{0,8},{8,0},{16,24},{24,16},{1,9},{9,1},{17,25},{25,17},{2,10},{10... | collective-permute-start | bytes 7225352 | tf_op jit(solution)/shard_map/ppermute | solution.py:1128
  500.8 29.6 %collective-permute-start.55 = (bf16[832,768]{1,0:T(8,128)(2,1)}, bf16[832,768]{1,0:T(8,128)(2,1)}, u32[]{:S(2)}, u32[]{:S(2)}) collective-permute-start(bf16[832,768]{1,0:T(8,128)(2,1)} %get-tuple-element.282.refs_0_), channel_id=1, source_target_pairs={{0,1},{1,0},{2,3},{3,2},{4,5},{5,4},{6,7},{7,6},{8,9},{9,8},{10,11... | collective-permute-start | bytes 3833864 | tf_op jit(solution)/shard_map/ppermute | solution.py:1043
  506.4 19.3 %collective-permute-start.52 = (bf16[4,56,768]{2,1,0:T(8,128)(2,1)}, bf16[4,56,768]{2,1,0:T(8,128)(2,1)S(1)}, u32[]{:S(2)}, u32[]{:S(2)}) collective-permute-start(bf16[4,56,768]{2,1,0:T(8,128)(2,1)} %pad_maximum_fusion.2), channel_id=1, source_target_pairs={{0,16},{8,24},{16,0},{24,8},{1,17},{9,25},{17,1},{25,9},{2,18},{10... | collective-permute-start | bytes 1032200 | tf_op jit(solution)/shard_map/ppermute | solution.py:1125
  506.4 19.3 %collective-permute-start.53 = (bf16[4,56,768]{2,1,0:T(8,128)(2,1)}, bf16[4,56,768]{2,1,0:T(8,128)(2,1)}, u32[]{:S(2)}, u32[]{:S(2)}) collective-permute-start(bf16[4,56,768]{2,1,0:T(8,128)(2,1)} %pad_maximum_fusion.3), channel_id=1, source_target_pairs={{0,16},{8,24},{16,0},{24,8},{1,17},{9,25},{17,1},{25,9},{2,18},{10... | collective-permute-start | bytes 1032200 | tf_op jit(solution)/shard_map/ppermute | solution.py:1125
  534.3 6.1 %collective-permute-start.56 = (bf16[1664,768]{1,0:T(8,128)(2,1)}, bf16[1664,768]{1,0:T(8,128)(2,1)}, u32[]{:S(2)}, u32[]{:S(2)}) collective-permute-start(bf16[1664,768]{1,0:T(8,128)(2,1)} %get-tuple-element.284.refs_0_), channel_id=1, source_target_pairs={{0,8},{8,0},{16,24},{24,16},{1,9},{9,1},{17,25},{25,17},{2,10},{10... | collective-permute-start | bytes 7667720 | tf_op jit(solution)/shard_map/ppermute | solution.py:1128
  (34 other events, 193.7 us)
Sparse Core Ops, SparseCore 0:
  75.8 65.5 all-gather.2
  213.7 75.4 all-gather.4
